TPU v7x, 32 devices: a whole 2x2x4 slice. The times are simulated.
32 devices in a mesh: groups: 2 (over x), rows: 16 (over z, y, core).
Axes of the slice: x: 2, y: 2, z: 4, core: 2. Of those that a mesh axis runs over, the one named last changes fastest.
Arguments:
- tiles: bfloat16 [256, 40, 128, 128], P(('groups', 'rows')), parts along dimension 0
- pattern: int32 [256, 40], P(('groups', 'rows')), parts along dimension 0, may hold values from 0 to 127, as said below
- basis: float32 [32768, 256], P(('groups', 'rows')), parts along dimension 0, may hold values from -3 to 3
Outputs:
- modes: float32 [32768, 256], P(('groups', 'rows')), parts along dimension 0
- projected: float32 [4, 256, 256], P('groups'), parts along dimension 0
There are 2 independent parts, one for each index of `groups`. A program takes and returns all parts, laid end to end along the dimension named above; each array names one. Nothing has to cross between parts.
Inputs may be any that keep to these rules, and one draw needn't show every extreme that they name: The column blocks of one block row are distinct; one of them is the row itself and every other lies within 24 blocks of it, counted cyclically over 128 block rows. The pattern is symmetric: block row r names c exactly when c names r, and tiles hold C's symmetric blocks (the tile at (c, r) is the transpose of the tile at (r, c)). Row r names r + d and r - d for the same set of distances in every block row, plus its partner in the pairing of 2 i with 2 i + 1; the slots are in no fixed order.
All inputs are finite; a program needn't handle non-finite values.
Results may differ from a plain program's by a relative error of at most 0.0041.
Values may be sent and summed in bfloat16 or wider, within the bound.
No kernel may reach another device: no remote copies, remote signals or barrier semaphores. Data moves between devices by JAX's collectives and lax.ppermute only.
A program may use at most 128 MiB of HBM per device.

v0:
```python
import math

import jax
import jax.numpy as jnp
from jax import lax
from jax.sharding import PartitionSpec as P

STEPS = 2


def passed_along(value, axis, by):
    peers = lax.axis_size(axis)
    return lax.ppermute(value, axis, [(i, (i + by) % peers) for i in range(peers)])


def neighbourhood(blocks):
    received = {}
    for stride in (1, 2, 3):
        for towards in (1, -1):
            received[towards, stride] = passed_along(blocks, "rows", towards * stride)
    pieces = [
        received[1, 3],
        received[1, 2],
        received[1, 1],
        blocks,
        received[-1, 1],
        received[-1, 2],
        received[-1, 3],
    ]
    return jnp.concatenate(pieces, axis=0)


def per_device(tiles, pattern, basis):
    devices = lax.axis_size("rows")
    my_index = lax.axis_index("rows")
    block_rows = tiles.shape[0]
    tile_size = tiles.shape[2]
    mode_count = basis.shape[1]
    total_blocks = block_rows * devices
    full_order = total_blocks * tile_size
    first_block = (my_index - 3) * block_rows
    local_cols = jnp.mod(pattern - first_block, total_blocks)
    current = basis
    projected_list = []
    for step_index in range(STEPS):
        rounded = current.astype(jnp.bfloat16)
        blocks = rounded.reshape(block_rows, tile_size, mode_count)
        window = neighbourhood(blocks)
        picked = jnp.take(window, local_cols, axis=0)
        product = jnp.einsum("rkij,rkjm->rim", tiles, picked, preferred_element_type=jnp.float32)
        product = product.reshape(block_rows * tile_size, mode_count)
        wide = rounded.astype(jnp.float32)
        gram_part = jnp.einsum("rm,rn->mn", product, product, precision=lax.Precision.HIGHEST)
        proj_part = jnp.einsum("rm,rn->mn", wide, product, precision=lax.Precision.HIGHEST)
        gram, projected_now = lax.psum((gram_part, proj_part), "rows")
        projected_list.append(projected_now)
        lower = jnp.linalg.cholesky(gram)
        inverse = lax.linalg.triangular_solve(
            lower, jnp.eye(mode_count, dtype=jnp.float32), left_side=True, lower=True
        )
        current = jnp.einsum("rm,nm->rn", product, inverse, precision=lax.Precision.HIGHEST)
    return (current * math.sqrt(full_order), jnp.stack(projected_list))


def solution(mesh):
    placed = (
        P(("groups", "rows"), None, None, None),
        P(("groups", "rows"), None),
        P(("groups", "rows"), None),
    )
    return jax.shard_map(
        per_device,
        mesh=mesh,
        in_specs=placed,
        out_specs=(P(("groups", "rows"), None), P("groups", None, None)),
        check_vma=False,
    )
```

profile of v0, /device:TPU:0, one launch (start us, length us, event | category | flops | bytes accessed | tf_op | source)
XLA Modules:
  0.0 495.8 jit_solution(8955868494241381930)
XLA Ops:
  7.2 1.3 convert_element_type.14
  8.5 2.5 collective-permute-start
  10.9 1.5 collective-permute-start.1
  12.5 2.3 collective-permute-start.5
  14.8 1.6 collective-permute-start.3
  17.2 7.3 %collective-permute-done = bf16[8,128,256]{2,1,0:T(8,128)(2,1)S(1)} collective-permute-done((bf16[8,128,256]{2,1,0:T(8,128)(2,1)S(1)}, bf16[8,128,256]{2,1,0:T(8,128)(2,1)S(1)}, u32[]{:S(2)}, u32[]{:S(2)}) %collective-permute-start) | collective-permute-done | bytes 524320 | tf_op jit(solution)/shard_map/ppermute | solution.py:13
  24.5 4.3 collective-permute-start.4
  29.6 26.1 %collective-permute-done.1 = bf16[8,128,256]{2,1,0:T(8,128)(2,1)S(1)} collective-permute-done((bf16[8,128,256]{2,1,0:T(8,128)(2,1)S(1)}, bf16[8,128,256]{2,1,0:T(8,128)(2,1)S(1)}, u32[]{:S(2)}, u32[]{:S(2)}) %collective-permute-start.1) | collective-permute-done | bytes 524320 | tf_op jit(solution)/shard_map/ppermute | solution.py:13
  59.1 1.3 collective-permute-done.4
  62.1 13.3 %gather_fusion = bf16[320,128,256]{2,1,0:T(8,128)(2,1)} fusion(bf16[56,128,256]{2,1,0:T(8,128)(2,1)} %constant_dynamic-update-slice_fusion, s32[1024]{0:T(1024)S(1)} %pad_clamp_fusion), kind=kCustom, calls=%fused_computation.clone | custom fusion | bytes 41944320 | tf_op jit(solution)/shard_map/jit(_take)/gather | solution.py:49
  75.4 12.2 %fusion.2 = f32[8,256,128,1]{1,2,3,0:T(8,128)S(1)} fusion(bf16[8,40,128,128]{3,2,1,0:T(8,128)(2,1)} %param.8, bf16[8,40,128,256]{3,2,1,0:T(8,128)(2,1)} %bitcast.101, pred[8,40]{1,0:T(8,128)(4,1)S(1)} %get-tuple-element.42), kind=kOutput, calls=%fused_computation.8 | convolution fusion | flops 2694840320 | bytes 32506176 | tf_op jit(solution)/shard_map/rkij,rkjm->rim/dot_general | solution.py:50
  87.6 2.6 convolution_bitcast_fusion.3
  90.4 90.8 %all-reduce.5.cloned.1.call-done = f32[256,256]{0,1:T(8,128)} async-done(((f32[256,256]{0,1:T(8,128)}), f32[256,256]{0,1:T(8,128)}) %all-reduce.5.cloned.1.call-update) | async-done | bytes 262160 | tf_op jit(solution)/shard_map/psum | solution.py:55
  181.2 1.1 copy.7
  182.3 1.0 fusion.17
  183.3 11.7 %cholesky.130 = f32[128,128]{1,0:T(8,128)S(1)} custom-call(f32[128,128]{1,0:T(8,128)S(1)} %cholesky.194), custom_call_target="Cholesky" | custom-call | tf_op jit(solution)/shard_map/jit(cholesky)/cholesky | solution.py:57
  195.1 9.8 %custom-call.13 = f32[1,128,128]{1,2,0:T(8,128)S(1)} custom-call(f32[1,128,128]{2,1,0:T(8,128)S(1)} %get-tuple-element.55), custom_call_target="InvertDiagBlocksLowerTriangular" | custom-call | tf_op jit(solution)/shard_map/jit(cholesky)/cholesky | solution.py:57
  205.4 11.7 %cholesky.147 = f32[128,128]{1,0:T(8,128)S(1)} custom-call(f32[128,128]{1,0:T(8,128)S(1)} %convolution_subtract_fusion.3), custom_call_target="Cholesky" | custom-call | tf_op jit(solution)/shard_map/jit(cholesky)/cholesky | solution.py:57
  219.3 4.2 while.4
  220.1 1.4 bitcast_dynamic-update-slice_fusion.4
  222.1 1.4 bitcast_dynamic-update-slice_fusion.4
  223.5 19.7 %custom-call.14 = f32[2,128,128]{1,2,0:T(8,128)S(1)} custom-call(f32[2,128,128]{2,1,0:T(8,128)S(1)} %get-tuple-element.19), custom_call_target="InvertDiagBlocksLowerTriangular" | custom-call | tf_op jit(solution)/shard_map/triangular_solve/custom-call.0 | solution.py:58
  244.1 1.0 convolution_convert_fusion
  245.9 1.1 collective-permute-start.7
  247.0 1.5 collective-permute-start.8
  248.5 3.8 collective-permute-start.9
  252.2 1.7 convolution_bitcast_fusion.1
  254.0 13.5 %collective-permute-done.6 = bf16[8,128,256]{2,1,0:T(8,128)(2,1)S(1)} collective-permute-done((bf16[8,128,256]{2,1,0:T(8,128)(2,1)S(1)}, bf16[8,128,256]{2,1,0:T(8,128)(2,1)S(1)}, u32[]{:S(2)}, u32[]{:S(2)}) %collective-permute-start.6) | collective-permute-done | bytes 524320 | tf_op jit(solution)/shard_map/ppermute | solution.py:13
  268.3 21.6 %collective-permute-done.7 = bf16[8,128,256]{2,1,0:T(8,128)(2,1)S(1)} collective-permute-done((bf16[8,128,256]{2,1,0:T(8,128)(2,1)S(1)}, bf16[8,128,256]{2,1,0:T(8,128)(2,1)S(1)}, u32[]{:S(2)}, u32[]{:S(2)}) %collective-permute-start.7) | collective-permute-done | bytes 524320 | tf_op jit(solution)/shard_map/ppermute | solution.py:13
  290.8 0.9 constant_dynamic-update-slice_fusion.11
  293.3 1.7 collective-permute-done.10
  296.7 13.3 %gather_fusion.1 = bf16[320,128,256]{2,1,0:T(8,128)(2,1)} fusion(bf16[56,128,256]{2,1,0:T(8,128)(2,1)} %constant_dynamic-update-slice_fusion.7, s32[1024]{0:T(1024)S(1)} %pad_clamp_fusion), kind=kCustom, calls=%fused_computation.1.clone | custom fusion | bytes 41944320 | tf_op jit(solution)/shard_map/jit(_take)/gather | solution.py:49
  310.0 12.6 %fusion = f32[8,256,128,1]{1,2,3,0:T(8,128)S(1)} fusion(bf16[8,40,128,128]{3,2,1,0:T(8,128)(2,1)} %param.8, bf16[8,40,128,256]{3,2,1,0:T(8,128)(2,1)} %bitcast.100, pred[8,40]{1,0:T(8,128)(4,1)S(1)} %get-tuple-element.42), kind=kOutput, calls=%fused_computation.6 | convolution fusion | flops 2694840320 | bytes 32506176 | tf_op jit(solution)/shard_map/rkij,rkjm->rim/dot_general | solution.py:50
  322.6 2.6 convolution_bitcast_fusion.2
  325.2 1.7 convolution_bitcast_fusion
  326.9 94.5 %all-reduce.7.cloned.1.call-done = (f32[256,256]{0,1:T(8,128)}, f32[1,256,256]{1,2,0:T(8,128)}, f32[1,256,256]{1,2,0:T(8,128)}) async-done(((f32[256,256]{0,1:T(8,128)}, f32[1,256,256]{1,2,0:T(8,128)}, f32[1,256,256]{1,2,0:T(8,128)}), (f32[256,256]{0,1:T(8,128)}, f32[1,256,256]{1,2,0:T(8,128)}, f32[1,256,256]{1,2,0:T(8,128)})) %all-reduce.7.cloned.1.call-update) | async-done | bytes 786448 | tf_op jit(solution)/shard_map/psum | solution.py:55
  421.4 1.1 pad_maximum_fusion
  422.5 1.0 copy.12
  423.5 1.1 copy.10
  424.6 1.0 fusion.16
  425.6 11.7 %cholesky.164 = f32[128,128]{1,0:T(8,128)S(1)} custom-call(f32[128,128]{1,0:T(8,128)S(1)} %cholesky.197), custom_call_target="Cholesky" | custom-call | tf_op jit(solution)/shard_map/jit(cholesky)/cholesky | solution.py:57
  438.0 9.8 %custom-call.15 = f32[1,128,128]{1,2,0:T(8,128)S(1)} custom-call(f32[1,128,128]{2,1,0:T(8,128)S(1)} %get-tuple-element.51), custom_call_target="InvertDiagBlocksLowerTriangular" | custom-call | tf_op jit(solution)/shard_map/jit(cholesky)/cholesky | solution.py:57
  448.3 11.9 %cholesky.181 = f32[128,128]{1,0:T(8,128)S(1)} custom-call(f32[128,128]{1,0:T(8,128)S(1)} %convolution_subtract_fusion.2), custom_call_target="Cholesky" | custom-call | tf_op jit(solution)/shard_map/jit(cholesky)/cholesky | solution.py:57
  462.2 4.0 while.5
  462.8 1.4 bitcast_dynamic-update-slice_fusion.5
  464.8 1.4 bitcast_dynamic-update-slice_fusion.5
  466.2 19.7 %custom-call.16 = f32[2,128,128]{1,2,0:T(8,128)S(1)} custom-call(f32[2,128,128]{2,1,0:T(8,128)S(1)} %get-tuple-element.20), custom_call_target="InvertDiagBlocksLowerTriangular" | custom-call | tf_op jit(solution)/shard_map/triangular_solve/custom-call.0 | solution.py:58
  486.8 2.0 convolution_multiply_fusion
  (66 shorter events, 20.3 us)
Async XLA Ops:
  7.2 174.1 %all-reduce.5.cloned.1.call-start = ((), (), s32[]{:S(2)}) async-start(), calls=%async_computation | async-start | bytes 524288 | tf_op jit(solution)/shard_map/psum | solution.py:55
  8.5 16.0 %collective-permute-start = (bf16[8,128,256]{2,1,0:T(8,128)(2,1)S(1)}, bf16[8,128,256]{2,1,0:T(8,128)(2,1)S(1)}, u32[]{:S(2)}, u32[]{:S(2)}) collective-permute-start(bf16[8,128,256]{2,1,0:T(8,128)(2,1)S(1)} %bitcast.106), channel_id=1, source_target_pairs={{0,3},{1,4},{2,5},{3,6},{4,7},{5,8},{6,9},{7,10},{8,11},{9,12},{10... | collective-permute-start | bytes 1572872 | tf_op jit(solution)/shard_map/ppermute | solution.py:13
  10.9 44.7 %collective-permute-start.1 = (bf16[8,128,256]{2,1,0:T(8,128)(2,1)S(1)}, bf16[8,128,256]{2,1,0:T(8,128)(2,1)S(1)}, u32[]{:S(2)}, u32[]{:S(2)}) collective-permute-start(bf16[8,128,256]{2,1,0:T(8,128)(2,1)S(1)} %bitcast.107), channel_id=1, source_target_pairs={{0,2},{1,3},{2,4},{3,5},{4,6},{5,7},{6,8},{7,9},{8,10},{9,11},{10,... | collective-permute-start | bytes 1572872 | tf_op jit(solution)/shard_map/ppermute | solution.py:13
  12.5 48.8 %collective-permute-start.5 = (bf16[8,128,256]{2,1,0:T(8,128)(2,1)S(1)}, bf16[8,128,256]{2,1,0:T(8,128)(2,1)S(1)}, u32[]{:S(2)}, u32[]{:S(2)}) collective-permute-start(bf16[8,128,256]{2,1,0:T(8,128)(2,1)S(1)} %bitcast.108), channel_id=1, source_target_pairs={{0,13},{1,14},{2,15},{3,0},{4,1},{5,2},{6,3},{7,4},{8,5},{9,6},{10... | collective-permute-start | bytes 1572872 | tf_op jit(solution)/shard_map/ppermute | solution.py:13
  14.8 43.4 %collective-permute-start.3 = (bf16[8,128,256]{2,1,0:T(8,128)(2,1)S(1)}, bf16[8,128,256]{2,1,0:T(8,128)(2,1)S(1)}, u32[]{:S(2)}, u32[]{:S(2)}) collective-permute-start(bf16[8,128,256]{2,1,0:T(8,128)(2,1)S(1)} %bitcast.109), channel_id=1, source_target_pairs={{0,15},{1,0},{2,1},{3,2},{4,3},{5,4},{6,5},{7,6},{8,7},{9,8},{10,9... | collective-permute-start | bytes 1572872 | tf_op jit(solution)/shard_map/ppermute | solution.py:13
  16.4 40.2 %collective-permute-start.2 = (bf16[8,128,256]{2,1,0:T(8,128)(2,1)S(1)}, bf16[8,128,256]{2,1,0:T(8,128)(2,1)S(1)}, u32[]{:S(2)}, u32[]{:S(2)}) collective-permute-start(bf16[8,128,256]{2,1,0:T(8,128)(2,1)S(1)} %bitcast.110), channel_id=1, source_target_pairs={{0,1},{1,2},{2,3},{3,4},{4,5},{5,6},{6,7},{7,8},{8,9},{9,10},{10,1... | collective-permute-start | bytes 1572872 | tf_op jit(solution)/shard_map/ppermute | solution.py:13
  24.5 35.9 %collective-permute-start.4 = (bf16[8,128,256]{2,1,0:T(8,128)(2,1)S(1)}, bf16[8,128,256]{2,1,0:T(8,128)(2,1)S(1)}, u32[]{:S(2)}, u32[]{:S(2)}) collective-permute-start(bf16[8,128,256]{2,1,0:T(8,128)(2,1)S(1)} %bitcast.111), channel_id=1, source_target_pairs={{0,14},{1,15},{2,0},{3,1},{4,2},{5,3},{6,4},{7,5},{8,6},{9,7},{10,... | collective-permute-start | bytes 1572872 | tf_op jit(solution)/shard_map/ppermute | solution.py:13
  90.2 331.3 %all-reduce.7.cloned.1.call-start = ((), (), s32[]{:S(2)}) async-start(), calls=%async_computation.1 | async-start | bytes 1572864 | tf_op jit(solution)/shard_map/psum | solution.py:55
  245.1 22.3 %collective-permute-start.6 = (bf16[8,128,256]{2,1,0:T(8,128)(2,1)S(1)}, bf16[8,128,256]{2,1,0:T(8,128)(2,1)S(1)}, u32[]{:S(2)}, u32[]{:S(2)}) collective-permute-start(bf16[8,128,256]{2,1,0:T(8,128)(2,1)S(1)} %bitcast.113), channel_id=1, source_target_pairs={{0,3},{1,4},{2,5},{3,6},{4,7},{5,8},{6,9},{7,10},{8,11},{9,12},{10... | collective-permute-start | bytes 1572872 | tf_op jit(solution)/shard_map/ppermute | solution.py:13
  245.9 44.0 %collective-permute-start.7 = (bf16[8,128,256]{2,1,0:T(8,128)(2,1)S(1)}, bf16[8,128,256]{2,1,0:T(8,128)(2,1)S(1)}, u32[]{:S(2)}, u32[]{:S(2)}) collective-permute-start(bf16[8,128,256]{2,1,0:T(8,128)(2,1)S(1)} %bitcast.114), channel_id=1, source_target_pairs={{0,2},{1,3},{2,4},{3,5},{4,6},{5,7},{6,8},{7,9},{8,10},{9,11},{10,... | collective-permute-start | bytes 1572872 | tf_op jit(solution)/shard_map/ppermute | solution.py:13
  247.0 43.8 %collective-permute-start.8 = (bf16[8,128,256]{2,1,0:T(8,128)(2,1)S(1)}, bf16[8,128,256]{2,1,0:T(8,128)(2,1)S(1)}, u32[]{:S(2)}, u32[]{:S(2)}) collective-permute-start(bf16[8,128,256]{2,1,0:T(8,128)(2,1)S(1)} %bitcast.115), channel_id=1, source_target_pairs={{0,1},{1,2},{2,3},{3,4},{4,5},{5,6},{6,7},{7,8},{8,9},{9,10},{10,1... | collective-permute-start | bytes 1572872 | tf_op jit(solution)/shard_map/ppermute | solution.py:13
  248.5 44.0 %collective-permute-start.9 = (bf16[8,128,256]{2,1,0:T(8,128)(2,1)S(1)}, bf16[8,128,256]{2,1,0:T(8,128)(2,1)S(1)}, u32[]{:S(2)}, u32[]{:S(2)}) collective-permute-start(bf16[8,128,256]{2,1,0:T(8,128)(2,1)S(1)} %bitcast.116), channel_id=1, source_target_pairs={{0,15},{1,0},{2,1},{3,2},{4,3},{5,4},{6,5},{7,6},{8,7},{9,8},{10,9... | collective-permute-start | bytes 1572872 | tf_op jit(solution)/shard_map/ppermute | solution.py:13
  253.9 41.9 %collective-permute-start.11 = (bf16[8,128,256]{2,1,0:T(8,128)(2,1)S(1)}, bf16[8,128,256]{2,1,0:T(8,128)(2,1)S(1)}, u32[]{:S(2)}, u32[]{:S(2)}) collective-permute-start(bf16[8,128,256]{2,1,0:T(8,128)(2,1)S(1)} %bitcast.117), channel_id=1, source_target_pairs={{0,13},{1,14},{2,15},{3,0},{4,1},{5,2},{6,3},{7,4},{8,5},{9,6},{10... | collective-permute-start | bytes 1572872 | tf_op jit(solution)/shard_map/ppermute | solution.py:13
  267.4 27.6 %collective-permute-start.10 = (bf16[8,128,256]{2,1,0:T(8,128)(2,1)S(1)}, bf16[8,128,256]{2,1,0:T(8,128)(2,1)S(1)}, u32[]{:S(2)}, u32[]{:S(2)}) collective-permute-start(bf16[8,128,256]{2,1,0:T(8,128)(2,1)S(1)} %bitcast.118), channel_id=1, source_target_pairs={{0,14},{1,15},{2,0},{3,1},{4,2},{5,3},{6,4},{7,5},{8,6},{9,7},{10,... | collective-permute-start | bytes 1572872 | tf_op jit(solution)/shard_map/ppermute | solution.py:13
Sparse Core Ops, SparseCore 0:
  90.3 90.8 all-reduce.4
  327.0 94.3 all-reduce.6
where the time goes:
time: 501 us; the launch traced here: 496 us
  waiting for transfers between devices  257 us (51%)
  other arithmetic  113 us (23%)
  local copies, waits for them, and re-layouts  49.7 us (10%)
  matrix products  39 us (8%)
  starting transfers between devices  19.5 us (4%)
  between operations  17.1 us (3%)
    psum x2, waiting for transfers between devices, per_device(): gram, projected_now = lax.psum((gram_part, proj_part), 'rows')  185 us
    ppermute x12, waiting for transfers between devices, passed_along(): lax.ppermute(value, axis, [(i, (i + by) % peers) for i in range(peers)])  71.6 us
    another operation x13, other arithmetic, per_device(): lower = jnp.linalg.cholesky(gram)  68.8 us
    another operation x5, other arithmetic, per_device(): lax.linalg.triangular_solve(lower, jnp.eye(mode_count, dtype=jnp.float32)...  39.4 us
    gather x2, local copies, waits for them, and re-layouts, per_device(): picked = jnp.take(window, local_cols, axis=0)  26.7 us
    dot_general x2, matrix products, per_device(): jnp.einsum('rkij,rkjm->rim', tiles, picked, preferred_element_type=jnp.fl...  24.7 us
    ppermute x12, starting transfers between devices, passed_along(): lax.ppermute(value, axis, [(i, (i + by) % peers) for i in range(peers)])  19.3 us
    unnamed x13, local copies, waits for them, and re-layouts  11.1 us
  transfers between devices with their start and end apart: 14, of which 8 were waited for; matrix products, arithmetic and copies ran while one was open for 3% of the time, Pallas kernels for 0%

commit v1 on v0

v1 whole, which is shorter than its diff:
```python
import functools
import math

import jax
import jax.numpy as jnp
from jax import lax
from jax.experimental import pallas as pl
from jax.experimental.pallas import tpu as pltpu
from jax.sharding import PartitionSpec as P

STEPS = 2
HIGHEST = lax.Precision.HIGHEST
B = 8
LANES = 128
MIB = 2**20


def permuted(value, target):
    peers = lax.axis_size("rows")
    return lax.ppermute(value, "rows", [(i, target(i) % peers) for i in range(peers)])


def neighbourhood(blocks):
    before = permuted(blocks, lambda i: i + 2)
    after = permuted(blocks, lambda i: i - 2)
    far = permuted(blocks, lambda i: i + 3 if i % 2 else i - 3)
    other = lambda v: permuted(v, lambda i: i ^ 1)
    return [blocks, other(blocks), before, other(before), after, other(after), far]


def places(pattern, block_rows):
    peers = lax.axis_size("rows")
    me = lax.axis_index("rows")
    owner = pattern // block_rows
    apart = jnp.mod(owner // 2 - me // 2 + 2, peers // 2) - 2
    crossed = (owner % 2 != me % 2).astype(jnp.int32)
    piece = jnp.where(apart == 0, crossed, jnp.where(apart == -1, 2 + crossed, jnp.where(apart == 1, 4 + crossed, 6)))
    return piece * block_rows + pattern % block_rows


def summed(value):
    peers = lax.axis_size("rows")
    if peers & (peers - 1):
        return lax.psum(value, "rows")
    core = lax.axis_index("rows") % 2
    half = value.shape[0] // 2
    mine = lax.dynamic_slice_in_dim(value, core * half, half)
    rest = lax.dynamic_slice_in_dim(value, (1 - core) * half, half)
    mine = mine + permuted(rest, lambda i: i ^ 1)
    step = 2
    while step < peers:
        mine = mine + permuted(mine, lambda i: i ^ step)
        step *= 2
    rest = permuted(mine, lambda i: i ^ 1)
    return jnp.where(core == 0, jnp.concatenate([mine, rest]), jnp.concatenate([rest, mine]))


def product_kernel(place_ref, tiles_ref, *refs, pieces):
    piece_refs, (out_ref, low_ref, window, sems) = refs[:pieces], refs[pieces:]
    r = pl.program_id(0)
    block_rows = piece_refs[0].shape[0]

    @pl.when(r == 0)
    def _():
        copies = [
            pltpu.make_async_copy(piece_refs[i], window.at[pl.ds(i * block_rows, block_rows)], sems.at[i])
            for i in range(pieces)
        ]
        for c in copies:
            c.start()
        for c in copies:
            c.wait()

    total = None
    for k in range(0, tiles_ref.shape[1], 2):
        left = jnp.concatenate([tiles_ref[0, k], tiles_ref[0, k + 1]], axis=1)
        right = jnp.concatenate([window[place_ref[r, k]], window[place_ref[r, k + 1]]], axis=0)
        term = jnp.dot(left, right, preferred_element_type=jnp.float32)
        total = term if total is None else total + term
    out_ref[...] = total
    low_ref[...] = total.astype(jnp.bfloat16)


def product_of(place, tiles, pieces):
    block_rows, slots, tile, _ = tiles.shape
    modes = pieces[0].shape[-1]
    n = len(pieces)
    rows = block_rows * tile
    return pl.pallas_call(
        functools.partial(product_kernel, pieces=n),
        grid_spec=pltpu.PrefetchScalarGridSpec(
            num_scalar_prefetch=1,
            grid=(block_rows,),
            in_specs=[pl.BlockSpec((1, slots, tile, tile), lambda r, s: (r, 0, 0, 0))]
            + [pl.BlockSpec(memory_space=pl.ANY)] * n,
            out_specs=[pl.BlockSpec((tile, modes), lambda r, s: (r, 0))] * 2,
            scratch_shapes=[pltpu.VMEM((n * block_rows, tile, modes), jnp.bfloat16), pltpu.SemaphoreType.DMA((n,))],
        ),
        out_shape=[
            jax.ShapeDtypeStruct((rows, modes), jnp.float32),
            jax.ShapeDtypeStruct((rows, modes), jnp.bfloat16),
        ],
        cost_estimate=pl.CostEstimate(
            flops=2 * rows * slots * tile * modes, bytes_accessed=2 * tiles.size, transcendentals=0
        ),
        compiler_params=pltpu.CompilerParams(vmem_limit_bytes=20 * MIB),
    )(place, tiles, *[p.reshape(block_rows, tile, modes) for p in pieces])


def dot(a, b, dims=((1,), (0,))):
    return lax.dot_general(a, b, (dims, ((), ())), precision=HIGHEST, preferred_element_type=jnp.float32)


def pack(full, out_ref):
    h = full.shape[0] // 2
    out_ref[0:h, :] = full[:h, :h]
    out_ref[h : 2 * h, :] = full[h:, :h]
    out_ref[2 * h : 3 * h, :] = full[h:, h:]


def unpacked(ref):
    h = ref.shape[0] // 3
    a, b, d = ref[0:h, :], ref[h : 2 * h, :], ref[2 * h : 3 * h, :]
    return jnp.concatenate([jnp.concatenate([a, b.T], axis=1), jnp.concatenate([b, d], axis=1)], axis=0)


def first_sums_kernel(product_ref, rounded_ref, gram_ref, proj_ref):
    product = product_ref[...]
    pack(dot(product, product, ((0,), (0,))), gram_ref)
    pack(dot(rounded_ref[...].astype(jnp.float32), product, ((0,), (0,))), proj_ref)


def later_sums_kernel(raw_ref, sent_ref, inverse_ref, product_ref, gram_ref, proj_ref):
    inverse = inverse_ref[...]
    product = dot(raw_ref[...], inverse, ((1,), (1,)))
    product_ref[...] = product
    pack(dot(product, product, ((0,), (0,))), gram_ref)
    pack(dot(inverse, dot(sent_ref[...].astype(jnp.float32), product, ((0,), (0,)))), proj_ref)


def on_chip(kernel, out_shape, *args, flops=0):
    return pl.pallas_call(
        kernel,
        out_shape=out_shape,
        cost_estimate=pl.CostEstimate(flops=flops, bytes_accessed=2**20, transcendentals=0),
        compiler_params=pltpu.CompilerParams(vmem_limit_bytes=24 * MIB),
    )(*args)


def lane_bcast(x, j):
    return jnp.take_along_axis(x, jnp.full(x.shape, j, jnp.int32), axis=1)

def sub_bcast(x, i):
    return jnp.broadcast_to(x[i:i+1, :], x.shape)

def wide(x, n):
    return x if n == 1 else jnp.concatenate([x] * n, axis=1)

def reciprocal(x):
    return 1.0 / x

def rsqrt(x):
    y = lax.rsqrt(x)
    return y * (1.5 - 0.5 * x * y * y)

def inverse_factor(g):
    n = g.shape[0]
    groups, tiles = n // B, n // LANES
    row = lax.broadcasted_iota(jnp.int32, (n, n), 0)
    lane_n = lax.broadcasted_iota(jnp.int32, (n, n), 1)
    diagonal = jnp.where(row == lane_n, g, 0.0)
    scale_row = rsqrt(jnp.sum(diagonal, axis=0, keepdims=True))
    scale_col = rsqrt(jnp.sum(diagonal, axis=1, keepdims=True))
    g = g * scale_col * scale_row
    x = [g[B*k:B*k+B, :] for k in range(groups)]
    lane = lax.broadcasted_iota(jnp.int32, (B, n), 1)
    sub = lax.broadcasted_iota(jnp.int32, (B, n), 0)
    for k in range(groups - 1):
        t = B * k // LANES
        at = B * k % LANES
        tile = slice(t * LANES, (t + 1) * LANES)
        here = lane // B == k
        cols = [lane_bcast(x[k][:, tile], at + j) for j in range(B)]
        p = [[sub_bcast(cols[j], i) for j in range(B)] for i in range(B)]
        start = jnp.where(here, jnp.where(lane - B * k == sub, 1.0, 0.0), x[k])
        rows = [sub_bcast(start, i) for i in range(B)]
        for a in range(0, B, 2):
            b = a + 1
            inv = reciprocal(p[a][a] * p[b][b] - p[a][b] * p[a][b])
            i00, i01, i11 = p[b][b] * inv, -p[a][b] * inv, p[a][a] * inv
            w00, w01, w11 = wide(i00, tiles), wide(i01, tiles), wide(i11, tiles)
            rows[a], rows[b] = w00 * rows[a] + w01 * rows[b], w01 * rows[a] + w11 * rows[b]
            for j in range(b + 1, B):
                p[a][j], p[b][j] = i00 * p[a][j] + i01 * p[b][j], i01 * p[a][j] + i11 * p[b][j]
            for i in range(B):
                if i in (a, b):
                    continue
                ca, cb = p[i][a], p[i][b]
                rows[i] = rows[i] - (wide(ca, tiles) * rows[a] + wide(cb, tiles) * rows[b])
                for j in range(b + 1, B):
                    p[i][j] = p[i][j] - (ca * p[a][j] + cb * p[b][j])
        for i in range(k + 1, groups):
            c = [wide(lane_bcast(x[i][:, tile], at + j), tiles) for j in range(B)]
            s = [c[j] * rows[j] for j in range(B)]
            s = ((s[0] + s[1]) + (s[2] + s[3])) + ((s[4] + s[5]) + (s[6] + s[7]))
            x[i] = jnp.where(here, 0.0, x[i]) - s
    strip = jnp.zeros((B, n), jnp.float32)
    for k in range(groups):
        strip = jnp.where(lane // B == k, x[k], strip)
    w8 = []
    sub1 = sub[:, :LANES]
    lane1 = lane[:, :LANES]
    for t in range(tiles):
        d = strip[:, t * LANES:(t + 1) * LANES]
        base = lane1 // B * B
        cols = [jnp.take_along_axis(d, base + j, axis=1) for j in range(B)]
        p = [[sub_bcast(cols[j], i) for j in range(B)] for i in range(B)]
        m = [[None] * B for _ in range(B)]
        pivots = []
        for a in range(B):
            pivots.append(p[a][a])
            inv = reciprocal(p[a][a])
            for i in range(a + 1, B):
                l = p[i][a] * inv
                for j in range(a + 1, i + 1):
                    p[i][j] = p[i][j] - l * p[j][a]
                for j in range(a):
                    m[i][j] = m[i][j] - l * m[a][j]
                m[i][a] = -l
        out = jnp.zeros((B, LANES), jnp.float32)
        for i in range(B):
            r = rsqrt(pivots[i])
            for j in range(i + 1):
                v = r if i == j else r * m[i][j]
                out = jnp.where((sub1 == i) & (lane1 % B == j), v, out)
        w8.append(out)
    result = []
    for k in range(groups):
        t, at = B * k // LANES, B * k % LANES
        here = lane // B == k
        start = jnp.where(lane < B * k, x[k], jnp.where(here & (lane - B * k == sub), 1.0, 0.0))
        s = [wide(lane_bcast(w8[t], at + j), tiles) * sub_bcast(start, j) for j in range(B)]
        s = ((s[0] + s[1]) + (s[2] + s[3])) + ((s[4] + s[5]) + (s[6] + s[7]))
        result.append(s)
    return jnp.concatenate(result, axis=0) * scale_row

def inverse_kernel(gram_ref, inverse_ref):
    inverse_ref[...] = inverse_factor(unpacked(gram_ref))


def modes_kernel(scale, gram_ref, product_ref, modes_ref):
    inverse = inverse_factor(unpacked(gram_ref)) * scale
    modes_ref[...] = dot(product_ref[...], inverse, ((1,), (1,)))


def symmetric(packed):
    h = packed.shape[0] // 3
    a, b, d = packed[:h], packed[h : 2 * h], packed[2 * h :]
    return jnp.concatenate([jnp.concatenate([a, b.T], axis=1), jnp.concatenate([b, d], axis=1)], axis=0)


def per_device(tiles, pattern, basis):
    block_rows, _, tile, _ = tiles.shape
    rows, modes = basis.shape
    order = rows * lax.axis_size("rows")
    f32 = lambda *shape: jax.ShapeDtypeStruct(shape, jnp.float32)
    packed = f32(3 * modes // 2, modes // 2)
    chain = 200_000_000
    place = places(pattern, block_rows)

    rounded = basis.astype(jnp.bfloat16)
    product, sent = product_of(place, tiles, neighbourhood(rounded))
    pieces = neighbourhood(sent)
    gram, proj = on_chip(first_sums_kernel, (packed, packed), product, rounded, flops=24 * rows * modes * modes)
    gram, first = summed(gram), summed(proj)
    inverse = on_chip(inverse_kernel, f32(modes, modes), gram, flops=chain)

    raw, _ = product_of(place, tiles, pieces)
    product, gram, proj = on_chip(
        later_sums_kernel, (f32(rows, modes), packed, packed), raw, sent, inverse, flops=36 * rows * modes * modes
    )
    gram, second = summed(gram), summed(proj)
    out = on_chip(functools.partial(modes_kernel, math.sqrt(order)), f32(rows, modes), gram, product, flops=chain)
    return out, jnp.stack([symmetric(first), symmetric(second)])


def solution(mesh):
    placed = (
        P(("groups", "rows"), None, None, None),
        P(("groups", "rows"), None),
        P(("groups", "rows"), None),
    )
    return jax.shard_map(
        per_device,
        mesh=mesh,
        in_specs=placed,
        out_specs=(P(("groups", "rows"), None), P("groups", None, None)),
        check_vma=False,
    )
```

time: 501 us -> 164 us (0.33); the launches traced: 496 us -> 164 us
  waiting for transfers between devices: 257 us -> 80.1 us
  other arithmetic: 113 us -> 3.14 us
  Pallas kernels: 0 us -> 42.4 us
  local copies, waits for them, and re-layouts: 49.7 us -> 10.1 us
  matrix products: 39 us -> 0 us
  between operations: 17.1 us -> 0.94 us
  starting transfers between devices: 19.5 us -> 27.2 us
    psum x2 -> x0, waiting for transfers between devices: 185 us -> none  [per_device(): gram, projected_now = lax.psum((gram_part, proj_part), 'rows')]
    another operation x19 -> x2, other arithmetic: 109 us -> 0.87 us  [per_device(): return (out, jnp.stack([symmetric(first), symmetric(second)]))]
    pallas_call x0 -> x6, Pallas kernels: none -> 42.4 us  [the longest x4 28.8 us: on_chip(): pl.pallas_call(kernel, out_shape=out_shape, cost_estimate=pl.CostEstimate...]
    dot_general x8 -> x0, matrix products: 36.3 us -> none  [the longest x2 24.7 us: per_device(): jnp.einsum('rkij,rkjm->rim', tiles, picked, preferred_element_type=jnp.fl...]
    gather x2 -> x0, local copies, waits for them, and re-layouts: 26.7 us -> none  [per_device(): picked = jnp.take(window, local_cols, axis=0)]
    ppermute x12 -> x32, waiting for transfers between devices: 71.6 us -> 80.1 us  [permuted(): lax.ppermute(value, 'rows', [(i, target(i) % peers) for i in range(peers)])]
    another operation x19 -> x0, local copies, waits for them, and re-layouts: 7.99 us -> none  [the longest x15 7.94 us: per_device(): lax.linalg.triangular_solve(lower, jnp.eye(mode_count, dtype=jnp.float32)...]
    ppermute x12 -> x32, starting transfers between devices: 19.3 us -> 27.2 us  [permuted(): lax.ppermute(value, 'rows', [(i, target(i) % peers) for i in range(peers)])]
  transfers between devices with their start and end apart: 14 -> 32, of which waited for: 8 -> 20; matrix products, arithmetic and copies ran while one was open for 3% -> 1% of each run, Pallas kernels for 0% -> 15%
where the time goes in v1:
time: 164 us
  waiting for transfers between devices  80.1 us (49%)
  Pallas kernels  42.4 us (26%)
  starting transfers between devices  27.2 us (17%)
  local copies, waits for them, and re-layouts  10.1 us (6%)
  other arithmetic  3.14 us (2%)
    ppermute x32, waiting for transfers between devices, permuted(): lax.ppermute(value, 'rows', [(i, target(i) % peers) for i in range(peers)])  80.1 us
    pallas_call x4, Pallas kernels, on_chip(): pl.pallas_call(kernel, out_shape=out_shape, cost_estimate=pl.CostEstimate...  28.8 us
    ppermute x32, starting transfers between devices, permuted(): lax.ppermute(value, 'rows', [(i, target(i) % peers) for i in range(peers)])  27.2 us
    pallas_call x2, Pallas kernels, product_of(): pl.pallas_call(functools.partial(product_kernel, pieces=n), grid_spec=plt...  13.6 us
    unnamed x10, local copies, waits for them, and re-layouts  9.96 us
  transfers between devices with their start and end apart: 32, of which 20 were waited for; matrix products, arithmetic and copies ran while one was open for 1% of the time, Pallas kernels for 15%

profile of v1, /device:TPU:0, one launch (start us, length us, event | category | flops | bytes accessed | tf_op | source)
XLA Modules:
  0.0 163.9 jit_solution(15382869448024109947)
XLA Ops:
  0.6 1.3 convert_element_type.7.rounded_ref
  1.9 3.0 %collective-permute-start.1 = (bf16[1024,256]{1,0:T(8,128)(2,1)S(1)}, bf16[1024,256]{1,0:T(8,128)(2,1)S(1)}, u32[]{:S(2)}, u32[]{:S(2)}) collective-permute-start(bf16[1024,256]{1,0:T(8,128)(2,1)S(1)} %convert_element_type.7.rounded_ref), channel_id=1, source_target_pairs={{0,2},{1,3},{2,4},{3,5},{4,6},{5,7},{6,8},{7,9},{8,10},{9,11},{10,... | collective-permute-start | bytes 1572872 | tf_op jit(solution)/shard_map/ppermute | solution.py:20
  4.9 3.1 %collective-permute-start.3 = (bf16[1024,256]{1,0:T(8,128)(2,1)S(1)}, bf16[1024,256]{1,0:T(8,128)(2,1)S(1)}, u32[]{:S(2)}, u32[]{:S(2)}) collective-permute-start(bf16[1024,256]{1,0:T(8,128)(2,1)S(1)} %convert_element_type.7.rounded_ref), channel_id=1, source_target_pairs={{0,14},{1,15},{2,0},{3,1},{4,2},{5,3},{6,4},{7,5},{8,6},{9,7},{10,... | collective-permute-start | bytes 1572872 | tf_op jit(solution)/shard_map/ppermute | solution.py:20
  8.0 2.0 %collective-permute-start.5 = (bf16[1024,256]{1,0:T(8,128)(2,1)S(1)}, bf16[1024,256]{1,0:T(8,128)(2,1)S(1)}, u32[]{:S(2)}, u32[]{:S(2)}) collective-permute-start(bf16[1024,256]{1,0:T(8,128)(2,1)S(1)} %convert_element_type.7.rounded_ref), channel_id=1, source_target_pairs={{0,13},{1,4},{2,15},{3,6},{4,1},{5,8},{6,3},{7,10},{8,5},{9,12},{1... | collective-permute-start | bytes 1572872 | tf_op jit(solution)/shard_map/ppermute | solution.py:20
  10.1 17.3 %collective-permute-done.1 = bf16[1024,256]{1,0:T(8,128)(2,1)S(1)} collective-permute-done((bf16[1024,256]{1,0:T(8,128)(2,1)S(1)}, bf16[1024,256]{1,0:T(8,128)(2,1)S(1)}, u32[]{:S(2)}, u32[]{:S(2)}) %collective-permute-start.1) | collective-permute-done | bytes 524320 | tf_op jit(solution)/shard_map/ppermute | solution.py:20
  27.4 2.2 %collective-permute-done.3 = bf16[1024,256]{1,0:T(8,128)(2,1)S(1)} collective-permute-done((bf16[1024,256]{1,0:T(8,128)(2,1)S(1)}, bf16[1024,256]{1,0:T(8,128)(2,1)S(1)}, u32[]{:S(2)}, u32[]{:S(2)}) %collective-permute-start.3) | collective-permute-done | bytes 524320 | tf_op jit(solution)/shard_map/ppermute | solution.py:20
  29.6 0.7 fusion.5.place_ref
  30.3 0.9 collective-permute-done.5
  31.2 0.8 copy-done.2
  32.0 4.0 %copy-done = bf16[8,40,128,128]{3,2,1,0:T(8,128)(2,1)S(1)} copy-done((bf16[8,40,128,128]{3,2,1,0:T(8,128)(2,1)S(1)}, bf16[8,40,128,128]{3,2,1,0:T(8,128)(2,1)}, u32[]{:S(2)}) %copy-start) | copy-done | bytes 10485784
  35.9 1.0 copy-done.3
  37.0 6.4 %shard_map.50 = (f32[1024,256]{1,0:T(8,128)S(1)}, bf16[1024,256]{1,0:T(8,128)(2,1)S(1)}) custom-call(s32[8,40]{1,0:T(8,128)S(1)} %fusion.5.place_ref, bf16[8,40,128,128]{3,2,1,0:T(8,128)(2,1)S(1)} %copy-done, bf16[8,128,256]{2,1,0:T(8,128)(2,1)S(1)} %bitcast.21, bf16[8,128,256]{2,1,0:T(8,128)(2,1)S(1)} %bitcast.27, bf16[8,128,256]{2,1,0:T(8,128)(2,1)S(1)} %bitcast.25, ...), custom_call_target="tpu_custom_call" | custom-call | flops 2684354560 | bytes 10485760 | tf_op jit(solution)/shard_map/pallas_call | solution.py:89
  43.4 1.3 collective-permute-start.7
  44.7 3.5 %collective-permute-start.9 = (bf16[1024,256]{1,0:T(8,128)(2,1)S(1)}, bf16[1024,256]{1,0:T(8,128)(2,1)S(1)}, u32[]{:S(2)}, u32[]{:S(2)}) collective-permute-start(bf16[1024,256]{1,0:T(8,128)(2,1)S(1)} %get-tuple-element.10.sent_ref), channel_id=1, source_target_pairs={{0,14},{1,15},{2,0},{3,1},{4,2},{5,3},{6,4},{7,5},{8,6},{9,7},{10,... | collective-permute-start | bytes 1572872 | tf_op jit(solution)/shard_map/ppermute | solution.py:20
  48.1 1.9 %shard_map.52 = (f32[384,128]{1,0:T(8,128)S(1)}, f32[384,128]{1,0:T(8,128)S(1)}) custom-call(f32[1024,256]{1,0:T(8,128)S(1)} %get-tuple-element.12.product_ref, bf16[1024,256]{1,0:T(8,128)(2,1)S(1)} %convert_element_type.7.rounded_ref), custom_call_target="tpu_custom_call" | custom-call | flops 1610612736 | bytes 1048576 | tf_op jit(solution)/shard_map/pallas_call | solution.py:142
  50.2 0.5 collective-permute-start.22
  50.8 0.7 collective-permute-done.12
  51.7 2.0 %collective-permute-start.23 = (f32[192,128]{1,0:T(8,128)S(1)}, f32[192,128]{1,0:T(8,128)S(1)}, u32[]{:S(2)}, u32[]{:S(2)}) collective-permute-start(f32[192,128]{1,0:T(8,128)S(1)} %dynamic-slice_add_fusion.1), channel_id=1, source_target_pairs={{0,2},{1,3},{2,0},{3,1},{4,6},{5,7},{6,4},{7,5},{8,10},{9,11},{10,... | collective-permute-start | bytes 294920 | tf_op jit(solution)/shard_map/ppermute | solution.py:20
  53.7 19.1 %collective-permute-done.13 = f32[192,128]{1,0:T(8,128)S(1)} collective-permute-done((f32[192,128]{1,0:T(8,128)S(1)}, f32[192,128]{1,0:T(8,128)S(1)}, u32[]{:S(2)}, u32[]{:S(2)}) %collective-permute-start.13) | collective-permute-done | bytes 98336 | tf_op jit(solution)/shard_map/ppermute | solution.py:20
  72.9 1.0 collective-permute-done.23
  73.8 1.1 collective-permute-start.24
  75.0 1.9 %collective-permute-start.11 = (bf16[1024,256]{1,0:T(8,128)(2,1)S(1)}, bf16[1024,256]{1,0:T(8,128)(2,1)S(1)}, u32[]{:S(2)}, u32[]{:S(2)}) collective-permute-start(bf16[1024,256]{1,0:T(8,128)(2,1)S(1)} %get-tuple-element.10.sent_ref), channel_id=1, source_target_pairs={{0,13},{1,4},{2,15},{3,6},{4,1},{5,8},{6,3},{7,10},{8,5},{9,12},{1... | collective-permute-start | bytes 1572872 | tf_op jit(solution)/shard_map/ppermute | solution.py:20
  76.8 0.8 collective-permute-done.14
  77.7 0.5 collective-permute-start.8
  78.3 0.4 collective-permute-done.24
  78.7 2.3 %collective-permute-start.15 = (f32[192,128]{1,0:T(8,128)S(1)}, f32[192,128]{1,0:T(8,128)S(1)}, u32[]{:S(2)}, u32[]{:S(2)}) collective-permute-start(f32[192,128]{1,0:T(8,128)S(1)} %add.114), channel_id=1, source_target_pairs={{0,8},{1,9},{2,10},{3,11},{4,12},{5,13},{6,14},{7,15},{8,0},{9,1},... | collective-permute-start | bytes 294920 | tf_op jit(solution)/shard_map/ppermute | solution.py:20
  81.1 14.3 %collective-permute-done.15 = f32[192,128]{1,0:T(8,128)S(1)} collective-permute-done((f32[192,128]{1,0:T(8,128)S(1)}, f32[192,128]{1,0:T(8,128)S(1)}, u32[]{:S(2)}, u32[]{:S(2)}) %collective-permute-start.15) | collective-permute-done | bytes 98336 | tf_op jit(solution)/shard_map/ppermute | solution.py:20
  95.4 5.5 %collective-permute-done.25 = f32[192,128]{1,0:T(8,128)S(1)} collective-permute-done((f32[192,128]{1,0:T(8,128)S(1)}, f32[192,128]{1,0:T(8,128)S(1)}, u32[]{:S(2)}, u32[]{:S(2)}) %collective-permute-start.25) | collective-permute-done | bytes 98336 | tf_op jit(solution)/shard_map/ppermute | solution.py:20
  100.9 1.3 collective-permute-done.16
  102.4 9.6 %shard_map.53.inverse_ref = f32[256,256]{1,0:T(8,128)S(1)} custom-call(f32[384,128]{1,0:T(8,128)S(1)} %maximum_select_fusion.gram_ref), custom_call_target="tpu_custom_call" | custom-call | flops 200000000 | bytes 1048576 | tf_op jit(solution)/shard_map/pallas_call | solution.py:142
  112.0 4.0 %copy-done.1 = bf16[8,40,128,128]{3,2,1,0:T(8,128)(2,1)S(1)} copy-done((bf16[8,40,128,128]{3,2,1,0:T(8,128)(2,1)S(1)}, bf16[8,40,128,128]{3,2,1,0:T(8,128)(2,1)}, u32[]{:S(2)}) %copy-start.1) | copy-done | bytes 10485784
  116.0 7.2 %shard_map.51 = (f32[1024,256]{1,0:T(8,128)S(1)}, bf16[1024,256]{1,0:T(8,128)(2,1)}) custom-call(s32[8,40]{1,0:T(8,128)S(1)} %fusion.5.place_ref, bf16[8,40,128,128]{3,2,1,0:T(8,128)(2,1)S(1)} %copy-done.1, bf16[8,128,256]{2,1,0:T(8,128)(2,1)S(1)} %bitcast.22, bf16[8,128,256]{2,1,0:T(8,128)(2,1)S(1)} %bitcast.31, bf16[8,128,256]{2,1,0:T(8,128)(2,1)S(1)} %bitcast.23, ...), custom_call_target="tpu_custom_call" | custom-call | flops 2684354560 | bytes 10485760 | tf_op jit(solution)/shard_map/pallas_call | solution.py:89
  123.2 5.1 %shard_map.54 = (f32[1024,256]{1,0:T(8,128)S(1)}, f32[384,128]{1,0:T(8,128)S(1)}, f32[384,128]{1,0:T(8,128)S(1)}) custom-call(f32[1024,256]{1,0:T(8,128)S(1)} %get-tuple-element.11.raw_ref, bf16[1024,256]{1,0:T(8,128)(2,1)S(1)} %get-tuple-element.10.sent_ref, f32[256,256]{1,0:T(8,128)S(1)} %shard_map.53.inverse_ref), custom_call_target="tpu_custom_call" | custom-call | flops 2415919104 | bytes 1048576 | tf_op jit(solution)/shard_map/pallas_call | solution.py:142
  128.3 0.4 collective-permute-start.27
  128.9 0.7 collective-permute-done.27
  129.7 0.7 collective-permute-start.28
  130.4 1.5 collective-permute-start.18
  131.8 3.5 %collective-permute-done.28 = f32[192,128]{1,0:T(8,128)S(1)} collective-permute-done((f32[192,128]{1,0:T(8,128)S(1)}, f32[192,128]{1,0:T(8,128)S(1)}, u32[]{:S(2)}, u32[]{:S(2)}) %collective-permute-start.28) | collective-permute-done | bytes 98336 | tf_op jit(solution)/shard_map/ppermute | solution.py:20
  135.5 1.4 collective-permute-done.18
  136.9 0.7 collective-permute-start.19
  137.6 3.4 %collective-permute-done.29 = f32[192,128]{1,0:T(8,128)S(1)} collective-permute-done((f32[192,128]{1,0:T(8,128)S(1)}, f32[192,128]{1,0:T(8,128)S(1)}, u32[]{:S(2)}, u32[]{:S(2)}) %collective-permute-start.29) | collective-permute-done | bytes 98336 | tf_op jit(solution)/shard_map/ppermute | solution.py:20
  141.3 1.2 collective-permute-done.19
  142.6 1.6 collective-permute-start.20
  144.2 5.0 %collective-permute-done.30 = f32[192,128]{1,0:T(8,128)S(1)} collective-permute-done((f32[192,128]{1,0:T(8,128)S(1)}, f32[192,128]{1,0:T(8,128)S(1)}, u32[]{:S(2)}, u32[]{:S(2)}) %collective-permute-start.30) | collective-permute-done | bytes 98336 | tf_op jit(solution)/shard_map/ppermute | solution.py:20
  149.4 0.8 collective-permute-done.20
  150.3 0.2 collective-permute-done.31
  150.8 0.8 pad_maximum_fusion
  151.6 12.3 %shard_map.55 = f32[1024,256]{1,0:T(8,128)} custom-call(f32[384,128]{1,0:T(8,128)S(1)} %maximum_select_fusion.1.gram_ref, f32[1024,256]{1,0:T(8,128)S(1)} %get-tuple-element.15.product_ref), custom_call_target="tpu_custom_call" | custom-call | flops 200000000 | bytes 1048576 | tf_op jit(solution)/shard_map/pallas_call | solution.py:142
  (64 shorter events, 2.0 us)
Async XLA Ops:
  1.9 25.4 %collective-permute-start.1 = (bf16[1024,256]{1,0:T(8,128)(2,1)S(1)}, bf16[1024,256]{1,0:T(8,128)(2,1)S(1)}, u32[]{:S(2)}, u32[]{:S(2)}) collective-permute-start(bf16[1024,256]{1,0:T(8,128)(2,1)S(1)} %convert_element_type.7.rounded_ref), channel_id=1, source_target_pairs={{0,2},{1,3},{2,4},{3,5},{4,6},{5,7},{6,8},{7,9},{8,10},{9,11},{10,... | collective-permute-start | bytes 1572872 | tf_op jit(solution)/shard_map/ppermute | solution.py:20
  4.9 24.6 %collective-permute-start.3 = (bf16[1024,256]{1,0:T(8,128)(2,1)S(1)}, bf16[1024,256]{1,0:T(8,128)(2,1)S(1)}, u32[]{:S(2)}, u32[]{:S(2)}) collective-permute-start(bf16[1024,256]{1,0:T(8,128)(2,1)S(1)} %convert_element_type.7.rounded_ref), channel_id=1, source_target_pairs={{0,14},{1,15},{2,0},{3,1},{4,2},{5,3},{6,4},{7,5},{8,6},{9,7},{10,... | collective-permute-start | bytes 1572872 | tf_op jit(solution)/shard_map/ppermute | solution.py:20
  8.0 22.2 %collective-permute-start = (bf16[1024,256]{1,0:T(8,128)(2,1)S(1)}, bf16[1024,256]{1,0:T(8,128)(2,1)S(1)}, u32[]{:S(2)}, u32[]{:S(2)}) collective-permute-start(bf16[1024,256]{1,0:T(8,128)(2,1)S(1)} %convert_element_type.7.rounded_ref), channel_id=1, source_target_pairs={{0,1},{1,0},{2,3},{3,2},{4,5},{5,4},{6,7},{7,6},{8,9},{9,8},{10,11... | collective-permute-start | bytes 1572872 | tf_op jit(solution)/shard_map/ppermute | solution.py:20
  8.0 23.1 %collective-permute-start.5 = (bf16[1024,256]{1,0:T(8,128)(2,1)S(1)}, bf16[1024,256]{1,0:T(8,128)(2,1)S(1)}, u32[]{:S(2)}, u32[]{:S(2)}) collective-permute-start(bf16[1024,256]{1,0:T(8,128)(2,1)S(1)} %convert_element_type.7.rounded_ref), channel_id=1, source_target_pairs={{0,13},{1,4},{2,15},{3,6},{4,1},{5,8},{6,3},{7,10},{8,5},{9,12},{1... | collective-permute-start | bytes 1572872 | tf_op jit(solution)/shard_map/ppermute | solution.py:20
  27.3 3.8 %collective-permute-start.2 = (bf16[1024,256]{1,0:T(8,128)(2,1)S(1)}, bf16[1024,256]{1,0:T(8,128)(2,1)S(1)}, u32[]{:S(2)}, u32[]{:S(2)}) collective-permute-start(bf16[1024,256]{1,0:T(8,128)(2,1)S(1)} %collective-permute-done.1), channel_id=1, source_target_pairs={{0,1},{1,0},{2,3},{3,2},{4,5},{5,4},{6,7},{7,6},{8,9},{9,8},{10,11... | collective-permute-start | bytes 1572872 | tf_op jit(solution)/shard_map/ppermute | solution.py:20
  29.5 2.4 %collective-permute-start.4 = (bf16[1024,256]{1,0:T(8,128)(2,1)S(1)}, bf16[1024,256]{1,0:T(8,128)(2,1)}, u32[]{:S(2)}, u32[]{:S(2)}) collective-permute-start(bf16[1024,256]{1,0:T(8,128)(2,1)S(1)} %collective-permute-done.3), channel_id=1, source_target_pairs={{0,1},{1,0},{2,3},{3,2},{4,5},{5,4},{6,7},{7,6},{8,9},{9,8},{10,11... | collective-permute-start | bytes 1572872 | tf_op jit(solution)/shard_map/ppermute | solution.py:20
  31.2 0.8 copy-start.2
  32.0 4.0 %copy-start = (bf16[8,40,128,128]{3,2,1,0:T(8,128)(2,1)S(1)}, bf16[8,40,128,128]{3,2,1,0:T(8,128)(2,1)}, u32[]{:S(2)}) copy-start(bf16[8,40,128,128]{3,2,1,0:T(8,128)(2,1)} %tiles_ref.3) | copy-start | bytes 31457284
  35.9 1.0 copy-start.3
  43.4 34.3 %collective-permute-start.7 = (bf16[1024,256]{1,0:T(8,128)(2,1)S(1)}, bf16[1024,256]{1,0:T(8,128)(2,1)S(1)}, u32[]{:S(2)}, u32[]{:S(2)}) collective-permute-start(bf16[1024,256]{1,0:T(8,128)(2,1)S(1)} %get-tuple-element.10.sent_ref), channel_id=1, source_target_pairs={{0,2},{1,3},{2,4},{3,5},{4,6},{5,7},{6,8},{7,9},{8,10},{9,11},{10,... | collective-permute-start | bytes 1572872 | tf_op jit(solution)/shard_map/ppermute | solution.py:20
  44.7 33.5 %collective-permute-start.9 = (bf16[1024,256]{1,0:T(8,128)(2,1)S(1)}, bf16[1024,256]{1,0:T(8,128)(2,1)S(1)}, u32[]{:S(2)}, u32[]{:S(2)}) collective-permute-start(bf16[1024,256]{1,0:T(8,128)(2,1)S(1)} %get-tuple-element.10.sent_ref), channel_id=1, source_target_pairs={{0,14},{1,15},{2,0},{3,1},{4,2},{5,3},{6,4},{7,5},{8,6},{9,7},{10,... | collective-permute-start | bytes 1572872 | tf_op jit(solution)/shard_map/ppermute | solution.py:20
  50.1 1.4 collective-permute-start.12
  50.2 1.5 collective-permute-start.22
  51.5 21.3 %collective-permute-start.13 = (f32[192,128]{1,0:T(8,128)S(1)}, f32[192,128]{1,0:T(8,128)S(1)}, u32[]{:S(2)}, u32[]{:S(2)}) collective-permute-start(f32[192,128]{1,0:T(8,128)S(1)} %dynamic-slice_add_fusion.3), channel_id=1, source_target_pairs={{0,2},{1,3},{2,0},{3,1},{4,6},{5,7},{6,4},{7,5},{8,10},{9,11},{10,... | collective-permute-start | bytes 294920 | tf_op jit(solution)/shard_map/ppermute | solution.py:20
  51.7 22.1 %collective-permute-start.23 = (f32[192,128]{1,0:T(8,128)S(1)}, f32[192,128]{1,0:T(8,128)S(1)}, u32[]{:S(2)}, u32[]{:S(2)}) collective-permute-start(f32[192,128]{1,0:T(8,128)S(1)} %dynamic-slice_add_fusion.1), channel_id=1, source_target_pairs={{0,2},{1,3},{2,0},{3,1},{4,6},{5,7},{6,4},{7,5},{8,10},{9,11},{10,... | collective-permute-start | bytes 294920 | tf_op jit(solution)/shard_map/ppermute | solution.py:20
  72.8 4.9 %collective-permute-start.14 = (f32[192,128]{1,0:T(8,128)S(1)}, f32[192,128]{1,0:T(8,128)S(1)}, u32[]{:S(2)}, u32[]{:S(2)}) collective-permute-start(f32[192,128]{1,0:T(8,128)S(1)} %add.113), channel_id=1, source_target_pairs={{0,4},{1,5},{2,6},{3,7},{4,0},{5,1},{6,2},{7,3},{8,12},{9,13},{10,... | collective-permute-start | bytes 294920 | tf_op jit(solution)/shard_map/ppermute | solution.py:20
  73.8 4.9 %collective-permute-start.24 = (f32[192,128]{1,0:T(8,128)S(1)}, f32[192,128]{1,0:T(8,128)S(1)}, u32[]{:S(2)}, u32[]{:S(2)}) collective-permute-start(f32[192,128]{1,0:T(8,128)S(1)} %add.121), channel_id=1, source_target_pairs={{0,4},{1,5},{2,6},{3,7},{4,0},{5,1},{6,2},{7,3},{8,12},{9,13},{10,... | collective-permute-start | bytes 294920 | tf_op jit(solution)/shard_map/ppermute | solution.py:20
  75.0 37.0 %collective-permute-start.11 = (bf16[1024,256]{1,0:T(8,128)(2,1)S(1)}, bf16[1024,256]{1,0:T(8,128)(2,1)S(1)}, u32[]{:S(2)}, u32[]{:S(2)}) collective-permute-start(bf16[1024,256]{1,0:T(8,128)(2,1)S(1)} %get-tuple-element.10.sent_ref), channel_id=1, source_target_pairs={{0,13},{1,4},{2,15},{3,6},{4,1},{5,8},{6,3},{7,10},{8,5},{9,12},{1... | collective-permute-start | bytes 1572872 | tf_op jit(solution)/shard_map/ppermute | solution.py:20
  77.7 34.3 %collective-permute-start.6 = (bf16[1024,256]{1,0:T(8,128)(2,1)S(1)}, bf16[1024,256]{1,0:T(8,128)(2,1)S(1)}, u32[]{:S(2)}, u32[]{:S(2)}) collective-permute-start(bf16[1024,256]{1,0:T(8,128)(2,1)S(1)} %get-tuple-element.10.sent_ref), channel_id=1, source_target_pairs={{0,1},{1,0},{2,3},{3,2},{4,5},{5,4},{6,7},{7,6},{8,9},{9,8},{10,11... | collective-permute-start | bytes 1572872 | tf_op jit(solution)/shard_map/ppermute | solution.py:20
  77.7 34.3 %collective-permute-start.8 = (bf16[1024,256]{1,0:T(8,128)(2,1)S(1)}, bf16[1024,256]{1,0:T(8,128)(2,1)S(1)}, u32[]{:S(2)}, u32[]{:S(2)}) collective-permute-start(bf16[1024,256]{1,0:T(8,128)(2,1)S(1)} %collective-permute-done.7), channel_id=1, source_target_pairs={{0,1},{1,0},{2,3},{3,2},{4,5},{5,4},{6,7},{7,6},{8,9},{9,8},{10,11... | collective-permute-start | bytes 1572872 | tf_op jit(solution)/shard_map/ppermute | solution.py:20
  78.2 33.8 %collective-permute-start.10 = (bf16[1024,256]{1,0:T(8,128)(2,1)S(1)}, bf16[1024,256]{1,0:T(8,128)(2,1)}, u32[]{:S(2)}, u32[]{:S(2)}) collective-permute-start(bf16[1024,256]{1,0:T(8,128)(2,1)S(1)} %collective-permute-done.9), channel_id=1, source_target_pairs={{0,1},{1,0},{2,3},{3,2},{4,5},{5,4},{6,7},{7,6},{8,9},{9,8},{10,11... | collective-permute-start | bytes 1572872 | tf_op jit(solution)/shard_map/ppermute | solution.py:20
  78.7 16.6 %collective-permute-start.15 = (f32[192,128]{1,0:T(8,128)S(1)}, f32[192,128]{1,0:T(8,128)S(1)}, u32[]{:S(2)}, u32[]{:S(2)}) collective-permute-start(f32[192,128]{1,0:T(8,128)S(1)} %add.114), channel_id=1, source_target_pairs={{0,8},{1,9},{2,10},{3,11},{4,12},{5,13},{6,14},{7,15},{8,0},{9,1},... | collective-permute-start | bytes 294920 | tf_op jit(solution)/shard_map/ppermute | solution.py:20
  95.4 5.5 %collective-permute-start.25 = (f32[192,128]{1,0:T(8,128)S(1)}, f32[192,128]{1,0:T(8,128)S(1)}, u32[]{:S(2)}, u32[]{:S(2)}) collective-permute-start(f32[192,128]{1,0:T(8,128)S(1)} %add.122), channel_id=1, source_target_pairs={{0,8},{1,9},{2,10},{3,11},{4,12},{5,13},{6,14},{7,15},{8,0},{9,1},... | collective-permute-start | bytes 294920 | tf_op jit(solution)/shard_map/ppermute | solution.py:20
  100.9 1.3 collective-permute-start.16
  102.2 33.3 %collective-permute-start.26 = (f32[192,128]{1,0:T(8,128)S(1)}, f32[192,128]{1,0:T(8,128)S(1)}, u32[]{:S(2)}, u32[]{:S(2)}) collective-permute-start(f32[192,128]{1,0:T(8,128)S(1)} %add.123), channel_id=1, source_target_pairs={{0,1},{1,0},{2,3},{3,2},{4,5},{5,4},{6,7},{7,6},{8,9},{9,8},{10,11... | collective-permute-start | bytes 294920 | tf_op jit(solution)/shard_map/ppermute | solution.py:20
  112.0 4.0 %copy-start.1 = (bf16[8,40,128,128]{3,2,1,0:T(8,128)(2,1)S(1)}, bf16[8,40,128,128]{3,2,1,0:T(8,128)(2,1)}, u32[]{:S(2)}) copy-start(bf16[8,40,128,128]{3,2,1,0:T(8,128)(2,1)} %tiles_ref.3) | copy-start | bytes 31457284
  128.3 1.4 collective-permute-start.27
  128.7 1.7 %collective-permute-start.17 = (f32[192,128]{1,0:T(8,128)S(1)}, f32[192,128]{1,0:T(8,128)S(1)}, u32[]{:S(2)}, u32[]{:S(2)}) collective-permute-start(f32[192,128]{1,0:T(8,128)S(1)} %constant_dynamic-slice_fusion.2), channel_id=1, source_target_pairs={{0,1},{1,0},{2,3},{3,2},{4,5},{5,4},{6,7},{7,6},{8,9},{9,8},{10,11... | collective-permute-start | bytes 294920 | tf_op jit(solution)/shard_map/ppermute | solution.py:20
  129.7 5.7 %collective-permute-start.28 = (f32[192,128]{1,0:T(8,128)S(1)}, f32[192,128]{1,0:T(8,128)S(1)}, u32[]{:S(2)}, u32[]{:S(2)}) collective-permute-start(f32[192,128]{1,0:T(8,128)S(1)} %dynamic-slice_add_fusion), channel_id=1, source_target_pairs={{0,2},{1,3},{2,0},{3,1},{4,6},{5,7},{6,4},{7,5},{8,10},{9,11},{10,... | collective-permute-start | bytes 294920 | tf_op jit(solution)/shard_map/ppermute | solution.py:20
  130.4 6.5 %collective-permute-start.18 = (f32[192,128]{1,0:T(8,128)S(1)}, f32[192,128]{1,0:T(8,128)S(1)}, u32[]{:S(2)}, u32[]{:S(2)}) collective-permute-start(f32[192,128]{1,0:T(8,128)S(1)} %dynamic-slice_add_fusion.2), channel_id=1, source_target_pairs={{0,2},{1,3},{2,0},{3,1},{4,6},{5,7},{6,4},{7,5},{8,10},{9,11},{10,... | collective-permute-start | bytes 294920 | tf_op jit(solution)/shard_map/ppermute | solution.py:20
  135.4 5.6 %collective-permute-start.29 = (f32[192,128]{1,0:T(8,128)S(1)}, f32[192,128]{1,0:T(8,128)S(1)}, u32[]{:S(2)}, u32[]{:S(2)}) collective-permute-start(f32[192,128]{1,0:T(8,128)S(1)} %add.125), channel_id=1, source_target_pairs={{0,4},{1,5},{2,6},{3,7},{4,0},{5,1},{6,2},{7,3},{8,12},{9,13},{10,... | collective-permute-start | bytes 294920 | tf_op jit(solution)/shard_map/ppermute | solution.py:20
  136.9 5.6 %collective-permute-start.19 = (f32[192,128]{1,0:T(8,128)S(1)}, f32[192,128]{1,0:T(8,128)S(1)}, u32[]{:S(2)}, u32[]{:S(2)}) collective-permute-start(f32[192,128]{1,0:T(8,128)S(1)} %add.117), channel_id=1, source_target_pairs={{0,4},{1,5},{2,6},{3,7},{4,0},{5,1},{6,2},{7,3},{8,12},{9,13},{10,... | collective-permute-start | bytes 294920 | tf_op jit(solution)/shard_map/ppermute | solution.py:20
  141.0 8.2 %collective-permute-start.30 = (f32[192,128]{1,0:T(8,128)S(1)}, f32[192,128]{1,0:T(8,128)S(1)}, u32[]{:S(2)}, u32[]{:S(2)}) collective-permute-start(f32[192,128]{1,0:T(8,128)S(1)} %add.126), channel_id=1, source_target_pairs={{0,8},{1,9},{2,10},{3,11},{4,12},{5,13},{6,14},{7,15},{8,0},{9,1},... | collective-permute-start | bytes 294920 | tf_op jit(solution)/shard_map/ppermute | solution.py:20
  142.6 7.7 %collective-permute-start.20 = (f32[192,128]{1,0:T(8,128)S(1)}, f32[192,128]{1,0:T(8,128)S(1)}, u32[]{:S(2)}, u32[]{:S(2)}) collective-permute-start(f32[192,128]{1,0:T(8,128)S(1)} %add.118), channel_id=1, source_target_pairs={{0,8},{1,9},{2,10},{3,11},{4,12},{5,13},{6,14},{7,15},{8,0},{9,1},... | collective-permute-start | bytes 294920 | tf_op jit(solution)/shard_map/ppermute | solution.py:20
  149.2 1.4 collective-permute-start.31
  150.3 1.4 collective-permute-start.21

commit v2 on v0

v2 whole, which is shorter than its diff:
```python
import functools
import math

import jax
import jax.numpy as jnp
from jax import lax
from jax.experimental import pallas as pl
from jax.experimental.pallas import tpu as pltpu
from jax.sharding import PartitionSpec as P

B = 8
LANES = 128
CHUNK = 8
MIB = 2**20


def permuted(value, target):
    peers = lax.axis_size("rows")
    return lax.ppermute(value, "rows", [(i, target(i) % peers) for i in range(peers)])


def swapped(value):
    return permuted(value, lambda i: i ^ 1)


def after(value, *others):
    return lax.optimization_barrier((value, others))[0]


def neighbourhood(blocks, meanwhile, then=lambda made: made):
    before = permuted(blocks, lambda i: i + 2)
    behind = permuted(blocks, lambda i: i - 2)
    made = meanwhile()
    later = after(blocks, made)
    far = permuted(later, lambda i: i + 3 if i % 2 else i - 3)
    made = then(made)
    before, behind = after((before, behind), made)
    return [blocks, swapped(later), before, swapped(before), behind, swapped(behind), far], made


def kernel_call(kernel, out_shape, *args, flops=0, limit=16, **kwargs):
    return pl.pallas_call(
        kernel,
        out_shape=out_shape,
        cost_estimate=pl.CostEstimate(flops=flops, bytes_accessed=2**20, transcendentals=0),
        compiler_params=pltpu.CompilerParams(vmem_limit_bytes=limit * MIB),
        **kwargs,
    )(*args)


def prepare_kernel(pattern_ref, basis_ref, place_ref, rounded_ref, *, block_rows, peers):
    rounded_ref[...] = basis_ref[...].astype(jnp.bfloat16)
    me = lax.axis_index("rows")
    pattern = pattern_ref[...]
    owner = lax.div(pattern, block_rows)
    apart = lax.rem(lax.div(owner, 2) - lax.div(me, 2) + (2 + peers // 2), peers // 2) - 2
    crossed = lax.rem(owner + me, 2)
    piece = jnp.where(apart == 0, crossed, jnp.where(apart == -1, 2 + crossed, jnp.where(apart == 1, 4 + crossed, 6)))
    place_ref[...] = piece * block_rows + lax.rem(pattern, block_rows)


def held_kernel(tiles_ref, held_ref, sems):
    copies = [pltpu.make_async_copy(tiles_ref.at[r], held_ref.at[r], sems.at[r]) for r in range(tiles_ref.shape[0])]
    for c in copies:
        c.start()
    for c in copies:
        c.wait()


def held(tiles):
    return pl.pallas_call(
        held_kernel,
        in_specs=[pl.BlockSpec(memory_space=pltpu.HBM)],
        out_specs=pl.BlockSpec(memory_space=pltpu.VMEM),
        scratch_shapes=[pltpu.SemaphoreType.DMA((tiles.shape[0],))],
        out_shape=jax.ShapeDtypeStruct(tiles.shape, tiles.dtype),
        cost_estimate=pl.CostEstimate(flops=0, bytes_accessed=4 * tiles.size, transcendentals=0),
        compiler_params=pltpu.CompilerParams(vmem_limit_bytes=14 * MIB),
    )(tiles)


def product_kernel(place_ref, tiles_ref, *refs, pieces):
    piece_refs, (out_ref, low_ref, window) = refs[:pieces], refs[pieces:]
    block_rows, tile = piece_refs[0].shape[:2]
    for i in range(pieces):
        window[i * block_rows : (i + 1) * block_rows] = piece_refs[i][...]
    for r in range(block_rows):
        total = None
        for k in range(0, tiles_ref.shape[1], 2):
            left = jnp.concatenate([tiles_ref[r, k], tiles_ref[r, k + 1]], axis=1)
            right = jnp.concatenate([window[place_ref[r, k]], window[place_ref[r, k + 1]]], axis=0)
            term = jnp.dot(left, right, preferred_element_type=jnp.float32)
            total = term if total is None else total + term
        out_ref[r * tile : (r + 1) * tile, :] = total
        low_ref[r * tile : (r + 1) * tile, :] = total.astype(jnp.bfloat16)


def product_of(place, tiles, pieces):
    block_rows, slots, tile, _ = tiles.shape
    modes = pieces[0].shape[-1]
    n = len(pieces)
    rows = block_rows * tile
    return pl.pallas_call(
        functools.partial(product_kernel, pieces=n),
        in_specs=[pl.BlockSpec(memory_space=pltpu.SMEM)] + [pl.BlockSpec(memory_space=pltpu.VMEM)] * (n + 1),
        scratch_shapes=[pltpu.VMEM((n * block_rows, tile, modes), jnp.bfloat16)],
        out_shape=[
            jax.ShapeDtypeStruct((rows, modes), jnp.float32),
            jax.ShapeDtypeStruct((rows, modes), jnp.bfloat16),
        ],
        cost_estimate=pl.CostEstimate(
            flops=2 * rows * slots * tile * modes, bytes_accessed=2 * tiles.size, transcendentals=0
        ),
        compiler_params=pltpu.CompilerParams(vmem_limit_bytes=12 * MIB),
    )(place, tiles, *[p.reshape(block_rows, tile, modes) for p in pieces])


def dot(a, b, dims=((1,), (0,))):
    return lax.dot_general(a, b, (dims, ((), ())), precision=lax.Precision.HIGHEST, preferred_element_type=jnp.float32)


def write_sums(product_ref, rounded_ref, out_refs):
    down = ((0,), (0,))
    h = product_ref.shape[1] // 2
    pa, pb = product_ref[:, :h], product_ref[:, h:]
    xa, xb = rounded_ref[:, :h].astype(jnp.float32), rounded_ref[:, h:].astype(jnp.float32)
    core = lax.rem(lax.axis_index("rows"), 2)
    for (mine_ref, rest_ref), la, lb in ((out_refs[:2], pa, pb), (out_refs[-2:], xa, xb)):
        low, mid, high = dot(la, pa, down), dot(lb, pa, down), dot(lb, pb, down)
        first = jnp.concatenate([low, mid[: h // 2]], axis=0)
        last = jnp.concatenate([mid[h // 2 :], high], axis=0)
        to = slice(None) if len(out_refs) == 4 else slice(0, 3 * h // 2) if la is pa else slice(3 * h // 2, 3 * h)
        mine_ref[to, :] = jnp.where(core == 0, first, last)
        rest_ref[to, :] = jnp.where(core == 0, last, first)


def first_sums_kernel(product_ref, rounded_ref, *out_refs):
    write_sums(product_ref, rounded_ref, out_refs)


def later_sums_kernel(product_ref, rounded_ref, a_ref, b_ref, added_ref, *out_refs):
    write_sums(product_ref, rounded_ref, out_refs)
    added_ref[...] = a_ref[...] + b_ref[...]


def added_kernel(a_ref, b_ref, out_ref):
    out_ref[...] = a_ref[...] + b_ref[...]


def added(a, b):
    return kernel_call(added_kernel, jax.ShapeDtypeStruct(a.shape, a.dtype), a, b, limit=4)


def summed(mine, rest, first=1, last=None):
    step = first
    while step < (last or lax.axis_size("rows")):
        mine = added(mine, permuted(rest if step == 1 else mine, lambda i: i ^ step))
        step *= 2
    return mine


def unpacked(mine, rest):
    core = lax.rem(lax.axis_index("rows"), 2)
    first, last = jnp.where(core == 0, mine, rest), jnp.where(core == 0, rest, mine)
    h = 2 * mine.shape[0] // 3
    a, d = first[:h], last[h // 2 :]
    b = jnp.concatenate([first[h:], last[: h // 2]], axis=0)
    return jnp.concatenate([jnp.concatenate([a, b.T], axis=1), jnp.concatenate([b, d], axis=1)], axis=0)


def lane_bcast(x, j):
    return jnp.take_along_axis(x, jnp.broadcast_to(j, x.shape).astype(jnp.int32), axis=1)


def sub_bcast(x, i):
    return jnp.broadcast_to(x[i : i + 1, :], x.shape)


def wide(x, n):
    return x if n == 1 else jnp.concatenate([x] * n, axis=1)


def rsqrt(x):
    y = lax.rsqrt(x)
    return y * (1.5 - 0.5 * x * y * y)


def tree(terms):
    while len(terms) > 1:
        terms = [a + b for a, b in zip(terms[::2], terms[1::2])]
    return terms[0]


def pivot_rows(xk, k, tile, at, lane, sub, tiles):
    here = lane // B == k
    cols = [lane_bcast(xk[:, tile], at + j) for j in range(B)]
    p = [[None] * B for i in range(B)]
    for i in range(B):
        for j in range(i, B):
            p[i][j] = p[j][i] = sub_bcast(cols[j], i)
    start = jnp.where(here, jnp.where(lane - B * k == sub, 1.0, 0.0), xk)
    rows = [sub_bcast(start, i) for i in range(B)]
    for a in range(0, B, 2):
        b, c, d = a + 1, a + 2, a + 3
        if a % 4 == 0:
            det = p[a][a] * p[b][b] - p[a][b] * p[a][b]
            inv = 1.0 / det
            i00, i01, i11 = p[b][b] * inv, -p[a][b] * inv, p[a][a] * inv
            def schur(i, j):
                left = p[b][b] * p[a][j] - p[a][b] * p[b][j]
                right = p[a][a] * p[b][j] - p[a][b] * p[a][j]
                return det * p[i][j] - (p[i][a] * left + p[i][b] * right)

            scc, scd, sdd = schur(c, c), schur(c, d), schur(d, d)
            follow = det / (scc * sdd - scd * scd)
        else:
            i00, i01, i11 = sdd * follow, -scd * follow, scc * follow
        w00, w01, w11 = wide(i00, tiles), wide(i01, tiles), wide(i11, tiles)
        rows[a], rows[b] = w00 * rows[a] + w01 * rows[b], w01 * rows[a] + w11 * rows[b]
        for j in range(b + 1, B):
            p[a][j], p[b][j] = i00 * p[a][j] + i01 * p[b][j], i01 * p[a][j] + i11 * p[b][j]
        for i in range(B):
            if i in (a, b):
                continue
            ca, cb = p[i][a], p[i][b]
            rows[i] = rows[i] - (wide(ca, tiles) * rows[a] + wide(cb, tiles) * rows[b])
            for j in range(b + 1, B):
                p[i][j] = p[i][j] - (ca * p[a][j] + cb * p[b][j])
    return rows


def pivot_factors(d, sub, lane):
    base = lane // B * B
    cols = [jnp.take_along_axis(d, base + j, axis=1) for j in range(B)]
    p = [[sub_bcast(cols[j], i) for j in range(B)] for i in range(B)]
    m = [[None] * B for _ in range(B)]
    out = jnp.zeros(d.shape, jnp.float32)
    for a in range(B):
        inv = 1.0 / p[a][a]
        for i in range(a + 1, B):
            l = p[i][a] * inv
            for j in range(a + 1, i + 1):
                p[i][j] = p[i][j] - l * p[j][a]
            for j in range(a):
                m[i][j] = m[i][j] - l * m[a][j]
            m[i][a] = -l
    for i in range(B):
        r = rsqrt(p[i][i])
        for j in range(i + 1):
            out = jnp.where((sub == i) & (lane % B == j), r if i == j else r * m[i][j], out)
    return out


def eliminated_block(x, first, groups, lane, sub, tiles):
    acting = []
    for s in range(groups):
        k = first + s
        t = k * B // LANES
        tile, at = slice(t * LANES, (t + 1) * LANES), k * B - t * LANES
        here = lane // B == k
        rows = pivot_rows(x[s], k, tile, at, lane, sub, tiles)
        for i in range(s + 1, groups):
            c = [wide(lane_bcast(x[i][:, tile], at + j), tiles) for j in range(B)]
            x[i] = jnp.where(here, 0.0, x[i]) - tree([c[j] * rows[j] for j in range(B)])
        own = rows[0]
        for j in range(1, B):
            own = jnp.where(sub == j, rows[j], own)
        acting.append(jnp.where((lane // B > k) & (lane // B < first + groups), 0.0, own))
    return x, acting


def inverse_factors(grams):
    n = grams[0].shape[0]
    tiles, many, per = n // LANES, range(len(grams)), CHUNK
    lane = lax.broadcasted_iota(jnp.int32, (B, n), 1)
    sub = lax.broadcasted_iota(jnp.int32, (B, n), 0)
    row = lax.broadcasted_iota(jnp.int32, (n, n), 0)
    all_lanes = lax.broadcasted_iota(jnp.int32, (n, n), 1)
    rest, scales, done = [], [], [[] for _ in many]
    for g in grams:
        d = jnp.where(row == all_lanes, g, 0.0)
        scales.append(rsqrt(jnp.sum(d, axis=0, keepdims=True)))
        rest.append(g * rsqrt(jnp.sum(d, axis=1, keepdims=True)) * scales[-1])
    for first in range(0, n // B, per):
        size = per * B
        lo = first * B
        both = [
            eliminated_block([rest[m][i * B : i * B + B, :] for i in range(per)], first, per, lane, sub, tiles)
            for m in many
        ]
        for m in many:
            x, acting = both[m]
            done[m] += x
            if lo + size < n:
                left = jnp.concatenate(x, axis=0)
                below = (lo + size) // LANES * LANES
                update = dot(left[:, below:], jnp.concatenate(acting, axis=0), ((0,), (0,)))[lo + size - below :]
                inside = all_lanes[lo + size :] // size == lo // size
                rest[m] = jnp.where(inside, 0.0, rest[m][size:]) - update
    result = []
    for m in many:
        strip = done[m][0]
        for k in range(1, n // B):
            strip = jnp.where(lane // B == k, done[m][k], strip)
        factors = [pivot_factors(strip[:, t * LANES : (t + 1) * LANES], sub[:, :LANES], lane[:, :LANES]) for t in range(tiles)]
        out = []
        for k in range(n // B):
            t, at = k * B // LANES, k * B % LANES
            unit = jnp.where((lane // B == k) & (lane - B * k == sub), 1.0, 0.0)
            start = jnp.where(lane < B * k, done[m][k], unit)
            out.append(tree([wide(lane_bcast(factors[t], at + j), tiles) * sub_bcast(start, j) for j in range(B)]))
        result.append(jnp.concatenate(out, axis=0) * scales[m])
    return result


def modes_kernel(first_ref, first_rest_ref, raw_ref, raw_rest_ref, product_ref, modes_ref, inverse_ref, *, scale):
    n = raw_ref.shape[0]
    first = unpacked(first_ref[:n, :], first_rest_ref[:n, :])
    inverse, both = inverse_factors([first, unpacked(raw_ref[...], raw_rest_ref[...])])
    h = both.shape[0] // 2
    along = ((1,), (1,))
    both = both * scale
    modes_ref[:, :h] = dot(product_ref[:, :h], both[:h, :h], along)
    modes_ref[:, h:] = dot(product_ref[...], both[h:, :], along)
    inverse_ref[...] = inverse


def projected_kernel(first_ref, first_rest_ref, proj_ref, proj_rest_ref, inverse_ref, projected_ref):
    n = proj_ref.shape[0]
    inverse = inverse_ref[...]
    projected_ref[0] = unpacked(first_ref[n:, :], first_rest_ref[n:, :])
    proj = unpacked(proj_ref[...], proj_rest_ref[...])
    projected_ref[1] = dot(dot(inverse, proj), inverse, ((1,), (1,)))


def per_device(tiles, pattern, basis):
    block_rows, _, tile, _ = tiles.shape
    rows, modes = basis.shape
    peers = lax.axis_size("rows")
    shape = jax.ShapeDtypeStruct
    half_sum = 3 * modes // 4
    flops = 12 * rows * modes * modes
    place, rounded = kernel_call(
        functools.partial(prepare_kernel, block_rows=block_rows, peers=peers),
        (shape(pattern.shape, jnp.int32), shape((rows, modes), jnp.bfloat16)),
        pattern, basis,
        limit=8,
    )
    pieces, tiles = neighbourhood(rounded, lambda: held(tiles))
    product, sent = product_of(place, tiles, pieces)
    both = (shape((2 * half_sum, modes // 2), jnp.float32),) * 2
    pieces, first = neighbourhood(
        sent,
        lambda: summed(*kernel_call(first_sums_kernel, both, product, rounded, flops=flops), 1, 2),
        lambda made: summed(made, None, 2, 4),
    )
    partner = permuted(first, lambda i: i ^ 4)

    raw, _ = product_of(place, tiles, pieces)
    single = (shape((half_sum, modes // 2), jnp.float32),) * 4
    first, gram, gram_rest, proj, proj_rest = kernel_call(
        later_sums_kernel, (both[0],) + single, raw, sent, first, partner, flops=flops
    )
    first = summed(first, None, 8)
    first_rest = swapped(first)
    gram, proj = summed(gram, gram_rest), summed(proj, proj_rest)
    modes_out, inverse = kernel_call(
        functools.partial(modes_kernel, scale=math.sqrt(rows * peers)),
        (shape((rows, modes), jnp.float32), shape((modes, modes), jnp.float32)),
        first, first_rest, gram, swapped(gram), raw,
        flops=4_000_000_000,
    )
    projected = kernel_call(
        projected_kernel, shape((2, modes, modes), jnp.float32), first, first_rest, proj, swapped(proj), inverse
    )
    return modes_out, projected


def solution(mesh):
    placed = (
        P(("groups", "rows"), None, None, None),
        P(("groups", "rows"), None),
        P(("groups", "rows"), None),
    )
    return jax.shard_map(
        per_device,
        mesh=mesh,
        in_specs=placed,
        out_specs=(P(("groups", "rows"), None), P("groups", None, None)),
        check_vma=False,
    )
```

time: 501 us -> 119 us (0.24)
  waiting for transfers between devices: 257 us -> 54.7 us
  other arithmetic: 113 us -> 0 us
  local copies, waits for them, and re-layouts: 49.7 us -> 5.88 us
  matrix products: 39 us -> 0 us
  Pallas kernels: 0 us -> 30.4 us
  between operations: 17.1 us -> 0.82 us
  starting transfers between devices: 19.5 us -> 26.6 us
    psum x2 -> x0, waiting for transfers between devices: 185 us -> none  [per_device(): gram, projected_now = lax.psum((gram_part, proj_part), 'rows')]
    another operation x19 -> x0, other arithmetic: 109 us -> none  [the longest x13 68.8 us: per_device(): lower = jnp.linalg.cholesky(gram)]
    dot_general x8 -> x0, matrix products: 36.3 us -> none  [the longest x2 24.7 us: per_device(): jnp.einsum('rkij,rkjm->rim', tiles, picked, preferred_element_type=jnp.fl...]
    pallas_call x0 -> x19, Pallas kernels: none -> 30.4 us  [the longest x16 20.8 us: kernel_call(): pl.pallas_call(kernel, out_shape=out_shape, cost_estimate=pl.CostEstimate...]
    gather x2 -> x0, local copies, waits for them, and re-layouts: 26.7 us -> none  [per_device(): picked = jnp.take(window, local_cols, axis=0)]
    ppermute x12 -> x27, waiting for transfers between devices: 71.6 us -> 54.7 us  [permuted(): lax.ppermute(value, 'rows', [(i, target(i) % peers) for i in range(peers)])]
    another operation x19 -> x0, local copies, waits for them, and re-layouts: 7.99 us -> none  [the longest x15 7.94 us: per_device(): lax.linalg.triangular_solve(lower, jnp.eye(mode_count, dtype=jnp.float32)...]
    ppermute x12 -> x27, starting transfers between devices: 19.3 us -> 26.6 us  [permuted(): lax.ppermute(value, 'rows', [(i, target(i) % peers) for i in range(peers)])]
  transfers between devices with their start and end apart: 14 -> 27, of which waited for: 8 -> 15; matrix products, arithmetic and copies ran while one was open for 3% -> 0% of each run, Pallas kernels for 0% -> 18%
where the time goes in v2:
time: 119 us; the launch traced here: 118 us
  waiting for transfers between devices  54.7 us (46%)
  Pallas kernels  30.4 us (26%)
  starting transfers between devices  26.6 us (22%)
  local copies, waits for them, and re-layouts  5.88 us (5%)
    ppermute x27, waiting for transfers between devices, permuted(): lax.ppermute(value, 'rows', [(i, target(i) % peers) for i in range(peers)])  54.7 us
    ppermute x27, starting transfers between devices, permuted(): lax.ppermute(value, 'rows', [(i, target(i) % peers) for i in range(peers)])  26.6 us
    pallas_call x16, Pallas kernels, kernel_call(): pl.pallas_call(kernel, out_shape=out_shape, cost_estimate=pl.CostEstimate...  20.8 us
    pallas_call x2, Pallas kernels, product_of(): pl.pallas_call(functools.partial(product_kernel, pieces=n), in_specs=[pl....  8.82 us
    unnamed x6, local copies, waits for them, and re-layouts  5.88 us
  transfers between devices with their start and end apart: 27, of which 15 were waited for; matrix products, arithmetic and copies ran while one was open for 0% of the time, Pallas kernels for 18%

profile of v2, /device:TPU:0, one launch (start us, length us, event | category | flops | bytes accessed | tf_op | source)
XLA Modules:
  0.0 118.4 jit_solution(886653128042830858)
XLA Ops:
  0.6 1.2 %copy-done.1 = f32[1024,256]{1,0:T(8,128)S(1)} copy-done((f32[1024,256]{1,0:T(8,128)S(1)}, f32[1024,256]{1,0:T(8,128)}, u32[]{:S(2)}) %copy-start.1) | copy-done | bytes 1048600
  1.9 0.7 copy-done.2
  2.5 0.1 shard_map.50
  2.6 3.0 %collective-permute-start.1 = (bf16[1024,256]{1,0:T(8,128)(2,1)S(1)}, bf16[1024,256]{1,0:T(8,128)(2,1)S(1)}, u32[]{:S(2)}, u32[]{:S(2)}) collective-permute-start(bf16[1024,256]{1,0:T(8,128)(2,1)S(1)} %get-tuple-element.24.rounded_ref), channel_id=1, source_target_pairs={{0,2},{1,3},{2,4},{3,5},{4,6},{5,7},{6,8},{7,9},{8,10},{9,11},{10,... | collective-permute-start | bytes 1572872 | tf_op jit(solution)/shard_map/ppermute | solution.py:19
  5.6 3.1 %collective-permute-start.2 = (bf16[1024,256]{1,0:T(8,128)(2,1)S(1)}, bf16[1024,256]{1,0:T(8,128)(2,1)S(1)}, u32[]{:S(2)}, u32[]{:S(2)}) collective-permute-start(bf16[1024,256]{1,0:T(8,128)(2,1)S(1)} %get-tuple-element.24.rounded_ref), channel_id=1, source_target_pairs={{0,14},{1,15},{2,0},{3,1},{4,2},{5,3},{6,4},{7,5},{8,6},{9,7},{10,... | collective-permute-start | bytes 1572872 | tf_op jit(solution)/shard_map/ppermute | solution.py:19
  8.7 4.0 %copy-done = bf16[8,40,128,128]{3,2,1,0:T(8,128)(2,1)S(1)} copy-done((bf16[8,40,128,128]{3,2,1,0:T(8,128)(2,1)S(1)}, bf16[8,40,128,128]{3,2,1,0:T(8,128)(2,1)}, u32[]{:S(2)}) %copy-start) | copy-done | bytes 10485784
  12.7 0.8 shard_map.51.tiles_ref
  13.5 0.1 collective-permute-start
  13.6 2.0 %collective-permute-start.5 = (bf16[1024,256]{1,0:T(8,128)(2,1)S(1)}, bf16[1024,256]{1,0:T(8,128)(2,1)S(1)}, u32[]{:S(2)}, u32[]{:S(2)}) collective-permute-start(bf16[1024,256]{1,0:T(8,128)(2,1)S(1)} %get-tuple-element.24.rounded_ref), channel_id=1, source_target_pairs={{0,13},{1,4},{2,15},{3,6},{4,1},{5,8},{6,3},{7,10},{8,5},{9,12},{1... | collective-permute-start | bytes 1572872 | tf_op jit(solution)/shard_map/ppermute | solution.py:19
  15.6 12.5 %collective-permute-done.1 = bf16[1024,256]{1,0:T(8,128)(2,1)S(1)} collective-permute-done((bf16[1024,256]{1,0:T(8,128)(2,1)S(1)}, bf16[1024,256]{1,0:T(8,128)(2,1)S(1)}, u32[]{:S(2)}, u32[]{:S(2)}) %collective-permute-start.1) | collective-permute-done | bytes 524320 | tf_op jit(solution)/shard_map/ppermute | solution.py:19
  28.1 2.2 %collective-permute-done.2 = bf16[1024,256]{1,0:T(8,128)(2,1)S(1)} collective-permute-done((bf16[1024,256]{1,0:T(8,128)(2,1)S(1)}, bf16[1024,256]{1,0:T(8,128)(2,1)S(1)}, u32[]{:S(2)}, u32[]{:S(2)}) %collective-permute-start.2) | collective-permute-done | bytes 524320 | tf_op jit(solution)/shard_map/ppermute | solution.py:19
  30.3 0.5 collective-permute-start.4
  30.8 1.1 collective-permute-done.5
  31.9 0.3 collective-permute-done.3
  32.2 0.7 collective-permute-done.4
  32.9 4.0 %shard_map.52 = (f32[1024,256]{1,0:T(8,128)S(1)}, bf16[1024,256]{1,0:T(8,128)(2,1)S(1)}) custom-call(s32[8,40]{1,0:T(8,128)S(1)} %get-tuple-element.22.place_ref, bf16[8,40,128,128]{3,2,1,0:T(8,128)(2,1)S(1)} %shard_map.51.tiles_ref, bf16[8,128,256]{2,1,0:T(8,128)(2,1)S(1)} %bitcast.17, bf16[8,128,256]{2,1,0:T(8,128)(2,1)S(1)} %bitcast.22, ...), custom_call_target="tpu_custom_call" | custom-call | flops 2684354560 | bytes 10485760 | tf_op jit(solution)/shard_map/pallas_call | solution.py:103
  36.9 0.3 collective-permute-start.8
  37.3 4.4 %collective-permute-start.9 = (bf16[1024,256]{1,0:T(8,128)(2,1)S(1)}, bf16[1024,256]{1,0:T(8,128)(2,1)S(1)}, u32[]{:S(2)}, u32[]{:S(2)}) collective-permute-start(bf16[1024,256]{1,0:T(8,128)(2,1)S(1)} %get-tuple-element.31.rounded_ref), channel_id=1, source_target_pairs={{0,14},{1,15},{2,0},{3,1},{4,2},{5,3},{6,4},{7,5},{8,6},{9,7},{10,... | collective-permute-start | bytes 1572872 | tf_op jit(solution)/shard_map/ppermute | solution.py:19
  41.7 2.8 %shard_map.53 = (f32[384,128]{1,0:T(8,128)S(1)}, f32[384,128]{1,0:T(8,128)S(1)}) custom-call(f32[1024,256]{1,0:T(8,128)S(1)} %get-tuple-element.28.product_ref, bf16[1024,256]{1,0:T(8,128)(2,1)S(1)} %get-tuple-element.24.rounded_ref), custom_call_target="tpu_custom_call" | custom-call | flops 805306368 | bytes 1048576 | tf_op jit(solution)/shard_map/pallas_call | solution.py:42
  44.5 0.1 collective-permute-start.6
  44.6 1.4 %collective-permute-done.6.b_ref = f32[384,128]{1,0:T(8,128)S(1)} collective-permute-done((f32[384,128]{1,0:T(8,128)S(1)}, f32[384,128]{1,0:T(8,128)S(1)}, u32[]{:S(2)}, u32[]{:S(2)}) %collective-permute-start.6) | collective-permute-done | bytes 196640 | tf_op jit(solution)/shard_map/ppermute | solution.py:19
  46.0 0.1 collective-permute-start.10
  46.1 1.3 %collective-permute-start.13 = (bf16[1024,256]{1,0:T(8,128)(2,1)S(1)}, bf16[1024,256]{1,0:T(8,128)(2,1)S(1)}, u32[]{:S(2)}, u32[]{:S(2)}) collective-permute-start(bf16[1024,256]{1,0:T(8,128)(2,1)S(1)} %get-tuple-element.31.rounded_ref), channel_id=1, source_target_pairs={{0,13},{1,4},{2,15},{3,6},{4,1},{5,8},{6,3},{7,10},{8,5},{9,12},{1... | collective-permute-start | bytes 1572872 | tf_op jit(solution)/shard_map/ppermute | solution.py:19
  47.4 19.7 %collective-permute-done.10.b_ref = f32[384,128]{1,0:T(8,128)S(1)} collective-permute-done((f32[384,128]{1,0:T(8,128)S(1)}, f32[384,128]{1,0:T(8,128)S(1)}, u32[]{:S(2)}, u32[]{:S(2)}) %collective-permute-start.10) | collective-permute-done | bytes 196640 | tf_op jit(solution)/shard_map/ppermute | solution.py:19
  67.1 0.1 collective-permute-start.11
  67.2 0.5 collective-permute-start.12
  67.7 1.5 %collective-permute-start.14 = (f32[384,128]{1,0:T(8,128)S(1)}, f32[384,128]{1,0:T(8,128)S(1)}, u32[]{:S(2)}, u32[]{:S(2)}) collective-permute-start(f32[384,128]{1,0:T(8,128)S(1)} %shard_map.55.a_ref), channel_id=1, source_target_pairs={{0,4},{1,5},{2,6},{3,7},{4,0},{5,1},{6,2},{7,3},{8,12},{9,13},{10,... | collective-permute-start | bytes 589832 | tf_op jit(solution)/shard_map/ppermute | solution.py:19
  69.2 0.7 collective-permute-done.12
  69.9 4.8 %shard_map.56 = (f32[1024,256]{1,0:T(8,128)S(1)}, bf16[1024,256]{1,0:T(8,128)(2,1)}) custom-call(s32[8,40]{1,0:T(8,128)S(1)} %get-tuple-element.22.place_ref, bf16[8,40,128,128]{3,2,1,0:T(8,128)(2,1)S(1)} %shard_map.51.tiles_ref, bf16[8,128,256]{2,1,0:T(8,128)(2,1)S(1)} %bitcast.14, bf16[8,128,256]{2,1,0:T(8,128)(2,1)S(1)} %bitcast.19, ...), custom_call_target="tpu_custom_call" | custom-call | flops 2684354560 | bytes 10485760 | tf_op jit(solution)/shard_map/pallas_call | solution.py:103
  74.7 2.8 %shard_map.57 = (f32[384,128]{1,0:T(8,128)S(1)}, f32[192,128]{1,0:T(8,128)S(1)}, f32[192,128]{1,0:T(8,128)S(1)}, f32[192,128]{1,0:T(8,128)S(1)}, f32[192,128]{1,0:T(8,128)S(1)}) custom-call(f32[1024,256]{1,0:T(8,128)S(1)} %get-tuple-element.34.product_ref, bf16[1024,256]{1,0:T(8,128)(2,1)S(1)} %get-tuple-element.31.rounded_ref, ...), custom_call_target="tpu_custom_call" | custom-call | flops 805306368 | bytes 1048576 | tf_op jit(solution)/shard_map/pallas_call | solution.py:42
  77.4 0.2 collective-permute-start.17
  77.6 0.4 collective-permute-start.22
  78.0 2.5 %collective-permute-start.15 = (f32[384,128]{1,0:T(8,128)S(1)}, f32[384,128]{1,0:T(8,128)S(1)}, u32[]{:S(2)}, u32[]{:S(2)}) collective-permute-start(f32[384,128]{1,0:T(8,128)S(1)} %get-tuple-element.35.a_ref), channel_id=1, source_target_pairs={{0,8},{1,9},{2,10},{3,11},{4,12},{5,13},{6,14},{7,15},{8,0},{9,1},... | collective-permute-start | bytes 589832 | tf_op jit(solution)/shard_map/ppermute | solution.py:19
  80.6 2.1 %collective-permute-start.23 = (f32[192,128]{1,0:T(8,128)S(1)}, f32[192,128]{1,0:T(8,128)S(1)}, u32[]{:S(2)}, u32[]{:S(2)}) collective-permute-start(f32[192,128]{1,0:T(8,128)S(1)} %shard_map.64.a_ref), channel_id=1, source_target_pairs={{0,2},{1,3},{2,0},{3,1},{4,6},{5,7},{6,4},{7,5},{8,10},{9,11},{10,... | collective-permute-start | bytes 294920 | tf_op jit(solution)/shard_map/ppermute | solution.py:19
  82.7 3.5 %collective-permute-done.18.b_ref = f32[192,128]{1,0:T(8,128)S(1)} collective-permute-done((f32[192,128]{1,0:T(8,128)S(1)}, f32[192,128]{1,0:T(8,128)S(1)}, u32[]{:S(2)}, u32[]{:S(2)}) %collective-permute-start.18) | collective-permute-done | bytes 98336 | tf_op jit(solution)/shard_map/ppermute | solution.py:19
  86.2 1.1 collective-permute-start.19
  87.3 1.1 collective-permute-start.24
  88.4 1.8 %collective-permute-done.15.b_ref = f32[384,128]{1,0:T(8,128)S(1)} collective-permute-done((f32[384,128]{1,0:T(8,128)S(1)}, f32[384,128]{1,0:T(8,128)S(1)}, u32[]{:S(2)}, u32[]{:S(2)}) %collective-permute-start.15) | collective-permute-done | bytes 196640 | tf_op jit(solution)/shard_map/ppermute | solution.py:19
  90.2 2.1 %collective-permute-done.19.b_ref = f32[192,128]{1,0:T(8,128)S(1)} collective-permute-done((f32[192,128]{1,0:T(8,128)S(1)}, f32[192,128]{1,0:T(8,128)S(1)}, u32[]{:S(2)}, u32[]{:S(2)}) %collective-permute-start.19) | collective-permute-done | bytes 98336 | tf_op jit(solution)/shard_map/ppermute | solution.py:19
  92.3 1.1 collective-permute-start.20
  93.4 0.9 collective-permute-done.24.b_ref
  94.3 1.1 collective-permute-start.25
  95.4 6.6 %collective-permute-done.20.b_ref = f32[192,128]{1,0:T(8,128)S(1)} collective-permute-done((f32[192,128]{1,0:T(8,128)S(1)}, f32[192,128]{1,0:T(8,128)S(1)}, u32[]{:S(2)}, u32[]{:S(2)}) %collective-permute-start.20) | collective-permute-done | bytes 98336 | tf_op jit(solution)/shard_map/ppermute | solution.py:19
  102.1 1.1 collective-permute-done.25.b_ref
  103.2 0.1 collective-permute-start.26
  103.3 0.1 collective-permute-done.21.raw_rest_ref
  103.4 13.1 %shard_map.63 = (f32[1024,256]{1,0:T(8,128)}, f32[256,256]{1,0:T(8,128)S(1)}) custom-call(f32[384,128]{1,0:T(8,128)S(1)} %shard_map.58.first_ref, f32[384,128]{1,0:T(8,128)S(1)} %collective-permute-done.16.first_rest_ref, f32[192,128]{1,0:T(8,128)S(1)} %shard_map.62.raw_ref, f32[192,128]{1,0:T(8,128)S(1)} %collective-permute-done.21.raw_rest_ref, ...), custom_call_target="tpu_custom_call" | custom-call | flops 4000000000 | bytes 1048576 | tf_op jit(solution)/shard_map/pallas_call | solution.py:42
  116.5 1.9 %shard_map.68 = f32[2,256,256]{2,1,0:T(8,128)} custom-call(f32[384,128]{1,0:T(8,128)S(1)} %shard_map.58.first_ref, f32[384,128]{1,0:T(8,128)S(1)} %collective-permute-done.16.first_rest_ref, f32[192,128]{1,0:T(8,128)S(1)} %shard_map.67.proj_ref, f32[192,128]{1,0:T(8,128)S(1)} %collective-permute-done.26.proj_rest_ref, ...), custom_call_target="tpu_custom_call" | custom-call | bytes 1048576 | tf_op jit(solution)/shard_map/pallas_call | solution.py:42
  (31 shorter events, 0.4 us)
Async XLA Ops:
  0.6 1.2 %copy-start.1 = (f32[1024,256]{1,0:T(8,128)S(1)}, f32[1024,256]{1,0:T(8,128)}, u32[]{:S(2)}) copy-start(f32[1024,256]{1,0:T(8,128)} %basis_ref.1) | copy-start | bytes 3145732
  1.9 0.7 copy-start.2
  2.6 25.4 %collective-permute-start.1 = (bf16[1024,256]{1,0:T(8,128)(2,1)S(1)}, bf16[1024,256]{1,0:T(8,128)(2,1)S(1)}, u32[]{:S(2)}, u32[]{:S(2)}) collective-permute-start(bf16[1024,256]{1,0:T(8,128)(2,1)S(1)} %get-tuple-element.24.rounded_ref), channel_id=1, source_target_pairs={{0,2},{1,3},{2,4},{3,5},{4,6},{5,7},{6,8},{7,9},{8,10},{9,11},{10,... | collective-permute-start | bytes 1572872 | tf_op jit(solution)/shard_map/ppermute | solution.py:19
  5.6 24.6 %collective-permute-start.2 = (bf16[1024,256]{1,0:T(8,128)(2,1)S(1)}, bf16[1024,256]{1,0:T(8,128)(2,1)S(1)}, u32[]{:S(2)}, u32[]{:S(2)}) collective-permute-start(bf16[1024,256]{1,0:T(8,128)(2,1)S(1)} %get-tuple-element.24.rounded_ref), channel_id=1, source_target_pairs={{0,14},{1,15},{2,0},{3,1},{4,2},{5,3},{6,4},{7,5},{8,6},{9,7},{10,... | collective-permute-start | bytes 1572872 | tf_op jit(solution)/shard_map/ppermute | solution.py:19
  8.7 4.0 %copy-start = (bf16[8,40,128,128]{3,2,1,0:T(8,128)(2,1)S(1)}, bf16[8,40,128,128]{3,2,1,0:T(8,128)(2,1)}, u32[]{:S(2)}) copy-start(bf16[8,40,128,128]{3,2,1,0:T(8,128)(2,1)} %tiles_ref.1) | copy-start | bytes 31457284
  13.5 17.3 %collective-permute-start = (bf16[1024,256]{1,0:T(8,128)(2,1)S(1)}, bf16[1024,256]{1,0:T(8,128)(2,1)S(1)}, u32[]{:S(2)}, u32[]{:S(2)}) collective-permute-start(bf16[1024,256]{1,0:T(8,128)(2,1)S(1)} %get-tuple-element.24.rounded_ref), channel_id=1, source_target_pairs={{0,1},{1,0},{2,3},{3,2},{4,5},{5,4},{6,7},{7,6},{8,9},{9,8},{10,11... | collective-permute-start | bytes 1572872 | tf_op jit(solution)/shard_map/ppermute | solution.py:19
  13.6 18.3 %collective-permute-start.5 = (bf16[1024,256]{1,0:T(8,128)(2,1)S(1)}, bf16[1024,256]{1,0:T(8,128)(2,1)S(1)}, u32[]{:S(2)}, u32[]{:S(2)}) collective-permute-start(bf16[1024,256]{1,0:T(8,128)(2,1)S(1)} %get-tuple-element.24.rounded_ref), channel_id=1, source_target_pairs={{0,13},{1,4},{2,15},{3,6},{4,1},{5,8},{6,3},{7,10},{8,5},{9,12},{1... | collective-permute-start | bytes 1572872 | tf_op jit(solution)/shard_map/ppermute | solution.py:19
  30.3 1.9 %collective-permute-start.3 = (bf16[1024,256]{1,0:T(8,128)(2,1)S(1)}, bf16[1024,256]{1,0:T(8,128)(2,1)S(1)}, u32[]{:S(2)}, u32[]{:S(2)}) collective-permute-start(bf16[1024,256]{1,0:T(8,128)(2,1)S(1)} %collective-permute-done.1), channel_id=1, source_target_pairs={{0,1},{1,0},{2,3},{3,2},{4,5},{5,4},{6,7},{7,6},{8,9},{9,8},{10,11... | collective-permute-start | bytes 1572872 | tf_op jit(solution)/shard_map/ppermute | solution.py:19
  30.3 2.7 %collective-permute-start.4 = (bf16[1024,256]{1,0:T(8,128)(2,1)S(1)}, bf16[1024,256]{1,0:T(8,128)(2,1)S(1)}, u32[]{:S(2)}, u32[]{:S(2)}) collective-permute-start(bf16[1024,256]{1,0:T(8,128)(2,1)S(1)} %collective-permute-done.2), channel_id=1, source_target_pairs={{0,1},{1,0},{2,3},{3,2},{4,5},{5,4},{6,7},{7,6},{8,9},{9,8},{10,11... | collective-permute-start | bytes 1572872 | tf_op jit(solution)/shard_map/ppermute | solution.py:19
  36.9 30.2 %collective-permute-start.8 = (bf16[1024,256]{1,0:T(8,128)(2,1)S(1)}, bf16[1024,256]{1,0:T(8,128)(2,1)S(1)}, u32[]{:S(2)}, u32[]{:S(2)}) collective-permute-start(bf16[1024,256]{1,0:T(8,128)(2,1)S(1)} %get-tuple-element.31.rounded_ref), channel_id=1, source_target_pairs={{0,2},{1,3},{2,4},{3,5},{4,6},{5,7},{6,8},{7,9},{8,10},{9,11},{10,... | collective-permute-start | bytes 1572872 | tf_op jit(solution)/shard_map/ppermute | solution.py:19
  37.3 29.8 %collective-permute-start.9 = (bf16[1024,256]{1,0:T(8,128)(2,1)S(1)}, bf16[1024,256]{1,0:T(8,128)(2,1)S(1)}, u32[]{:S(2)}, u32[]{:S(2)}) collective-permute-start(bf16[1024,256]{1,0:T(8,128)(2,1)S(1)} %get-tuple-element.31.rounded_ref), channel_id=1, source_target_pairs={{0,14},{1,15},{2,0},{3,1},{4,2},{5,3},{6,4},{7,5},{8,6},{9,7},{10,... | collective-permute-start | bytes 1572872 | tf_op jit(solution)/shard_map/ppermute | solution.py:19
  44.5 1.5 %collective-permute-start.6 = (f32[384,128]{1,0:T(8,128)S(1)}, f32[384,128]{1,0:T(8,128)S(1)}, u32[]{:S(2)}, u32[]{:S(2)}) collective-permute-start(f32[384,128]{1,0:T(8,128)S(1)} %get-tuple-element.30), channel_id=1, source_target_pairs={{0,1},{1,0},{2,3},{3,2},{4,5},{5,4},{6,7},{7,6},{8,9},{9,8},{10,11... | collective-permute-start | bytes 589832 | tf_op jit(solution)/shard_map/ppermute | solution.py:19
  46.0 21.1 %collective-permute-start.10 = (f32[384,128]{1,0:T(8,128)S(1)}, f32[384,128]{1,0:T(8,128)S(1)}, u32[]{:S(2)}, u32[]{:S(2)}) collective-permute-start(f32[384,128]{1,0:T(8,128)S(1)} %shard_map.54.a_ref), channel_id=1, source_target_pairs={{0,2},{1,3},{2,0},{3,1},{4,6},{5,7},{6,4},{7,5},{8,10},{9,11},{10,... | collective-permute-start | bytes 589832 | tf_op jit(solution)/shard_map/ppermute | solution.py:19
  46.1 23.1 %collective-permute-start.13 = (bf16[1024,256]{1,0:T(8,128)(2,1)S(1)}, bf16[1024,256]{1,0:T(8,128)(2,1)S(1)}, u32[]{:S(2)}, u32[]{:S(2)}) collective-permute-start(bf16[1024,256]{1,0:T(8,128)(2,1)S(1)} %get-tuple-element.31.rounded_ref), channel_id=1, source_target_pairs={{0,13},{1,4},{2,15},{3,6},{4,1},{5,8},{6,3},{7,10},{8,5},{9,12},{1... | collective-permute-start | bytes 1572872 | tf_op jit(solution)/shard_map/ppermute | solution.py:19
  47.4 21.8 %collective-permute-start.7 = (bf16[1024,256]{1,0:T(8,128)(2,1)S(1)}, bf16[1024,256]{1,0:T(8,128)(2,1)S(1)}, u32[]{:S(2)}, u32[]{:S(2)}) collective-permute-start(bf16[1024,256]{1,0:T(8,128)(2,1)S(1)} %get-tuple-element.31.rounded_ref), channel_id=1, source_target_pairs={{0,1},{1,0},{2,3},{3,2},{4,5},{5,4},{6,7},{7,6},{8,9},{9,8},{10,11... | collective-permute-start | bytes 1572872 | tf_op jit(solution)/shard_map/ppermute | solution.py:19
  67.1 2.0 %collective-permute-start.11 = (bf16[1024,256]{1,0:T(8,128)(2,1)S(1)}, bf16[1024,256]{1,0:T(8,128)(2,1)S(1)}, u32[]{:S(2)}, u32[]{:S(2)}) collective-permute-start(bf16[1024,256]{1,0:T(8,128)(2,1)S(1)} %collective-permute-done.8), channel_id=1, source_target_pairs={{0,1},{1,0},{2,3},{3,2},{4,5},{5,4},{6,7},{7,6},{8,9},{9,8},{10,11... | collective-permute-start | bytes 1572872 | tf_op jit(solution)/shard_map/ppermute | solution.py:19
  67.2 2.6 %collective-permute-start.12 = (bf16[1024,256]{1,0:T(8,128)(2,1)S(1)}, bf16[1024,256]{1,0:T(8,128)(2,1)S(1)}, u32[]{:S(2)}, u32[]{:S(2)}) collective-permute-start(bf16[1024,256]{1,0:T(8,128)(2,1)S(1)} %collective-permute-done.9), channel_id=1, source_target_pairs={{0,1},{1,0},{2,3},{3,2},{4,5},{5,4},{6,7},{7,6},{8,9},{9,8},{10,11... | collective-permute-start | bytes 1572872 | tf_op jit(solution)/shard_map/ppermute | solution.py:19
  67.7 7.0 %collective-permute-start.14 = (f32[384,128]{1,0:T(8,128)S(1)}, f32[384,128]{1,0:T(8,128)S(1)}, u32[]{:S(2)}, u32[]{:S(2)}) collective-permute-start(f32[384,128]{1,0:T(8,128)S(1)} %shard_map.55.a_ref), channel_id=1, source_target_pairs={{0,4},{1,5},{2,6},{3,7},{4,0},{5,1},{6,2},{7,3},{8,12},{9,13},{10,... | collective-permute-start | bytes 589832 | tf_op jit(solution)/shard_map/ppermute | solution.py:19
  77.4 3.0 %collective-permute-start.17 = (f32[192,128]{1,0:T(8,128)S(1)}, f32[192,128]{1,0:T(8,128)S(1)}, u32[]{:S(2)}, u32[]{:S(2)}) collective-permute-start(f32[192,128]{1,0:T(8,128)S(1)} %get-tuple-element.37), channel_id=1, source_target_pairs={{0,1},{1,0},{2,3},{3,2},{4,5},{5,4},{6,7},{7,6},{8,9},{9,8},{10,11... | collective-permute-start | bytes 294920 | tf_op jit(solution)/shard_map/ppermute | solution.py:19
  77.6 2.9 %collective-permute-start.22 = (f32[192,128]{1,0:T(8,128)S(1)}, f32[192,128]{1,0:T(8,128)S(1)}, u32[]{:S(2)}, u32[]{:S(2)}) collective-permute-start(f32[192,128]{1,0:T(8,128)S(1)} %get-tuple-element.40), channel_id=1, source_target_pairs={{0,1},{1,0},{2,3},{3,2},{4,5},{5,4},{6,7},{7,6},{8,9},{9,8},{10,11... | collective-permute-start | bytes 294920 | tf_op jit(solution)/shard_map/ppermute | solution.py:19
  78.0 12.2 %collective-permute-start.15 = (f32[384,128]{1,0:T(8,128)S(1)}, f32[384,128]{1,0:T(8,128)S(1)}, u32[]{:S(2)}, u32[]{:S(2)}) collective-permute-start(f32[384,128]{1,0:T(8,128)S(1)} %get-tuple-element.35.a_ref), channel_id=1, source_target_pairs={{0,8},{1,9},{2,10},{3,11},{4,12},{5,13},{6,14},{7,15},{8,0},{9,1},... | collective-permute-start | bytes 589832 | tf_op jit(solution)/shard_map/ppermute | solution.py:19
  80.5 5.7 %collective-permute-start.18 = (f32[192,128]{1,0:T(8,128)S(1)}, f32[192,128]{1,0:T(8,128)S(1)}, u32[]{:S(2)}, u32[]{:S(2)}) collective-permute-start(f32[192,128]{1,0:T(8,128)S(1)} %shard_map.59.a_ref), channel_id=1, source_target_pairs={{0,2},{1,3},{2,0},{3,1},{4,6},{5,7},{6,4},{7,5},{8,10},{9,11},{10,... | collective-permute-start | bytes 294920 | tf_op jit(solution)/shard_map/ppermute | solution.py:19
  80.6 6.7 %collective-permute-start.23 = (f32[192,128]{1,0:T(8,128)S(1)}, f32[192,128]{1,0:T(8,128)S(1)}, u32[]{:S(2)}, u32[]{:S(2)}) collective-permute-start(f32[192,128]{1,0:T(8,128)S(1)} %shard_map.64.a_ref), channel_id=1, source_target_pairs={{0,2},{1,3},{2,0},{3,1},{4,6},{5,7},{6,4},{7,5},{8,10},{9,11},{10,... | collective-permute-start | bytes 294920 | tf_op jit(solution)/shard_map/ppermute | solution.py:19
  86.2 6.1 %collective-permute-start.19 = (f32[192,128]{1,0:T(8,128)S(1)}, f32[192,128]{1,0:T(8,128)S(1)}, u32[]{:S(2)}, u32[]{:S(2)}) collective-permute-start(f32[192,128]{1,0:T(8,128)S(1)} %shard_map.60.a_ref), channel_id=1, source_target_pairs={{0,4},{1,5},{2,6},{3,7},{4,0},{5,1},{6,2},{7,3},{8,12},{9,13},{10,... | collective-permute-start | bytes 294920 | tf_op jit(solution)/shard_map/ppermute | solution.py:19
  87.3 7.0 %collective-permute-start.24 = (f32[192,128]{1,0:T(8,128)S(1)}, f32[192,128]{1,0:T(8,128)S(1)}, u32[]{:S(2)}, u32[]{:S(2)}) collective-permute-start(f32[192,128]{1,0:T(8,128)S(1)} %shard_map.65.a_ref), channel_id=1, source_target_pairs={{0,4},{1,5},{2,6},{3,7},{4,0},{5,1},{6,2},{7,3},{8,12},{9,13},{10,... | collective-permute-start | bytes 294920 | tf_op jit(solution)/shard_map/ppermute | solution.py:19
  92.3 9.7 %collective-permute-start.20 = (f32[192,128]{1,0:T(8,128)S(1)}, f32[192,128]{1,0:T(8,128)S(1)}, u32[]{:S(2)}, u32[]{:S(2)}) collective-permute-start(f32[192,128]{1,0:T(8,128)S(1)} %shard_map.61.a_ref), channel_id=1, source_target_pairs={{0,8},{1,9},{2,10},{3,11},{4,12},{5,13},{6,14},{7,15},{8,0},{9,1},... | collective-permute-start | bytes 294920 | tf_op jit(solution)/shard_map/ppermute | solution.py:19
  93.4 9.8 %collective-permute-start.16 = (f32[384,128]{1,0:T(8,128)S(1)}, f32[384,128]{1,0:T(8,128)S(1)}, u32[]{:S(2)}, u32[]{:S(2)}) collective-permute-start(f32[384,128]{1,0:T(8,128)S(1)} %shard_map.58.first_ref), channel_id=1, source_target_pairs={{0,1},{1,0},{2,3},{3,2},{4,5},{5,4},{6,7},{7,6},{8,9},{9,8},{10,11... | collective-permute-start | bytes 589832 | tf_op jit(solution)/shard_map/ppermute | solution.py:19
  94.3 8.9 %collective-permute-start.25 = (f32[192,128]{1,0:T(8,128)S(1)}, f32[192,128]{1,0:T(8,128)S(1)}, u32[]{:S(2)}, u32[]{:S(2)}) collective-permute-start(f32[192,128]{1,0:T(8,128)S(1)} %shard_map.66.a_ref), channel_id=1, source_target_pairs={{0,8},{1,9},{2,10},{3,11},{4,12},{5,13},{6,14},{7,15},{8,0},{9,1},... | collective-permute-start | bytes 294920 | tf_op jit(solution)/shard_map/ppermute | solution.py:19
  102.0 1.4 %collective-permute-start.21 = (f32[192,128]{1,0:T(8,128)S(1)}, f32[192,128]{1,0:T(8,128)S(1)}, u32[]{:S(2)}, u32[]{:S(2)}) collective-permute-start(f32[192,128]{1,0:T(8,128)S(1)} %shard_map.62.raw_ref), channel_id=1, source_target_pairs={{0,1},{1,0},{2,3},{3,2},{4,5},{5,4},{6,7},{7,6},{8,9},{9,8},{10,11... | collective-permute-start | bytes 294920 | tf_op jit(solution)/shard_map/ppermute | solution.py:19
  103.2 13.3 %collective-permute-start.26 = (f32[192,128]{1,0:T(8,128)S(1)}, f32[192,128]{1,0:T(8,128)S(1)}, u32[]{:S(2)}, u32[]{:S(2)}) collective-permute-start(f32[192,128]{1,0:T(8,128)S(1)} %shard_map.67.proj_ref), channel_id=1, source_target_pairs={{0,1},{1,0},{2,3},{3,2},{4,5},{5,4},{6,7},{7,6},{8,9},{9,8},{10,11... | collective-permute-start | bytes 294920 | tf_op jit(solution)/shard_map/ppermute | solution.py:19

commit v3 on v2

v3 whole, which is shorter than its diff:
```python
import functools
import math

import jax
import jax.numpy as jnp
from jax import lax
from jax.experimental import pallas as pl
from jax.experimental.pallas import tpu as pltpu
from jax.sharding import PartitionSpec as P

B = 8
LANES = 128
CHUNK = 8
MIB = 2**20
LONG = 8_000_000_000


def permuted(value, target):
    peers = lax.axis_size("rows")
    return lax.ppermute(value, "rows", [(i, target(i) % peers) for i in range(peers)])


def swapped(value):
    return permuted(value, lambda i: i ^ 1)


def after(value, *others):
    return lax.optimization_barrier((value, others))[0]


def neighbourhood(blocks, meanwhile, then=lambda made: made):
    before = permuted(blocks, lambda i: i + 2)
    behind = permuted(blocks, lambda i: i - 2)
    far = permuted(blocks, lambda i: i + 3 if i % 2 else i - 3)
    made = meanwhile()
    other = swapped(after(blocks, made))
    made = then(made)
    before, behind = after(before, made), after(behind, made)
    return [blocks, other, before, swapped(before), behind, swapped(behind), far], made


def kernel_call(kernel, out_shape, *args, flops=0, limit=16, **kwargs):
    return pl.pallas_call(
        kernel,
        out_shape=out_shape,
        cost_estimate=pl.CostEstimate(flops=flops, bytes_accessed=2**20, transcendentals=0),
        compiler_params=pltpu.CompilerParams(vmem_limit_bytes=limit * MIB),
        **kwargs,
    )(*args)


def prepare_kernel(pattern_ref, basis_ref, place_ref, rounded_ref, held, sems, *, block_rows, peers):
    parts = sems.shape[0]
    step = basis_ref.shape[0] // parts
    at = [slice(i * step, (i + 1) * step) for i in range(parts)]
    copies = [pltpu.make_async_copy(basis_ref.at[at[i]], held.at[at[i]], sems.at[i]) for i in range(parts)]
    for c in copies:
        c.start()
    for i in range(parts):
        copies[i].wait()
        rounded_ref[at[i], :] = held[at[i], :].astype(jnp.bfloat16)
    me = lax.axis_index("rows")
    pattern = pattern_ref[...]
    owner = lax.div(pattern, block_rows)
    apart = lax.rem(lax.div(owner, 2) - lax.div(me, 2) + (2 + peers // 2), peers // 2) - 2
    crossed = lax.rem(owner + me, 2)
    piece = jnp.where(apart == 0, crossed, jnp.where(apart == -1, 2 + crossed, jnp.where(apart == 1, 4 + crossed, 6)))
    place_ref[...] = piece * block_rows + lax.rem(pattern, block_rows)


def held_kernel(tiles_ref, held_ref, turn_ref, sems):
    copies = [pltpu.make_async_copy(tiles_ref.at[r], held_ref.at[r], sems.at[r]) for r in range(tiles_ref.shape[0])]
    for c in copies:
        c.start()
    n = turn_ref.shape[0]
    both = lax.broadcasted_iota(jnp.int32, (n, n), 0) & lax.broadcasted_iota(jnp.int32, (n, n), 1)
    shift = 1
    while 2**shift < n:
        both = both ^ (both >> shift)
        shift *= 2
    turn_ref[...] = jnp.where(both & 1 == 0, 1.0, -1.0).astype(turn_ref.dtype) * (1.0 / math.sqrt(n))
    for c in copies:
        c.wait()


def held(tiles, modes):
    return pl.pallas_call(
        held_kernel,
        in_specs=[pl.BlockSpec(memory_space=pltpu.HBM)],
        out_specs=[pl.BlockSpec(memory_space=pltpu.VMEM)] * 2,
        scratch_shapes=[pltpu.SemaphoreType.DMA((tiles.shape[0],))],
        out_shape=[
            jax.ShapeDtypeStruct(tiles.shape, tiles.dtype),
            jax.ShapeDtypeStruct((modes, modes), jnp.bfloat16),
        ],
        cost_estimate=pl.CostEstimate(flops=0, bytes_accessed=4 * tiles.size, transcendentals=0),
        compiler_params=pltpu.CompilerParams(vmem_limit_bytes=14 * MIB),
    )(tiles)


def turned(x, turn, parts):
    total = None
    for _ in range(parts):
        part = x.astype(jnp.bfloat16)
        term = jnp.dot(part, turn, preferred_element_type=jnp.float32)
        total = term if total is None else total + term
        x = x - part.astype(jnp.float32)
    return total


def product_kernel(place_ref, tiles_ref, turn_ref, *refs, pieces):
    piece_refs, (product_ref, *sent_refs, window) = refs[:pieces], refs[pieces:]
    block_rows, tile = piece_refs[0].shape[:2]
    for i in range(pieces):
        window[i * block_rows : (i + 1) * block_rows] = piece_refs[i][...]
    for r in range(block_rows):
        total = None
        for k in range(0, tiles_ref.shape[1], 2):
            left = jnp.concatenate([tiles_ref[r, k], tiles_ref[r, k + 1]], axis=1)
            right = jnp.concatenate([window[place_ref[r, k]], window[place_ref[r, k + 1]]], axis=0)
            term = jnp.dot(left, right, preferred_element_type=jnp.float32)
            total = term if total is None else total + term
        product_ref[r * tile : (r + 1) * tile, :] = total
    if sent_refs:
        sent_refs[0][...] = turned(product_ref[...], turn_ref[...], 2).astype(sent_refs[0].dtype)
    else:
        product_ref[...] = turned(product_ref[...], turn_ref[...], 3)


def product_of(place, tiles, turn, pieces, *types):
    block_rows, slots, tile, _ = tiles.shape
    modes = pieces[0].shape[-1]
    n = len(pieces)
    rows = block_rows * tile
    return pl.pallas_call(
        functools.partial(product_kernel, pieces=n),
        in_specs=[pl.BlockSpec(memory_space=pltpu.SMEM)] + [pl.BlockSpec(memory_space=pltpu.VMEM)] * (n + 2),
        scratch_shapes=[pltpu.VMEM((n * block_rows, tile, modes), jnp.bfloat16)],
        out_shape=[jax.ShapeDtypeStruct((rows, modes), t) for t in types],
        cost_estimate=pl.CostEstimate(flops=LONG, bytes_accessed=2 * tiles.size, transcendentals=0),
        compiler_params=pltpu.CompilerParams(vmem_limit_bytes=12 * MIB),
    )(place, tiles, turn, *[p.reshape(block_rows, tile, modes) for p in pieces])


def dot(a, b, dims=((1,), (0,))):
    return lax.dot_general(a, b, (dims, ((), ())), precision=lax.Precision.HIGHEST, preferred_element_type=jnp.float32)


def my_bit(bit):
    return lax.rem(lax.div(lax.axis_index("rows"), bit), 2)


def halves(left, right):
    down = ((0,), (0,))
    h = right.shape[1] // 2
    la, lb, ra, rb = left[:, :h], left[:, h:], right[:, :h], right[:, h:]
    low, mid, high = dot(la, ra, down), dot(lb, ra, down), dot(lb, rb, down)
    first = jnp.concatenate([low, mid[: h // 2]], axis=0)
    last = jnp.concatenate([mid[h // 2 :], high], axis=0)
    core = my_bit(1)
    return jnp.where(core == 0, first, last), jnp.where(core == 0, last, first)


def first_sums_kernel(product_ref, rounded_ref, mine_ref, rest_ref):
    n = mine_ref.shape[0] // 2
    product = product_ref[...]
    mine_ref[:n, :], rest_ref[:n, :] = halves(product, product)
    mine_ref[n:, :], rest_ref[n:, :] = halves(rounded_ref[...].astype(jnp.float32), product)


def gram_kernel(product_ref, a_ref, b_ref, mine_ref, rest_ref, added_ref):
    product = product_ref[...]
    mine_ref[...], rest_ref[...] = halves(product, product)
    added_ref[...] = a_ref[...] + b_ref[...]


def proj_kernel(product_ref, sent_ref, turn_ref, mine_ref, rest_ref):
    rounded = jnp.dot(sent_ref[...], turn_ref[...], preferred_element_type=jnp.float32)
    mine_ref[...], rest_ref[...] = halves(rounded, product_ref[...])


def split_kernel(a_ref, b_ref, mine_ref, rest_ref):
    total = a_ref[...] + b_ref[...]
    n = total.shape[0] // 2
    bit = my_bit(2)
    mine_ref[...] = jnp.where(bit == 0, total[:n], total[n:])
    rest_ref[...] = jnp.where(bit == 0, total[n:], total[:n])


def added_kernel(a_ref, b_ref, out_ref):
    out_ref[...] = a_ref[...] + b_ref[...]


def added(a, b):
    return kernel_call(added_kernel, jax.ShapeDtypeStruct(a.shape, a.dtype), a, b, limit=4)


def summed(mine, rest, first=1, last=None):
    step = first
    while step < (last or lax.axis_size("rows")):
        mine = added(mine, permuted(rest if step == 1 else mine, lambda i: i ^ step))
        step *= 2
    return mine


def unpacked(mine, rest):
    core = my_bit(1)
    first, last = jnp.where(core == 0, mine, rest), jnp.where(core == 0, rest, mine)
    h = 2 * mine.shape[0] // 3
    a, d = first[:h], last[h // 2 :]
    b = jnp.concatenate([first[h:], last[: h // 2]], axis=0)
    return jnp.concatenate([jnp.concatenate([a, b.T], axis=1), jnp.concatenate([b, d], axis=1)], axis=0)


def lane_bcast(x, j):
    return jnp.take_along_axis(x, jnp.broadcast_to(j, x.shape).astype(jnp.int32), axis=1)


def sub_bcast(x, i):
    return jnp.broadcast_to(x[i : i + 1, :], x.shape)


def wide(x, n):
    return x if n == 1 else jnp.concatenate([x] * n, axis=1)


def rsqrt(x):
    y = lax.rsqrt(x)
    return y * (1.5 - 0.5 * x * y * y)


def tree(terms):
    while len(terms) > 1:
        terms = [a + b for a, b in zip(terms[::2], terms[1::2])]
    return terms[0]


def pivot_rows(xk, k, tile, at, lane, sub, tiles):
    here = lane // B == k
    cols = [lane_bcast(xk[:, tile], at + j) for j in range(B)]
    start = jnp.where(here, jnp.where(lane - B * k == sub, 1.0, 0.0), xk)
    x = start
    one = sub[:, :LANES]
    for a in range(0, B, 2):
        b = a + 1
        pa = [sub_bcast(cols[j], a) for j in range(B)]
        pb = [sub_bcast(cols[j], b) for j in range(B)]
        inv = 1.0 / (pa[a] * pb[b] - pa[b] * pa[b])
        i00, i01, i11 = pb[b] * inv, -pa[b] * inv, pa[a] * inv
        mine = (one == a) | (one == b)
        ra, rb = sub_bcast(x, a), sub_bcast(x, b)
        qa = wide(i00, tiles) * ra + wide(i01, tiles) * rb
        qb = wide(i01, tiles) * ra + wide(i11, tiles) * rb
        ca = jnp.where(mine, jnp.where(one == a, -1.0, 0.0), cols[a])
        cb = jnp.where(mine, jnp.where(one == b, -1.0, 0.0), cols[b])
        wm = wide(mine, tiles)
        x = jnp.where(wm, 0.0, x) - (wide(ca, tiles) * qa + wide(cb, tiles) * qb)
        for j in range(b + 1, B):
            ta, tb = i00 * pa[j] + i01 * pb[j], i01 * pa[j] + i11 * pb[j]
            cols[j] = jnp.where(mine, 0.0, cols[j]) - (ca * ta + cb * tb)
    return [sub_bcast(x, i) for i in range(B)]


def pivot_factors(d, sub, lane):
    base = lane // B * B
    cols = [jnp.take_along_axis(d, base + j, axis=1) for j in range(B)]
    p = [[sub_bcast(cols[j], i) for j in range(B)] for i in range(B)]
    m = [[None] * B for _ in range(B)]
    out = jnp.zeros(d.shape, jnp.float32)
    for a in range(B):
        inv = 1.0 / p[a][a]
        for i in range(a + 1, B):
            l = p[i][a] * inv
            for j in range(a + 1, i + 1):
                p[i][j] = p[i][j] - l * p[j][a]
            for j in range(a):
                m[i][j] = m[i][j] - l * m[a][j]
            m[i][a] = -l
    for i in range(B):
        r = rsqrt(p[i][i])
        for j in range(i + 1):
            out = jnp.where((sub == i) & (lane % B == j), r if i == j else r * m[i][j], out)
    return out


def eliminated_block(x, first, groups, lane, sub, tiles):
    acting = []
    for s in range(groups):
        k = first + s
        t = k * B // LANES
        tile, at = slice(t * LANES, (t + 1) * LANES), k * B - t * LANES
        here = lane // B == k
        rows = pivot_rows(x[s], k, tile, at, lane, sub, tiles)
        for i in range(s + 1, groups):
            c = [wide(lane_bcast(x[i][:, tile], at + j), tiles) for j in range(B)]
            x[i] = jnp.where(here, 0.0, x[i]) - tree([c[j] * rows[j] for j in range(B)])
        own = rows[0]
        for j in range(1, B):
            own = jnp.where(sub == j, rows[j], own)
        acting.append(jnp.where((lane // B > k) & (lane // B < first + groups), 0.0, own))
    return x, acting


def scaled(g):
    row = lax.broadcasted_iota(jnp.int32, g.shape, 0)
    d = jnp.where(row == lax.broadcasted_iota(jnp.int32, g.shape, 1), g, 0.0)
    scale = rsqrt(jnp.sum(d, axis=0, keepdims=True))
    return g * rsqrt(jnp.sum(d, axis=1, keepdims=True)) * scale, scale


def eliminated(rest, first, last):
    n = rest[0].shape[1]
    tiles, many, per = n // LANES, range(len(rest)), CHUNK
    lane = lax.broadcasted_iota(jnp.int32, (B, n), 1)
    sub = lax.broadcasted_iota(jnp.int32, (B, n), 0)
    rest, done = list(rest), [[] for _ in many]
    for start in range(first, last, per):
        size, lo = per * B, start * B
        both = [
            eliminated_block([rest[m][i * B : i * B + B, :] for i in range(per)], start, per, lane, sub, tiles)
            for m in many
        ]
        for m in many:
            x, acting = both[m]
            done[m] += x
            if lo + size < n:
                left = jnp.concatenate(x, axis=0)
                below = (lo + size) // LANES * LANES
                update = dot(left[:, below:], jnp.concatenate(acting, axis=0), ((0,), (0,)))[lo + size - below :]
                lanes = lax.broadcasted_iota(jnp.int32, update.shape, 1)
                rest[m] = jnp.where(lanes // size == lo // size, 0.0, rest[m][size:]) - update
    return [jnp.concatenate(d, axis=0) for d in done], rest


def inverse_factor(done, scale):
    n = done.shape[0]
    lane = lax.broadcasted_iota(jnp.int32, (B, n), 1)
    sub = lax.broadcasted_iota(jnp.int32, (B, n), 0)
    groups = [done[k * B : k * B + B, :] for k in range(n // B)]
    strip = groups[0]
    for k in range(1, n // B):
        strip = jnp.where(lane // B == k, groups[k], strip)
    factors = [
        pivot_factors(strip[:, t : t + LANES], sub[:, :LANES], lane[:, :LANES]) for t in range(0, n, LANES)
    ]
    spread = jnp.concatenate(factors, axis=1)
    blocks, unit = [], []
    for k in range(n // B):
        here = lane // B == k
        blocks.append(jnp.where(here, spread, 0.0))
        eye = jnp.where(here & (lane - B * k == sub), 1.0, 0.0)
        unit.append(jnp.where(lane < B * k, groups[k], eye))
    return dot(jnp.concatenate(blocks, axis=0), jnp.concatenate(unit, axis=0)) * scale


def upper_kernel(
    keep_ref, other_ref, keep_rest_ref, other_rest_ref, raw_ref, raw_rest_ref, done_ref, rest_ref, scale_ref
):
    bit = my_bit(2)
    mine = jnp.where(bit == 0, keep_ref[...], other_ref[...])
    rest = jnp.where(bit == 0, keep_rest_ref[...], other_rest_ref[...])
    one, scale_ref[0:1, :] = scaled(unpacked(mine, rest))
    two, scale_ref[1:2, :] = scaled(unpacked(raw_ref[...], raw_rest_ref[...]))
    done, rest = eliminated([one, two], 0, CHUNK)
    for m in range(2):
        done_ref[m] = done[m]
        rest_ref[m] = rest[m]


def lower_kernel(done_ref, rest_ref, scale_ref, inverse_ref, both_ref):
    done, _ = eliminated([rest_ref[0], rest_ref[1]], CHUNK, rest_ref.shape[2] // B)
    for m, ref in ((0, inverse_ref), (1, both_ref)):
        ref[...] = inverse_factor(jnp.concatenate([done_ref[m], done[m]], axis=0), scale_ref[m : m + 1, :])


def modes_kernel(product_ref, inverse_ref, modes_ref, *, scale):
    inverse = inverse_ref[...] * scale
    h = inverse.shape[0] // 2
    along = ((1,), (1,))
    modes_ref[:, :h] = dot(product_ref[:, :h], inverse[:h, :h], along)
    modes_ref[:, h:] = dot(product_ref[...], inverse[h:, :], along)


def projected_kernel(
    keep_ref, other_ref, keep_rest_ref, other_rest_ref, proj_ref, proj_rest_ref, inverse_ref, projected_ref
):
    bit = my_bit(2)
    mine = jnp.where(bit == 0, other_ref[...], keep_ref[...])
    rest = jnp.where(bit == 0, other_rest_ref[...], keep_rest_ref[...])
    projected_ref[0] = unpacked(mine, rest)
    inverse = inverse_ref[...]
    proj = dot(inverse, unpacked(proj_ref[...], proj_rest_ref[...]))
    projected_ref[1] = dot(proj, inverse, ((1,), (1,)))


def per_device(tiles, pattern, basis):
    block_rows, _, tile, _ = tiles.shape
    rows, modes = basis.shape
    peers = lax.axis_size("rows")
    f32 = lambda *shape: jax.ShapeDtypeStruct(shape, jnp.float32)
    half_sum = f32(3 * modes // 4, modes // 2)
    flops = 6 * rows * modes * modes
    place, rounded = kernel_call(
        functools.partial(prepare_kernel, block_rows=block_rows, peers=peers),
        (jax.ShapeDtypeStruct(pattern.shape, jnp.int32), jax.ShapeDtypeStruct((rows, modes), jnp.bfloat16)),
        pattern, basis,
        limit=8,
        in_specs=[pl.BlockSpec(memory_space=pltpu.VMEM), pl.BlockSpec(memory_space=pltpu.HBM)],
        scratch_shapes=[pltpu.VMEM(basis.shape, jnp.float32), pltpu.SemaphoreType.DMA((4,))],
    )
    pieces, (tiles, turn) = neighbourhood(rounded, lambda: held(tiles, modes))
    product, sent = product_of(place, tiles, turn, pieces, jnp.float32, jnp.bfloat16)

    def first_sums():
        mine, rest = kernel_call(
            first_sums_kernel, (f32(3 * modes // 2, modes // 2),) * 2, product, rounded, flops=LONG
        )
        return kernel_call(split_kernel, (half_sum,) * 2, mine, swapped(rest), limit=4)

    pieces, first = neighbourhood(sent, first_sums, lambda made: added(made[0], permuted(made[1], lambda i: i ^ 2)))
    partner = permuted(first, lambda i: i ^ 4)

    (raw,) = product_of(place, tiles, turn, pieces, jnp.float32)
    gram, rest, first = kernel_call(gram_kernel, (half_sum,) * 3, raw, first, partner, flops=LONG)
    gram = summed(gram, rest, 1, 2)
    first = after(first, gram)
    proj, rest = kernel_call(proj_kernel, (half_sum,) * 2, after(raw, gram), sent, turn, flops=LONG)
    gram = summed(gram, None, 2, 8)
    partner = permuted(first, lambda i: i ^ 8)
    first = added(*after((first, partner), gram))
    first, gram = summed(first, None, 16), summed(gram, None, 8)
    other = permuted(first, lambda i: i ^ 2)
    first = (first, other, swapped(first), swapped(other))
    proj = summed(proj, rest, 1, peers // 4)
    partner = permuted(proj, lambda i: i ^ (peers // 4))
    eliminating = kernel_call(
        upper_kernel,
        (f32(2, CHUNK * B, modes), f32(2, modes - CHUNK * B, modes), f32(2, modes)),
        *first, gram, swapped(gram),
        flops=LONG,
    )
    proj = added(*after((proj, partner), eliminating[0]))
    partner = permuted(proj, lambda i: i ^ (peers // 2))
    inverse, both = kernel_call(lower_kernel, (f32(modes, modes),) * 2, *eliminating, flops=3 * LONG)
    proj = added(*after((proj, partner), inverse))
    modes_out = kernel_call(
        functools.partial(modes_kernel, scale=math.sqrt(rows * peers)), f32(rows, modes), raw, both, flops=LONG
    )
    projected = kernel_call(projected_kernel, f32(2, modes, modes), *first, proj, swapped(proj), inverse)
    return modes_out, projected


def solution(mesh):
    placed = (
        P(("groups", "rows"), None, None, None),
        P(("groups", "rows"), None),
        P(("groups", "rows"), None),
    )
    return jax.shard_map(
        per_device,
        mesh=mesh,
        in_specs=placed,
        out_specs=(P(("groups", "rows"), None), P("groups", None, None)),
        check_vma=False,
    )
```

time: 119 us -> 111 us (0.933)
  waiting for transfers between devices: 54.7 us -> 46.1 us
  starting transfers between devices: 26.6 us -> 28.9 us
  Pallas kernels: 30.4 us -> 29.2 us
    ppermute x27 -> x29, waiting for transfers between devices: 54.7 us -> 46.1 us  [permuted(): lax.ppermute(value, 'rows', [(i, target(i) % peers) for i in range(peers)])]
    ppermute x27 -> x29, starting transfers between devices: 26.6 us -> 28.9 us  [permuted(): lax.ppermute(value, 'rows', [(i, target(i) % peers) for i in range(peers)])]
    pallas_call x16 -> x19, Pallas kernels: 20.8 us -> 20.1 us  [kernel_call(): pl.pallas_call(kernel, out_shape=out_shape, cost_estimate=pl.CostEstimate...]
  transfers between devices with their start and end apart: 27 -> 29, of which waited for: 15 -> 15; matrix products, arithmetic and copies ran while one was open for 0% -> 0% of each run, Pallas kernels for 18% -> 19%
where the time goes in v3:
time: 111 us
  waiting for transfers between devices  46.1 us (42%)
  Pallas kernels  29.2 us (26%)
  starting transfers between devices  28.9 us (26%)
  local copies, waits for them, and re-layouts  5.88 us (5%)
    ppermute x29, waiting for transfers between devices, permuted(): lax.ppermute(value, 'rows', [(i, target(i) % peers) for i in range(peers)])  46.1 us
    ppermute x29, starting transfers between devices, permuted(): lax.ppermute(value, 'rows', [(i, target(i) % peers) for i in range(peers)])  28.9 us
    pallas_call x19, Pallas kernels, kernel_call(): pl.pallas_call(kernel, out_shape=out_shape, cost_estimate=pl.CostEstimate...  20.1 us
    pallas_call x2, Pallas kernels, product_of(): pl.pallas_call(functools.partial(product_kernel, pieces=n), in_specs=[pl....  8.13 us
    unnamed x6, local copies, waits for them, and re-layouts  5.88 us
  transfers between devices with their start and end apart: 29, of which 15 were waited for; matrix products, arithmetic and copies ran while one was open for 0% of the time, Pallas kernels for 19%

profile of v3, /device:TPU:0, one launch (start us, length us, event | category | flops | bytes accessed | tf_op | source)
XLA Modules:
  0.0 110.9 jit_solution(12225063596149611873)
XLA Ops:
  0.6 1.2 %copy-done.1 = f32[1024,256]{1,0:T(8,128)S(1)} copy-done((f32[1024,256]{1,0:T(8,128)S(1)}, f32[1024,256]{1,0:T(8,128)}, u32[]{:S(2)}) %copy-start.1) | copy-done | bytes 1048600
  1.9 0.7 copy-done.2
  2.5 0.2 shard_map.50
  2.7 6.1 %collective-permute-start.3 = (bf16[1024,256]{1,0:T(8,128)(2,1)S(1)}, bf16[1024,256]{1,0:T(8,128)(2,1)S(1)}, u32[]{:S(2)}, u32[]{:S(2)}) collective-permute-start(bf16[1024,256]{1,0:T(8,128)(2,1)S(1)} %get-tuple-element.40.rounded_ref), channel_id=1, source_target_pairs={{0,14},{1,15},{2,0},{3,1},{4,2},{5,3},{6,4},{7,5},{8,6},{9,7},{10,... | collective-permute-start | bytes 1572872 | tf_op jit(solution)/shard_map/ppermute | solution.py:20
  8.8 4.0 %copy-done = bf16[8,40,128,128]{3,2,1,0:T(8,128)(2,1)S(1)} copy-done((bf16[8,40,128,128]{3,2,1,0:T(8,128)(2,1)S(1)}, bf16[8,40,128,128]{3,2,1,0:T(8,128)(2,1)}, u32[]{:S(2)}) %copy-start) | copy-done | bytes 10485784
  12.8 0.9 shard_map.51
  13.8 15.2 %collective-permute-done.3 = bf16[1024,256]{1,0:T(8,128)(2,1)S(1)} collective-permute-done((bf16[1024,256]{1,0:T(8,128)(2,1)S(1)}, bf16[1024,256]{1,0:T(8,128)(2,1)S(1)}, u32[]{:S(2)}, u32[]{:S(2)}) %collective-permute-start.3) | collective-permute-done | bytes 524320 | tf_op jit(solution)/shard_map/ppermute | solution.py:20
  28.9 0.2 collective-permute-done.1
  29.1 0.5 collective-permute-start.4
  29.6 1.7 %collective-permute-done.5 = bf16[1024,256]{1,0:T(8,128)(2,1)S(1)} collective-permute-done((bf16[1024,256]{1,0:T(8,128)(2,1)S(1)}, bf16[1024,256]{1,0:T(8,128)(2,1)S(1)}, u32[]{:S(2)}, u32[]{:S(2)}) %collective-permute-start.5) | collective-permute-done | bytes 524320 | tf_op jit(solution)/shard_map/ppermute | solution.py:20
  31.3 0.5 collective-permute-done.4
  31.7 4.0 %shard_map.52 = (f32[1024,256]{1,0:T(8,128)S(1)}, bf16[1024,256]{1,0:T(8,128)(2,1)S(1)}) custom-call(s32[8,40]{1,0:T(8,128)S(1)} %get-tuple-element.36.place_ref, bf16[8,40,128,128]{3,2,1,0:T(8,128)(2,1)S(1)} %get-tuple-element.37.tiles_ref, bf16[256,256]{1,0:T(8,128)(2,1)S(1)} %get-tuple-element.38.turn_ref, bf16[8,128,256]{2,1,0:T(8,128)(2,1)S(1)} %bitcast.17, ...), custom_call_target="tpu_custom_call" | custom-call | flops 8000000000 | bytes 10485760 | tf_op jit(solution)/shard_map/pallas_call | solution.py:135
  35.7 4.9 %collective-permute-start.11 = (bf16[1024,256]{1,0:T(8,128)(2,1)S(1)}, bf16[1024,256]{1,0:T(8,128)(2,1)S(1)}, u32[]{:S(2)}, u32[]{:S(2)}) collective-permute-start(bf16[1024,256]{1,0:T(8,128)(2,1)S(1)} %get-tuple-element.49.sent_ref), channel_id=1, source_target_pairs={{0,14},{1,15},{2,0},{3,1},{4,2},{5,3},{6,4},{7,5},{8,6},{9,7},{10,... | collective-permute-start | bytes 1572872 | tf_op jit(solution)/shard_map/ppermute | solution.py:20
  40.6 2.7 %shard_map.53 = (f32[384,128]{1,0:T(8,128)S(1)}, f32[384,128]{1,0:T(8,128)S(1)}) custom-call(f32[1024,256]{1,0:T(8,128)S(1)} %get-tuple-element.44.product_ref, bf16[1024,256]{1,0:T(8,128)(2,1)S(1)} %get-tuple-element.40.rounded_ref), custom_call_target="tpu_custom_call" | custom-call | flops 8000000000 | bytes 1048576 | tf_op jit(solution)/shard_map/pallas_call | solution.py:43
  43.4 0.1 collective-permute-start.6
  43.5 1.4 %collective-permute-done.6.b_ref = f32[384,128]{1,0:T(8,128)S(1)} collective-permute-done((f32[384,128]{1,0:T(8,128)S(1)}, f32[384,128]{1,0:T(8,128)S(1)}, u32[]{:S(2)}, u32[]{:S(2)}) %collective-permute-start.6) | collective-permute-done | bytes 196640 | tf_op jit(solution)/shard_map/ppermute | solution.py:20
  44.9 1.7 %collective-permute-start.9 = (f32[192,128]{1,0:T(8,128)S(1)}, f32[192,128]{1,0:T(8,128)S(1)}, u32[]{:S(2)}, u32[]{:S(2)}) collective-permute-start(f32[192,128]{1,0:T(8,128)S(1)} %get-tuple-element.48), channel_id=1, source_target_pairs={{0,2},{1,3},{2,0},{3,1},{4,6},{5,7},{6,4},{7,5},{8,10},{9,11},{10,... | collective-permute-start | bytes 294920 | tf_op jit(solution)/shard_map/ppermute | solution.py:20
  46.6 3.1 %collective-permute-start.13 = (bf16[1024,256]{1,0:T(8,128)(2,1)S(1)}, bf16[1024,256]{1,0:T(8,128)(2,1)S(1)}, u32[]{:S(2)}, u32[]{:S(2)}) collective-permute-start(bf16[1024,256]{1,0:T(8,128)(2,1)S(1)} %get-tuple-element.49.sent_ref), channel_id=1, source_target_pairs={{0,13},{1,4},{2,15},{3,6},{4,1},{5,8},{6,3},{7,10},{8,5},{9,12},{1... | collective-permute-start | bytes 1572872 | tf_op jit(solution)/shard_map/ppermute | solution.py:20
  49.7 14.3 %collective-permute-done.9.b_ref = f32[192,128]{1,0:T(8,128)S(1)} collective-permute-done((f32[192,128]{1,0:T(8,128)S(1)}, f32[192,128]{1,0:T(8,128)S(1)}, u32[]{:S(2)}, u32[]{:S(2)}) %collective-permute-start.9) | collective-permute-done | bytes 98336 | tf_op jit(solution)/shard_map/ppermute | solution.py:20
  64.0 0.1 collective-permute-start.12
  64.1 0.5 collective-permute-start.10
  64.6 1.2 %collective-permute-start.14 = (f32[192,128]{1,0:T(8,128)S(1)}, f32[192,128]{1,0:T(8,128)S(1)}, u32[]{:S(2)}, u32[]{:S(2)}) collective-permute-start(f32[192,128]{1,0:T(8,128)S(1)} %shard_map.55.a_ref), channel_id=1, source_target_pairs={{0,4},{1,5},{2,6},{3,7},{4,0},{5,1},{6,2},{7,3},{8,12},{9,13},{10,... | collective-permute-start | bytes 294920 | tf_op jit(solution)/shard_map/ppermute | solution.py:20
  65.8 0.2 collective-permute-done.12
  66.0 0.7 collective-permute-done.10
  66.8 4.1 %shard_map.56.product_ref = f32[1024,256]{1,0:T(8,128)S(1)} custom-call(s32[8,40]{1,0:T(8,128)S(1)} %get-tuple-element.36.place_ref, bf16[8,40,128,128]{3,2,1,0:T(8,128)(2,1)S(1)} %get-tuple-element.37.tiles_ref, bf16[256,256]{1,0:T(8,128)(2,1)S(1)} %get-tuple-element.38.turn_ref, bf16[8,128,256]{2,1,0:T(8,128)(2,1)S(1)} %bitcast.14, ...), custom_call_target="tpu_custom_call" | custom-call | flops 8000000000 | bytes 10485760 | tf_op jit(solution)/shard_map/pallas_call | solution.py:135
  70.9 1.5 %shard_map.57 = (f32[192,128]{1,0:T(8,128)S(1)}, f32[192,128]{1,0:T(8,128)S(1)}, f32[192,128]{1,0:T(8,128)S(1)}) custom-call(f32[1024,256]{1,0:T(8,128)S(1)} %shard_map.56.product_ref, f32[192,128]{1,0:T(8,128)S(1)} %shard_map.55.a_ref, f32[192,128]{1,0:T(8,128)S(1)} %collective-permute-done.14.b_ref), custom_call_target="tpu_custom_call" | custom-call | flops 8000000000 | bytes 1048576 | tf_op jit(solution)/shard_map/pallas_call | solution.py:43
  72.4 0.2 collective-permute-start.15
  72.6 1.2 %collective-permute-done.15.b_ref = f32[192,128]{1,0:T(8,128)S(1)} collective-permute-done((f32[192,128]{1,0:T(8,128)S(1)}, f32[192,128]{1,0:T(8,128)S(1)}, u32[]{:S(2)}, u32[]{:S(2)}) %collective-permute-start.15) | collective-permute-done | bytes 98336 | tf_op jit(solution)/shard_map/ppermute | solution.py:20
  73.8 2.5 %collective-permute-start.17 = (f32[192,128]{1,0:T(8,128)S(1)}, f32[192,128]{1,0:T(8,128)S(1)}, u32[]{:S(2)}, u32[]{:S(2)}) collective-permute-start(f32[192,128]{1,0:T(8,128)S(1)} %shard_map.58.a_ref), channel_id=1, source_target_pairs={{0,2},{1,3},{2,0},{3,1},{4,6},{5,7},{6,4},{7,5},{8,10},{9,11},{10,... | collective-permute-start | bytes 294920 | tf_op jit(solution)/shard_map/ppermute | solution.py:20
  76.3 2.1 %collective-permute-start.16 = (f32[192,128]{1,0:T(8,128)S(1)}, f32[192,128]{1,0:T(8,128)S(1)}, u32[]{:S(2)}, u32[]{:S(2)}) collective-permute-start(f32[192,128]{1,0:T(8,128)S(1)} %get-tuple-element.56.a_ref), channel_id=1, source_target_pairs={{0,8},{1,9},{2,10},{3,11},{4,12},{5,13},{6,14},{7,15},{8,0},{9,1},... | collective-permute-start | bytes 294920 | tf_op jit(solution)/shard_map/ppermute | solution.py:20
  78.5 1.0 collective-permute-done.17.b_ref
  79.5 0.7 collective-permute-start.18
  80.2 1.8 %shard_map.66 = (f32[192,128]{1,0:T(8,128)S(1)}, f32[192,128]{1,0:T(8,128)S(1)}) custom-call(f32[1024,256]{1,0:T(8,128)S(1)} %shard_map.56.product_ref, bf16[1024,256]{1,0:T(8,128)(2,1)S(1)} %get-tuple-element.49.sent_ref, bf16[256,256]{1,0:T(8,128)(2,1)S(1)} %get-tuple-element.38.turn_ref), custom_call_target="tpu_custom_call" | custom-call | flops 8000000000 | bytes 1048576 | tf_op jit(solution)/shard_map/pallas_call | solution.py:43
  82.0 0.1 collective-permute-start.24
  82.1 3.6 %collective-permute-done.18.b_ref = f32[192,128]{1,0:T(8,128)S(1)} collective-permute-done((f32[192,128]{1,0:T(8,128)S(1)}, f32[192,128]{1,0:T(8,128)S(1)}, u32[]{:S(2)}, u32[]{:S(2)}) %collective-permute-start.18) | collective-permute-done | bytes 98336 | tf_op jit(solution)/shard_map/ppermute | solution.py:20
  85.8 0.7 collective-permute-start.19
  86.5 1.6 %collective-permute-start.22 = (f32[192,128]{1,0:T(8,128)S(1)}, f32[192,128]{1,0:T(8,128)S(1)}, u32[]{:S(2)}, u32[]{:S(2)}) collective-permute-start(f32[192,128]{1,0:T(8,128)S(1)} %shard_map.60.a_ref), channel_id=1, source_target_pairs={{0,8},{1,9},{2,10},{3,11},{4,12},{5,13},{6,14},{7,15},{8,0},{9,1},... | collective-permute-start | bytes 294920 | tf_op jit(solution)/shard_map/ppermute | solution.py:20
  88.1 0.4 collective-permute-start.25
  88.6 2.8 %collective-permute-done.19.other_ref = f32[192,128]{1,0:T(8,128)S(1)} collective-permute-done((f32[192,128]{1,0:T(8,128)S(1)}, f32[192,128]{1,0:T(8,128)S(1)}, u32[]{:S(2)}, u32[]{:S(2)}) %collective-permute-start.19) | collective-permute-done | bytes 98336 | tf_op jit(solution)/shard_map/ppermute | solution.py:20
  91.4 2.0 %collective-permute-done.22.b_ref = f32[192,128]{1,0:T(8,128)S(1)} collective-permute-done((f32[192,128]{1,0:T(8,128)S(1)}, f32[192,128]{1,0:T(8,128)S(1)}, u32[]{:S(2)}, u32[]{:S(2)}) %collective-permute-start.22) | collective-permute-done | bytes 98336 | tf_op jit(solution)/shard_map/ppermute | solution.py:20
  93.5 1.1 collective-permute-start.26
  94.6 0.2 collective-permute-done.23.raw_rest_ref
  94.8 2.8 %shard_map.63 = (f32[2,64,256]{2,1,0:T(8,128)S(1)}, f32[2,192,256]{2,1,0:T(8,128)S(1)}, f32[2,256]{1,0:T(2,128)S(1)}) custom-call(f32[192,128]{1,0:T(8,128)S(1)} %shard_map.61.keep_ref, f32[192,128]{1,0:T(8,128)S(1)} %collective-permute-done.19.other_ref, f32[192,128]{1,0:T(8,128)S(1)} %collective-permute-done.20.keep_rest_ref, ...), custom_call_target="tpu_custom_call" | custom-call | flops 8000000000 | bytes 1048576 | tf_op jit(solution)/shard_map/pallas_call | solution.py:43
  97.6 1.1 %collective-permute-done.26.b_ref = f32[192,128]{1,0:T(8,128)S(1)} collective-permute-done((f32[192,128]{1,0:T(8,128)S(1)}, f32[192,128]{1,0:T(8,128)S(1)}, u32[]{:S(2)}, u32[]{:S(2)}) %collective-permute-start.26) | collective-permute-done | bytes 98336 | tf_op jit(solution)/shard_map/ppermute | solution.py:20
  98.8 1.1 collective-permute-start.27
  99.9 6.6 %shard_map.64 = (f32[256,256]{1,0:T(8,128)S(1)}, f32[256,256]{1,0:T(8,128)S(1)}) custom-call(f32[2,64,256]{2,1,0:T(8,128)S(1)} %get-tuple-element.58.done_ref, f32[2,192,256]{2,1,0:T(8,128)S(1)} %get-tuple-element.59.rest_ref, f32[2,256]{1,0:T(2,128)S(1)} %get-tuple-element.60.scale_ref), custom_call_target="tpu_custom_call" | custom-call | flops 24000000000 | bytes 1048576 | tf_op jit(solution)/shard_map/pallas_call | solution.py:43
  106.6 2.4 %shard_map.65 = f32[1024,256]{1,0:T(8,128)} custom-call(f32[1024,256]{1,0:T(8,128)S(1)} %shard_map.56.product_ref, f32[256,256]{1,0:T(8,128)S(1)} %get-tuple-element.61.inverse_ref), custom_call_target="tpu_custom_call" | custom-call | flops 8000000000 | bytes 1048576 | tf_op jit(solution)/shard_map/pallas_call | solution.py:43
  109.0 1.9 %shard_map.71 = f32[2,256,256]{2,1,0:T(8,128)} custom-call(f32[192,128]{1,0:T(8,128)S(1)} %shard_map.61.keep_ref, f32[192,128]{1,0:T(8,128)S(1)} %collective-permute-done.19.other_ref, f32[192,128]{1,0:T(8,128)S(1)} %collective-permute-done.20.keep_rest_ref, f32[192,128]{1,0:T(8,128)S(1)} %collective-permute-done.21.other_rest_ref, ...), custom_call_target="tpu_custom_call" | custom-call | bytes 1048576 | tf_op jit(solution)/shard_map/pallas_call | solution.py:43
  (38 shorter events, 0.4 us)
Async XLA Ops:
  0.6 1.2 %copy-start.1 = (f32[1024,256]{1,0:T(8,128)S(1)}, f32[1024,256]{1,0:T(8,128)}, u32[]{:S(2)}) copy-start(f32[1024,256]{1,0:T(8,128)} %basis_ref.1) | copy-start | bytes 3145732
  1.9 0.7 copy-start.2
  2.7 26.2 %collective-permute-start.3 = (bf16[1024,256]{1,0:T(8,128)(2,1)S(1)}, bf16[1024,256]{1,0:T(8,128)(2,1)S(1)}, u32[]{:S(2)}, u32[]{:S(2)}) collective-permute-start(bf16[1024,256]{1,0:T(8,128)(2,1)S(1)} %get-tuple-element.40.rounded_ref), channel_id=1, source_target_pairs={{0,14},{1,15},{2,0},{3,1},{4,2},{5,3},{6,4},{7,5},{8,6},{9,7},{10,... | collective-permute-start | bytes 1572872 | tf_op jit(solution)/shard_map/ppermute | solution.py:20
  8.8 20.3 %collective-permute-start.1 = (bf16[1024,256]{1,0:T(8,128)(2,1)S(1)}, bf16[1024,256]{1,0:T(8,128)(2,1)S(1)}, u32[]{:S(2)}, u32[]{:S(2)}) collective-permute-start(bf16[1024,256]{1,0:T(8,128)(2,1)S(1)} %get-tuple-element.40.rounded_ref), channel_id=1, source_target_pairs={{0,2},{1,3},{2,4},{3,5},{4,6},{5,7},{6,8},{7,9},{8,10},{9,11},{10,... | collective-permute-start | bytes 1572872 | tf_op jit(solution)/shard_map/ppermute | solution.py:20
  8.8 22.5 %collective-permute-start.5 = (bf16[1024,256]{1,0:T(8,128)(2,1)S(1)}, bf16[1024,256]{1,0:T(8,128)(2,1)S(1)}, u32[]{:S(2)}, u32[]{:S(2)}) collective-permute-start(bf16[1024,256]{1,0:T(8,128)(2,1)S(1)} %get-tuple-element.40.rounded_ref), channel_id=1, source_target_pairs={{0,13},{1,4},{2,15},{3,6},{4,1},{5,8},{6,3},{7,10},{8,5},{9,12},{1... | collective-permute-start | bytes 1572872 | tf_op jit(solution)/shard_map/ppermute | solution.py:20
  8.8 4.0 %copy-start = (bf16[8,40,128,128]{3,2,1,0:T(8,128)(2,1)S(1)}, bf16[8,40,128,128]{3,2,1,0:T(8,128)(2,1)}, u32[]{:S(2)}) copy-start(bf16[8,40,128,128]{3,2,1,0:T(8,128)(2,1)} %tiles_ref.1) | copy-start | bytes 31457284
  13.7 17.6 %collective-permute-start = (bf16[1024,256]{1,0:T(8,128)(2,1)S(1)}, bf16[1024,256]{1,0:T(8,128)(2,1)S(1)}, u32[]{:S(2)}, u32[]{:S(2)}) collective-permute-start(bf16[1024,256]{1,0:T(8,128)(2,1)S(1)} %get-tuple-element.40.rounded_ref), channel_id=1, source_target_pairs={{0,1},{1,0},{2,3},{3,2},{4,5},{5,4},{6,7},{7,6},{8,9},{9,8},{10,11... | collective-permute-start | bytes 1572872 | tf_op jit(solution)/shard_map/ppermute | solution.py:20
  29.1 2.2 %collective-permute-start.2 = (bf16[1024,256]{1,0:T(8,128)(2,1)S(1)}, bf16[1024,256]{1,0:T(8,128)(2,1)S(1)}, u32[]{:S(2)}, u32[]{:S(2)}) collective-permute-start(bf16[1024,256]{1,0:T(8,128)(2,1)S(1)} %collective-permute-done.1), channel_id=1, source_target_pairs={{0,1},{1,0},{2,3},{3,2},{4,5},{5,4},{6,7},{7,6},{8,9},{9,8},{10,11... | collective-permute-start | bytes 1572872 | tf_op jit(solution)/shard_map/ppermute | solution.py:20
  29.1 2.6 %collective-permute-start.4 = (bf16[1024,256]{1,0:T(8,128)(2,1)S(1)}, bf16[1024,256]{1,0:T(8,128)(2,1)S(1)}, u32[]{:S(2)}, u32[]{:S(2)}) collective-permute-start(bf16[1024,256]{1,0:T(8,128)(2,1)S(1)} %collective-permute-done.3), channel_id=1, source_target_pairs={{0,1},{1,0},{2,3},{3,2},{4,5},{5,4},{6,7},{7,6},{8,9},{9,8},{10,11... | collective-permute-start | bytes 1572872 | tf_op jit(solution)/shard_map/ppermute | solution.py:20
  35.7 28.3 %collective-permute-start.11 = (bf16[1024,256]{1,0:T(8,128)(2,1)S(1)}, bf16[1024,256]{1,0:T(8,128)(2,1)S(1)}, u32[]{:S(2)}, u32[]{:S(2)}) collective-permute-start(bf16[1024,256]{1,0:T(8,128)(2,1)S(1)} %get-tuple-element.49.sent_ref), channel_id=1, source_target_pairs={{0,14},{1,15},{2,0},{3,1},{4,2},{5,3},{6,4},{7,5},{8,6},{9,7},{10,... | collective-permute-start | bytes 1572872 | tf_op jit(solution)/shard_map/ppermute | solution.py:20
  40.6 23.5 %collective-permute-start.8 = (bf16[1024,256]{1,0:T(8,128)(2,1)S(1)}, bf16[1024,256]{1,0:T(8,128)(2,1)S(1)}, u32[]{:S(2)}, u32[]{:S(2)}) collective-permute-start(bf16[1024,256]{1,0:T(8,128)(2,1)S(1)} %get-tuple-element.49.sent_ref), channel_id=1, source_target_pairs={{0,2},{1,3},{2,4},{3,5},{4,6},{5,7},{6,8},{7,9},{8,10},{9,11},{10,... | collective-permute-start | bytes 1572872 | tf_op jit(solution)/shard_map/ppermute | solution.py:20
  43.4 1.5 %collective-permute-start.6 = (f32[384,128]{1,0:T(8,128)S(1)}, f32[384,128]{1,0:T(8,128)S(1)}, u32[]{:S(2)}, u32[]{:S(2)}) collective-permute-start(f32[384,128]{1,0:T(8,128)S(1)} %get-tuple-element.46), channel_id=1, source_target_pairs={{0,1},{1,0},{2,3},{3,2},{4,5},{5,4},{6,7},{7,6},{8,9},{9,8},{10,11... | collective-permute-start | bytes 589832 | tf_op jit(solution)/shard_map/ppermute | solution.py:20
  44.9 19.1 %collective-permute-start.9 = (f32[192,128]{1,0:T(8,128)S(1)}, f32[192,128]{1,0:T(8,128)S(1)}, u32[]{:S(2)}, u32[]{:S(2)}) collective-permute-start(f32[192,128]{1,0:T(8,128)S(1)} %get-tuple-element.48), channel_id=1, source_target_pairs={{0,2},{1,3},{2,0},{3,1},{4,6},{5,7},{6,4},{7,5},{8,10},{9,11},{10,... | collective-permute-start | bytes 294920 | tf_op jit(solution)/shard_map/ppermute | solution.py:20
  46.6 19.1 %collective-permute-start.13 = (bf16[1024,256]{1,0:T(8,128)(2,1)S(1)}, bf16[1024,256]{1,0:T(8,128)(2,1)S(1)}, u32[]{:S(2)}, u32[]{:S(2)}) collective-permute-start(bf16[1024,256]{1,0:T(8,128)(2,1)S(1)} %get-tuple-element.49.sent_ref), channel_id=1, source_target_pairs={{0,13},{1,4},{2,15},{3,6},{4,1},{5,8},{6,3},{7,10},{8,5},{9,12},{1... | collective-permute-start | bytes 1572872 | tf_op jit(solution)/shard_map/ppermute | solution.py:20
  49.7 16.0 %collective-permute-start.7 = (bf16[1024,256]{1,0:T(8,128)(2,1)S(1)}, bf16[1024,256]{1,0:T(8,128)(2,1)S(1)}, u32[]{:S(2)}, u32[]{:S(2)}) collective-permute-start(bf16[1024,256]{1,0:T(8,128)(2,1)S(1)} %get-tuple-element.49.sent_ref), channel_id=1, source_target_pairs={{0,1},{1,0},{2,3},{3,2},{4,5},{5,4},{6,7},{7,6},{8,9},{9,8},{10,11... | collective-permute-start | bytes 1572872 | tf_op jit(solution)/shard_map/ppermute | solution.py:20
  64.0 2.0 %collective-permute-start.12 = (bf16[1024,256]{1,0:T(8,128)(2,1)S(1)}, bf16[1024,256]{1,0:T(8,128)(2,1)S(1)}, u32[]{:S(2)}, u32[]{:S(2)}) collective-permute-start(bf16[1024,256]{1,0:T(8,128)(2,1)S(1)} %collective-permute-done.11), channel_id=1, source_target_pairs={{0,1},{1,0},{2,3},{3,2},{4,5},{5,4},{6,7},{7,6},{8,9},{9,8},{10,11... | collective-permute-start | bytes 1572872 | tf_op jit(solution)/shard_map/ppermute | solution.py:20
  64.1 2.6 %collective-permute-start.10 = (bf16[1024,256]{1,0:T(8,128)(2,1)S(1)}, bf16[1024,256]{1,0:T(8,128)(2,1)S(1)}, u32[]{:S(2)}, u32[]{:S(2)}) collective-permute-start(bf16[1024,256]{1,0:T(8,128)(2,1)S(1)} %collective-permute-done.8), channel_id=1, source_target_pairs={{0,1},{1,0},{2,3},{3,2},{4,5},{5,4},{6,7},{7,6},{8,9},{9,8},{10,11... | collective-permute-start | bytes 1572872 | tf_op jit(solution)/shard_map/ppermute | solution.py:20
  64.6 6.3 %collective-permute-start.14 = (f32[192,128]{1,0:T(8,128)S(1)}, f32[192,128]{1,0:T(8,128)S(1)}, u32[]{:S(2)}, u32[]{:S(2)}) collective-permute-start(f32[192,128]{1,0:T(8,128)S(1)} %shard_map.55.a_ref), channel_id=1, source_target_pairs={{0,4},{1,5},{2,6},{3,7},{4,0},{5,1},{6,2},{7,3},{8,12},{9,13},{10,... | collective-permute-start | bytes 294920 | tf_op jit(solution)/shard_map/ppermute | solution.py:20
  72.4 1.4 %collective-permute-start.15 = (f32[192,128]{1,0:T(8,128)S(1)}, f32[192,128]{1,0:T(8,128)S(1)}, u32[]{:S(2)}, u32[]{:S(2)}) collective-permute-start(f32[192,128]{1,0:T(8,128)S(1)} %get-tuple-element.54), channel_id=1, source_target_pairs={{0,1},{1,0},{2,3},{3,2},{4,5},{5,4},{6,7},{7,6},{8,9},{9,8},{10,11... | collective-permute-start | bytes 294920 | tf_op jit(solution)/shard_map/ppermute | solution.py:20
  73.8 5.7 %collective-permute-start.17 = (f32[192,128]{1,0:T(8,128)S(1)}, f32[192,128]{1,0:T(8,128)S(1)}, u32[]{:S(2)}, u32[]{:S(2)}) collective-permute-start(f32[192,128]{1,0:T(8,128)S(1)} %shard_map.58.a_ref), channel_id=1, source_target_pairs={{0,2},{1,3},{2,0},{3,1},{4,6},{5,7},{6,4},{7,5},{8,10},{9,11},{10,... | collective-permute-start | bytes 294920 | tf_op jit(solution)/shard_map/ppermute | solution.py:20
  76.3 9.4 %collective-permute-start.16 = (f32[192,128]{1,0:T(8,128)S(1)}, f32[192,128]{1,0:T(8,128)S(1)}, u32[]{:S(2)}, u32[]{:S(2)}) collective-permute-start(f32[192,128]{1,0:T(8,128)S(1)} %get-tuple-element.56.a_ref), channel_id=1, source_target_pairs={{0,8},{1,9},{2,10},{3,11},{4,12},{5,13},{6,14},{7,15},{8,0},{9,1},... | collective-permute-start | bytes 294920 | tf_op jit(solution)/shard_map/ppermute | solution.py:20
  79.5 6.3 %collective-permute-start.18 = (f32[192,128]{1,0:T(8,128)S(1)}, f32[192,128]{1,0:T(8,128)S(1)}, u32[]{:S(2)}, u32[]{:S(2)}) collective-permute-start(f32[192,128]{1,0:T(8,128)S(1)} %shard_map.59.a_ref), channel_id=1, source_target_pairs={{0,4},{1,5},{2,6},{3,7},{4,0},{5,1},{6,2},{7,3},{8,12},{9,13},{10,... | collective-permute-start | bytes 294920 | tf_op jit(solution)/shard_map/ppermute | solution.py:20
  82.0 6.1 %collective-permute-start.24 = (f32[192,128]{1,0:T(8,128)S(1)}, f32[192,128]{1,0:T(8,128)S(1)}, u32[]{:S(2)}, u32[]{:S(2)}) collective-permute-start(f32[192,128]{1,0:T(8,128)S(1)} %get-tuple-element.64), channel_id=1, source_target_pairs={{0,1},{1,0},{2,3},{3,2},{4,5},{5,4},{6,7},{7,6},{8,9},{9,8},{10,11... | collective-permute-start | bytes 294920 | tf_op jit(solution)/shard_map/ppermute | solution.py:20
  85.8 5.6 %collective-permute-start.19 = (f32[192,128]{1,0:T(8,128)S(1)}, f32[192,128]{1,0:T(8,128)S(1)}, u32[]{:S(2)}, u32[]{:S(2)}) collective-permute-start(f32[192,128]{1,0:T(8,128)S(1)} %shard_map.61.keep_ref), channel_id=1, source_target_pairs={{0,2},{1,3},{2,0},{3,1},{4,6},{5,7},{6,4},{7,5},{8,10},{9,11},{10,... | collective-permute-start | bytes 294920 | tf_op jit(solution)/shard_map/ppermute | solution.py:20
  86.5 6.9 %collective-permute-start.22 = (f32[192,128]{1,0:T(8,128)S(1)}, f32[192,128]{1,0:T(8,128)S(1)}, u32[]{:S(2)}, u32[]{:S(2)}) collective-permute-start(f32[192,128]{1,0:T(8,128)S(1)} %shard_map.60.a_ref), channel_id=1, source_target_pairs={{0,8},{1,9},{2,10},{3,11},{4,12},{5,13},{6,14},{7,15},{8,0},{9,1},... | collective-permute-start | bytes 294920 | tf_op jit(solution)/shard_map/ppermute | solution.py:20
  88.1 5.4 %collective-permute-start.25 = (f32[192,128]{1,0:T(8,128)S(1)}, f32[192,128]{1,0:T(8,128)S(1)}, u32[]{:S(2)}, u32[]{:S(2)}) collective-permute-start(f32[192,128]{1,0:T(8,128)S(1)} %shard_map.67.a_ref), channel_id=1, source_target_pairs={{0,2},{1,3},{2,0},{3,1},{4,6},{5,7},{6,4},{7,5},{8,10},{9,11},{10,... | collective-permute-start | bytes 294920 | tf_op jit(solution)/shard_map/ppermute | solution.py:20
  88.6 6.1 %collective-permute-start.20 = (f32[192,128]{1,0:T(8,128)S(1)}, f32[192,128]{1,0:T(8,128)S(1)}, u32[]{:S(2)}, u32[]{:S(2)}) collective-permute-start(f32[192,128]{1,0:T(8,128)S(1)} %shard_map.61.keep_ref), channel_id=1, source_target_pairs={{0,1},{1,0},{2,3},{3,2},{4,5},{5,4},{6,7},{7,6},{8,9},{9,8},{10,11... | collective-permute-start | bytes 294920 | tf_op jit(solution)/shard_map/ppermute | solution.py:20
  91.4 3.3 %collective-permute-start.21 = (f32[192,128]{1,0:T(8,128)S(1)}, f32[192,128]{1,0:T(8,128)S(1)}, u32[]{:S(2)}, u32[]{:S(2)}) collective-permute-start(f32[192,128]{1,0:T(8,128)S(1)} %collective-permute-done.19.other_ref), channel_id=1, source_target_pairs={{0,1},{1,0},{2,3},{3,2},{4,5},{5,4},{6,7},{7,6},{8,9},{9,8},{10,11... | collective-permute-start | bytes 294920 | tf_op jit(solution)/shard_map/ppermute | solution.py:20
  93.4 1.4 %collective-permute-start.23 = (f32[192,128]{1,0:T(8,128)S(1)}, f32[192,128]{1,0:T(8,128)S(1)}, u32[]{:S(2)}, u32[]{:S(2)}) collective-permute-start(f32[192,128]{1,0:T(8,128)S(1)} %shard_map.62.raw_ref), channel_id=1, source_target_pairs={{0,1},{1,0},{2,3},{3,2},{4,5},{5,4},{6,7},{7,6},{8,9},{9,8},{10,11... | collective-permute-start | bytes 294920 | tf_op jit(solution)/shard_map/ppermute | solution.py:20
  93.5 5.2 %collective-permute-start.26 = (f32[192,128]{1,0:T(8,128)S(1)}, f32[192,128]{1,0:T(8,128)S(1)}, u32[]{:S(2)}, u32[]{:S(2)}) collective-permute-start(f32[192,128]{1,0:T(8,128)S(1)} %shard_map.68.a_ref), channel_id=1, source_target_pairs={{0,4},{1,5},{2,6},{3,7},{4,0},{5,1},{6,2},{7,3},{8,12},{9,13},{10,... | collective-permute-start | bytes 294920 | tf_op jit(solution)/shard_map/ppermute | solution.py:20
  98.8 7.7 %collective-permute-start.27 = (f32[192,128]{1,0:T(8,128)S(1)}, f32[192,128]{1,0:T(8,128)S(1)}, u32[]{:S(2)}, u32[]{:S(2)}) collective-permute-start(f32[192,128]{1,0:T(8,128)S(1)} %shard_map.69.a_ref), channel_id=1, source_target_pairs={{0,8},{1,9},{2,10},{3,11},{4,12},{5,13},{6,14},{7,15},{8,0},{9,1},... | collective-permute-start | bytes 294920 | tf_op jit(solution)/shard_map/ppermute | solution.py:20
  106.5 2.5 %collective-permute-start.28 = (f32[192,128]{1,0:T(8,128)S(1)}, f32[192,128]{1,0:T(8,128)S(1)}, u32[]{:S(2)}, u32[]{:S(2)}) collective-permute-start(f32[192,128]{1,0:T(8,128)S(1)} %shard_map.70.proj_ref), channel_id=1, source_target_pairs={{0,1},{1,0},{2,3},{3,2},{4,5},{5,4},{6,7},{7,6},{8,9},{9,8},{10,11... | collective-permute-start | bytes 294920 | tf_op jit(solution)/shard_map/ppermute | solution.py:20

commit v4 on v3

--- a/solution.py
+++ b/solution.py
@@ -49,16 +49,7 @@
     )(*args)
 
 
-def prepare_kernel(pattern_ref, basis_ref, place_ref, rounded_ref, held, sems, *, block_rows, peers):
-    parts = sems.shape[0]
-    step = basis_ref.shape[0] // parts
-    at = [slice(i * step, (i + 1) * step) for i in range(parts)]
-    copies = [pltpu.make_async_copy(basis_ref.at[at[i]], held.at[at[i]], sems.at[i]) for i in range(parts)]
-    for c in copies:
-        c.start()
-    for i in range(parts):
-        copies[i].wait()
-        rounded_ref[at[i], :] = held[at[i], :].astype(jnp.bfloat16)
+def place_kernel(pattern_ref, place_ref, *, block_rows, peers):
     me = lax.axis_index("rows")
     pattern = pattern_ref[...]
     owner = lax.div(pattern, block_rows)
@@ -146,6 +137,16 @@
     return lax.dot_general(a, b, (dims, ((), ())), precision=lax.Precision.HIGHEST, preferred_element_type=jnp.float32)
 
 
+def two_parts(x):
+    high = x.astype(jnp.bfloat16)
+    return high, (x - high.astype(jnp.float32)).astype(jnp.bfloat16)
+
+
+def near_dot(a, b, dims=((1,), (0,))):
+    one = lambda u, v: lax.dot_general(u, v, (dims, ((), ())), preferred_element_type=jnp.float32)
+    return one(a[0], b[0]) + (one(a[0], b[1]) + one(a[1], b[0]))
+
+
 def my_bit(bit):
     return lax.rem(lax.div(lax.axis_index("rows"), bit), 2)
 
@@ -153,8 +154,9 @@
 def halves(left, right):
     down = ((0,), (0,))
     h = right.shape[1] // 2
-    la, lb, ra, rb = left[:, :h], left[:, h:], right[:, :h], right[:, h:]
-    low, mid, high = dot(la, ra, down), dot(lb, ra, down), dot(lb, rb, down)
+    left, right = two_parts(left), two_parts(right)
+    la, lb, ra, rb = ([p[:, at] for p in x] for x in (left, right) for at in (slice(0, h), slice(h, 2 * h)))
+    low, mid, high = near_dot(la, ra, down), near_dot(lb, ra, down), near_dot(lb, rb, down)
     first = jnp.concatenate([low, mid[: h // 2]], axis=0)
     last = jnp.concatenate([mid[h // 2 :], high], axis=0)
     core = my_bit(1)
@@ -373,24 +375,38 @@
         ref[...] = inverse_factor(jnp.concatenate([done_ref[m], done[m]], axis=0), scale_ref[m : m + 1, :])
 
 
-def modes_kernel(product_ref, inverse_ref, modes_ref, *, scale):
-    inverse = inverse_ref[...] * scale
-    h = inverse.shape[0] // 2
+def modes_kernel(product_ref, inverse_ref, modes_ref, held, sems, *, scale):
+    inverse = two_parts(inverse_ref[...] * scale)
+    h = inverse_ref.shape[0] // 2
     along = ((1,), (1,))
-    modes_ref[:, :h] = dot(product_ref[:, :h], inverse[:h, :h], along)
-    modes_ref[:, h:] = dot(product_ref[...], inverse[h:, :], along)
+    step = product_ref.shape[0] // sems.shape[0]
+    copies = []
+    for i in range(sems.shape[0]):
+        at = slice(i * step, (i + 1) * step)
+        product = two_parts(product_ref[at, :])
+        held[at, :h] = near_dot([p[:, :h] for p in product], [w[:h, :h] for w in inverse], along)
+        held[at, h:] = near_dot(product, [w[h:, :] for w in inverse], along)
+        copies.append(pltpu.make_async_copy(held.at[at], modes_ref.at[at], sems.at[i]))
+        copies[-1].start()
+    for c in copies:
+        c.wait()
 
 
 def projected_kernel(
-    keep_ref, other_ref, keep_rest_ref, other_rest_ref, proj_ref, proj_rest_ref, inverse_ref, projected_ref
+    keep_ref, other_ref, keep_rest_ref, other_rest_ref, proj_ref, proj_rest_ref, inverse_ref, projected_ref, held, sems
 ):
+    copies = [pltpu.make_async_copy(held.at[i], projected_ref.at[i], sems.at[i]) for i in range(2)]
     bit = my_bit(2)
     mine = jnp.where(bit == 0, other_ref[...], keep_ref[...])
     rest = jnp.where(bit == 0, other_rest_ref[...], keep_rest_ref[...])
-    projected_ref[0] = unpacked(mine, rest)
-    inverse = inverse_ref[...]
-    proj = dot(inverse, unpacked(proj_ref[...], proj_rest_ref[...]))
-    projected_ref[1] = dot(proj, inverse, ((1,), (1,)))
+    held[0] = unpacked(mine, rest)
+    copies[0].start()
+    inverse = two_parts(inverse_ref[...])
+    proj = near_dot(inverse, two_parts(unpacked(proj_ref[...], proj_rest_ref[...])))
+    held[1] = near_dot(two_parts(proj), inverse, ((1,), (1,)))
+    copies[1].start()
+    for c in copies:
+        c.wait()
 
 
 def per_device(tiles, pattern, basis):
@@ -400,16 +416,19 @@
     f32 = lambda *shape: jax.ShapeDtypeStruct(shape, jnp.float32)
     half_sum = f32(3 * modes // 4, modes // 2)
     flops = 6 * rows * modes * modes
-    place, rounded = kernel_call(
-        functools.partial(prepare_kernel, block_rows=block_rows, peers=peers),
-        (jax.ShapeDtypeStruct(pattern.shape, jnp.int32), jax.ShapeDtypeStruct((rows, modes), jnp.bfloat16)),
-        pattern, basis,
-        limit=8,
-        in_specs=[pl.BlockSpec(memory_space=pltpu.VMEM), pl.BlockSpec(memory_space=pltpu.HBM)],
-        scratch_shapes=[pltpu.VMEM(basis.shape, jnp.float32), pltpu.SemaphoreType.DMA((4,))],
-    )
-    pieces, (tiles, turn) = neighbourhood(rounded, lambda: held(tiles, modes))
-    product, sent = product_of(place, tiles, turn, pieces, jnp.float32, jnp.bfloat16)
+    rounded = basis.astype(jnp.bfloat16)
+
+    def meanwhile():
+        place = kernel_call(
+            functools.partial(place_kernel, block_rows=block_rows, peers=peers),
+            jax.ShapeDtypeStruct(pattern.shape, jnp.int32),
+            pattern,
+            limit=4,
+        )
+        return place, *held(tiles, modes)
+
+    pieces, (place, kept, turn) = neighbourhood(rounded, meanwhile)
+    product, sent = product_of(place, kept, turn, pieces, jnp.float32, jnp.bfloat16)
 
     def first_sums():
         mine, rest = kernel_call(
@@ -420,7 +439,7 @@
     pieces, first = neighbourhood(sent, first_sums, lambda made: added(made[0], permuted(made[1], lambda i: i ^ 2)))
     partner = permuted(first, lambda i: i ^ 4)
 
-    (raw,) = product_of(place, tiles, turn, pieces, jnp.float32)
+    (raw,) = product_of(place, kept, turn, pieces, jnp.float32)
     gram, rest, first = kernel_call(gram_kernel, (half_sum,) * 3, raw, first, partner, flops=LONG)
     gram = summed(gram, rest, 1, 2)
     first = after(first, gram)
@@ -437,16 +456,23 @@
         upper_kernel,
         (f32(2, CHUNK * B, modes), f32(2, modes - CHUNK * B, modes), f32(2, modes)),
         *first, gram, swapped(gram),
-        flops=LONG,
+        flops=0,
     )
     proj = added(*after((proj, partner), eliminating[0]))
     partner = permuted(proj, lambda i: i ^ (peers // 2))
     inverse, both = kernel_call(lower_kernel, (f32(modes, modes),) * 2, *eliminating, flops=3 * LONG)
     proj = added(*after((proj, partner), inverse))
     modes_out = kernel_call(
-        functools.partial(modes_kernel, scale=math.sqrt(rows * peers)), f32(rows, modes), raw, both, flops=LONG
+        functools.partial(modes_kernel, scale=math.sqrt(rows * peers)), f32(rows, modes), raw, both,
+        flops=LONG,
+        out_specs=pl.BlockSpec(memory_space=pltpu.HBM),
+        scratch_shapes=[pltpu.VMEM((rows, modes), jnp.float32), pltpu.SemaphoreType.DMA((4,))],
     )
-    projected = kernel_call(projected_kernel, f32(2, modes, modes), *first, proj, swapped(proj), inverse)
+    projected = kernel_call(
+        projected_kernel, f32(2, modes, modes), *first, proj, swapped(proj), inverse,
+        out_specs=pl.BlockSpec(memory_space=pltpu.HBM),
+        scratch_shapes=[pltpu.VMEM((2, modes, modes), jnp.float32), pltpu.SemaphoreType.DMA((2,))],
+    )
     return modes_out, projected
 
 

time: 111 us -> 109 us (0.982)
  Pallas kernels: 29.2 us -> 25.7 us
  starting transfers between devices: 28.9 us -> 30.4 us
  other arithmetic: 0 us -> 1.28 us
  local copies, waits for them, and re-layouts: 5.88 us -> 4.66 us
    pallas_call x19, Pallas kernels: 20.1 us -> 16.2 us  [kernel_call(): pl.pallas_call(kernel, out_shape=out_shape, cost_estimate=pl.CostEstimate...]
    ppermute x29, starting transfers between devices: 28.9 us -> 30.4 us  [permuted(): lax.ppermute(value, 'rows', [(i, target(i) % peers) for i in range(peers)])]
    convert_element_type x0 -> x1, other arithmetic: none -> 1.28 us  [per_device(): rounded = basis.astype(jnp.bfloat16)]
    unnamed x6 -> x4, local copies, waits for them, and re-layouts: 5.88 us -> 4.66 us
  transfers between devices with their start and end apart: 29 -> 29, of which waited for: 15 -> 13; matrix products, arithmetic and copies ran while one was open for 0% -> 0% of each run, Pallas kernels for 19% -> 18%
where the time goes in v4:
time: 109 us
  waiting for transfers between devices  45.9 us (42%)
  starting transfers between devices  30.4 us (28%)
  Pallas kernels  25.7 us (24%)
  local copies, waits for them, and re-layouts  4.66 us (4%)
  other arithmetic  1.28 us (1%)
    ppermute x29, waiting for transfers between devices, permuted(): lax.ppermute(value, 'rows', [(i, target(i) % peers) for i in range(peers)])  45.9 us
    ppermute x29, starting transfers between devices, permuted(): lax.ppermute(value, 'rows', [(i, target(i) % peers) for i in range(peers)])  30.4 us
    pallas_call x19, Pallas kernels, kernel_call(): pl.pallas_call(kernel, out_shape=out_shape, cost_estimate=pl.CostEstimate...  16.2 us
    pallas_call x2, Pallas kernels, product_of(): pl.pallas_call(functools.partial(product_kernel, pieces=n), in_specs=[pl....  8.63 us
    unnamed x4, local copies, waits for them, and re-layouts  4.66 us
  transfers between devices with their start and end apart: 29, of which 13 were waited for; matrix products, arithmetic and copies ran while one was open for 0% of the time, Pallas kernels for 18%

profile of v4, /device:TPU:0, one launch (start us, length us, event | category | flops | bytes accessed | tf_op | source)
XLA Modules:
  0.0 109.0 jit_solution(15173156774918269780)
XLA Ops:
  0.6 1.3 %convert_element_type.3.rounded_ref = bf16[1024,256]{1,0:T(8,128)(2,1)S(1)} convert(f32[1024,256]{1,0:T(8,128)} %param.5) | non-fusion elementwise | flops 262144 | bytes 1572864 | tf_op jit(solution)/shard_map/convert_element_type | solution.py:419
  1.9 6.1 %collective-permute-start.3 = (bf16[1024,256]{1,0:T(8,128)(2,1)S(1)}, bf16[1024,256]{1,0:T(8,128)(2,1)S(1)}, u32[]{:S(2)}, u32[]{:S(2)}) collective-permute-start(bf16[1024,256]{1,0:T(8,128)(2,1)S(1)} %convert_element_type.3.rounded_ref), channel_id=1, source_target_pairs={{0,14},{1,15},{2,0},{3,1},{4,2},{5,3},{6,4},{7,5},{8,6},{9,7},{10,... | collective-permute-start | bytes 1572872 | tf_op jit(solution)/shard_map/ppermute | solution.py:20
  8.0 0.7 copy-done.1
  8.7 4.0 %copy-done = bf16[8,40,128,128]{3,2,1,0:T(8,128)(2,1)S(1)} copy-done((bf16[8,40,128,128]{3,2,1,0:T(8,128)(2,1)S(1)}, bf16[8,40,128,128]{3,2,1,0:T(8,128)(2,1)}, u32[]{:S(2)}) %copy-start) | copy-done | bytes 10485784
  12.7 0.9 shard_map.51
  13.6 0.1 collective-permute-start
  13.6 14.4 %collective-permute-done.3 = bf16[1024,256]{1,0:T(8,128)(2,1)S(1)} collective-permute-done((bf16[1024,256]{1,0:T(8,128)(2,1)S(1)}, bf16[1024,256]{1,0:T(8,128)(2,1)S(1)}, u32[]{:S(2)}, u32[]{:S(2)}) %collective-permute-start.3) | collective-permute-done | bytes 524320 | tf_op jit(solution)/shard_map/ppermute | solution.py:20
  28.1 0.2 collective-permute-done.1
  28.3 0.5 collective-permute-start.4
  28.8 1.7 %collective-permute-done.5 = bf16[1024,256]{1,0:T(8,128)(2,1)S(1)} collective-permute-done((bf16[1024,256]{1,0:T(8,128)(2,1)S(1)}, bf16[1024,256]{1,0:T(8,128)(2,1)S(1)}, u32[]{:S(2)}, u32[]{:S(2)}) %collective-permute-start.5) | collective-permute-done | bytes 524320 | tf_op jit(solution)/shard_map/ppermute | solution.py:20
  30.4 0.5 collective-permute-done.4
  30.9 4.2 %shard_map.52 = (f32[1024,256]{1,0:T(8,128)S(1)}, bf16[1024,256]{1,0:T(8,128)(2,1)S(1)}) custom-call(s32[8,40]{1,0:T(8,128)S(1)} %shard_map.50.place_ref, bf16[8,40,128,128]{3,2,1,0:T(8,128)(2,1)S(1)} %get-tuple-element.34.tiles_ref, bf16[256,256]{1,0:T(8,128)(2,1)S(1)} %get-tuple-element.35.turn_ref, bf16[8,128,256]{2,1,0:T(8,128)(2,1)S(1)} %bitcast.14, ...), custom_call_target="tpu_custom_call" | custom-call | flops 8000000000 | bytes 10485760 | tf_op jit(solution)/shard_map/pallas_call | solution.py:126
  35.2 4.9 %collective-permute-start.11 = (bf16[1024,256]{1,0:T(8,128)(2,1)S(1)}, bf16[1024,256]{1,0:T(8,128)(2,1)S(1)}, u32[]{:S(2)}, u32[]{:S(2)}) collective-permute-start(bf16[1024,256]{1,0:T(8,128)(2,1)S(1)} %get-tuple-element.45.sent_ref), channel_id=1, source_target_pairs={{0,14},{1,15},{2,0},{3,1},{4,2},{5,3},{6,4},{7,5},{8,6},{9,7},{10,... | collective-permute-start | bytes 1572872 | tf_op jit(solution)/shard_map/ppermute | solution.py:20
  40.1 1.4 %shard_map.53 = (f32[384,128]{1,0:T(8,128)S(1)}, f32[384,128]{1,0:T(8,128)S(1)}) custom-call(f32[1024,256]{1,0:T(8,128)S(1)} %get-tuple-element.40.product_ref, bf16[1024,256]{1,0:T(8,128)(2,1)S(1)} %convert_element_type.3.rounded_ref), custom_call_target="tpu_custom_call" | custom-call | flops 8000000000 | bytes 1048576 | tf_op jit(solution)/shard_map/pallas_call | solution.py:43
  41.6 1.4 %collective-permute-done.6.b_ref = f32[384,128]{1,0:T(8,128)S(1)} collective-permute-done((f32[384,128]{1,0:T(8,128)S(1)}, f32[384,128]{1,0:T(8,128)S(1)}, u32[]{:S(2)}, u32[]{:S(2)}) %collective-permute-start.6) | collective-permute-done | bytes 196640 | tf_op jit(solution)/shard_map/ppermute | solution.py:20
  43.1 1.7 %collective-permute-start.9 = (f32[192,128]{1,0:T(8,128)S(1)}, f32[192,128]{1,0:T(8,128)S(1)}, u32[]{:S(2)}, u32[]{:S(2)}) collective-permute-start(f32[192,128]{1,0:T(8,128)S(1)} %get-tuple-element.44), channel_id=1, source_target_pairs={{0,2},{1,3},{2,0},{3,1},{4,6},{5,7},{6,4},{7,5},{8,10},{9,11},{10,... | collective-permute-start | bytes 294920 | tf_op jit(solution)/shard_map/ppermute | solution.py:20
  44.8 3.1 %collective-permute-start.13 = (bf16[1024,256]{1,0:T(8,128)(2,1)S(1)}, bf16[1024,256]{1,0:T(8,128)(2,1)S(1)}, u32[]{:S(2)}, u32[]{:S(2)}) collective-permute-start(bf16[1024,256]{1,0:T(8,128)(2,1)S(1)} %get-tuple-element.45.sent_ref), channel_id=1, source_target_pairs={{0,13},{1,4},{2,15},{3,6},{4,1},{5,8},{6,3},{7,10},{8,5},{9,12},{1... | collective-permute-start | bytes 1572872 | tf_op jit(solution)/shard_map/ppermute | solution.py:20
  47.9 15.5 %collective-permute-done.9.b_ref = f32[192,128]{1,0:T(8,128)S(1)} collective-permute-done((f32[192,128]{1,0:T(8,128)S(1)}, f32[192,128]{1,0:T(8,128)S(1)}, u32[]{:S(2)}, u32[]{:S(2)}) %collective-permute-start.9) | collective-permute-done | bytes 98336 | tf_op jit(solution)/shard_map/ppermute | solution.py:20
  63.4 0.1 collective-permute-start.12
  63.6 0.5 collective-permute-start.10
  64.0 1.2 %collective-permute-start.14 = (f32[192,128]{1,0:T(8,128)S(1)}, f32[192,128]{1,0:T(8,128)S(1)}, u32[]{:S(2)}, u32[]{:S(2)}) collective-permute-start(f32[192,128]{1,0:T(8,128)S(1)} %shard_map.55.a_ref), channel_id=1, source_target_pairs={{0,4},{1,5},{2,6},{3,7},{4,0},{5,1},{6,2},{7,3},{8,12},{9,13},{10,... | collective-permute-start | bytes 294920 | tf_op jit(solution)/shard_map/ppermute | solution.py:20
  65.2 0.2 collective-permute-done.12
  65.4 0.7 collective-permute-done.10
  66.2 4.4 %shard_map.56.product_ref = f32[1024,256]{1,0:T(8,128)S(1)} custom-call(s32[8,40]{1,0:T(8,128)S(1)} %shard_map.50.place_ref, bf16[8,40,128,128]{3,2,1,0:T(8,128)(2,1)S(1)} %get-tuple-element.34.tiles_ref, bf16[256,256]{1,0:T(8,128)(2,1)S(1)} %get-tuple-element.35.turn_ref, bf16[8,128,256]{2,1,0:T(8,128)(2,1)S(1)} %bitcast.15, ...), custom_call_target="tpu_custom_call" | custom-call | flops 8000000000 | bytes 10485760 | tf_op jit(solution)/shard_map/pallas_call | solution.py:126
  70.6 0.8 shard_map.57
  71.4 0.2 collective-permute-start.15
  71.6 1.2 %collective-permute-done.15.b_ref = f32[192,128]{1,0:T(8,128)S(1)} collective-permute-done((f32[192,128]{1,0:T(8,128)S(1)}, f32[192,128]{1,0:T(8,128)S(1)}, u32[]{:S(2)}, u32[]{:S(2)}) %collective-permute-start.15) | collective-permute-done | bytes 98336 | tf_op jit(solution)/shard_map/ppermute | solution.py:20
  72.8 2.5 %collective-permute-start.17 = (f32[192,128]{1,0:T(8,128)S(1)}, f32[192,128]{1,0:T(8,128)S(1)}, u32[]{:S(2)}, u32[]{:S(2)}) collective-permute-start(f32[192,128]{1,0:T(8,128)S(1)} %shard_map.58.a_ref), channel_id=1, source_target_pairs={{0,2},{1,3},{2,0},{3,1},{4,6},{5,7},{6,4},{7,5},{8,10},{9,11},{10,... | collective-permute-start | bytes 294920 | tf_op jit(solution)/shard_map/ppermute | solution.py:20
  75.3 2.1 %collective-permute-start.16 = (f32[192,128]{1,0:T(8,128)S(1)}, f32[192,128]{1,0:T(8,128)S(1)}, u32[]{:S(2)}, u32[]{:S(2)}) collective-permute-start(f32[192,128]{1,0:T(8,128)S(1)} %get-tuple-element.52.a_ref), channel_id=1, source_target_pairs={{0,8},{1,9},{2,10},{3,11},{4,12},{5,13},{6,14},{7,15},{8,0},{9,1},... | collective-permute-start | bytes 294920 | tf_op jit(solution)/shard_map/ppermute | solution.py:20
  77.5 1.0 collective-permute-done.17.b_ref
  78.5 0.7 collective-permute-start.18
  79.2 1.3 %shard_map.66 = (f32[192,128]{1,0:T(8,128)S(1)}, f32[192,128]{1,0:T(8,128)S(1)}) custom-call(f32[1024,256]{1,0:T(8,128)S(1)} %shard_map.56.product_ref, bf16[1024,256]{1,0:T(8,128)(2,1)S(1)} %get-tuple-element.45.sent_ref, bf16[256,256]{1,0:T(8,128)(2,1)S(1)} %get-tuple-element.35.turn_ref), custom_call_target="tpu_custom_call" | custom-call | flops 8000000000 | bytes 1048576 | tf_op jit(solution)/shard_map/pallas_call | solution.py:43
  80.5 0.1 collective-permute-start.24
  80.6 4.2 %collective-permute-done.18.b_ref = f32[192,128]{1,0:T(8,128)S(1)} collective-permute-done((f32[192,128]{1,0:T(8,128)S(1)}, f32[192,128]{1,0:T(8,128)S(1)}, u32[]{:S(2)}, u32[]{:S(2)}) %collective-permute-start.18) | collective-permute-done | bytes 98336 | tf_op jit(solution)/shard_map/ppermute | solution.py:20
  84.8 0.7 collective-permute-start.22
  85.4 1.7 %collective-permute-start.19 = (f32[192,128]{1,0:T(8,128)S(1)}, f32[192,128]{1,0:T(8,128)S(1)}, u32[]{:S(2)}, u32[]{:S(2)}) collective-permute-start(f32[192,128]{1,0:T(8,128)S(1)} %shard_map.61.keep_ref), channel_id=1, source_target_pairs={{0,2},{1,3},{2,0},{3,1},{4,6},{5,7},{6,4},{7,5},{8,10},{9,11},{10,... | collective-permute-start | bytes 294920 | tf_op jit(solution)/shard_map/ppermute | solution.py:20
  87.2 0.4 collective-permute-start.25
  87.6 4.2 %collective-permute-done.22.b_ref = f32[192,128]{1,0:T(8,128)S(1)} collective-permute-done((f32[192,128]{1,0:T(8,128)S(1)}, f32[192,128]{1,0:T(8,128)S(1)}, u32[]{:S(2)}, u32[]{:S(2)}) %collective-permute-start.22) | collective-permute-done | bytes 98336 | tf_op jit(solution)/shard_map/ppermute | solution.py:20
  91.8 0.1 collective-permute-start.23
  91.9 0.5 collective-permute-start.21
  92.4 1.6 %collective-permute-start.26 = (f32[192,128]{1,0:T(8,128)S(1)}, f32[192,128]{1,0:T(8,128)S(1)}, u32[]{:S(2)}, u32[]{:S(2)}) collective-permute-start(f32[192,128]{1,0:T(8,128)S(1)} %shard_map.68.a_ref), channel_id=1, source_target_pairs={{0,4},{1,5},{2,6},{3,7},{4,0},{5,1},{6,2},{7,3},{8,12},{9,13},{10,... | collective-permute-start | bytes 294920 | tf_op jit(solution)/shard_map/ppermute | solution.py:20
  94.0 2.6 %shard_map.63 = (f32[2,64,256]{2,1,0:T(8,128)S(1)}, f32[2,192,256]{2,1,0:T(8,128)S(1)}, f32[2,256]{1,0:T(2,128)S(1)}) custom-call(f32[192,128]{1,0:T(8,128)S(1)} %shard_map.61.keep_ref, f32[192,128]{1,0:T(8,128)S(1)} %collective-permute-done.19.other_ref, f32[192,128]{1,0:T(8,128)S(1)} %collective-permute-done.20.keep_rest_ref, ...), custom_call_target="tpu_custom_call" | custom-call | bytes 1048576 | tf_op jit(solution)/shard_map/pallas_call | solution.py:43
  96.7 0.6 collective-permute-done.26.b_ref
  97.3 1.5 %collective-permute-start.27 = (f32[192,128]{1,0:T(8,128)S(1)}, f32[192,128]{1,0:T(8,128)S(1)}, u32[]{:S(2)}, u32[]{:S(2)}) collective-permute-start(f32[192,128]{1,0:T(8,128)S(1)} %shard_map.69.a_ref), channel_id=1, source_target_pairs={{0,8},{1,9},{2,10},{3,11},{4,12},{5,13},{6,14},{7,15},{8,0},{9,1},... | collective-permute-start | bytes 294920 | tf_op jit(solution)/shard_map/ppermute | solution.py:20
  98.8 6.8 %shard_map.64 = (f32[256,256]{1,0:T(8,128)S(1)}, f32[256,256]{1,0:T(8,128)S(1)}) custom-call(f32[2,64,256]{2,1,0:T(8,128)S(1)} %get-tuple-element.54.done_ref, f32[2,192,256]{2,1,0:T(8,128)S(1)} %get-tuple-element.55.rest_ref, f32[2,256]{1,0:T(2,128)S(1)} %get-tuple-element.56.scale_ref), custom_call_target="tpu_custom_call" | custom-call | flops 24000000000 | bytes 1048576 | tf_op jit(solution)/shard_map/pallas_call | solution.py:43
  105.7 0.1 collective-permute-start.28
  105.8 1.6 %shard_map.65 = f32[1024,256]{1,0:T(8,128)} custom-call(f32[1024,256]{1,0:T(8,128)S(1)} %shard_map.56.product_ref, f32[256,256]{1,0:T(8,128)S(1)} %get-tuple-element.57.inverse_ref), custom_call_target="tpu_custom_call" | custom-call | flops 8000000000 | bytes 1048576 | tf_op jit(solution)/shard_map/pallas_call | solution.py:43
  107.4 1.4 %shard_map.71 = f32[2,256,256]{2,1,0:T(8,128)} custom-call(f32[192,128]{1,0:T(8,128)S(1)} %shard_map.61.keep_ref, f32[192,128]{1,0:T(8,128)S(1)} %collective-permute-done.19.other_ref, f32[192,128]{1,0:T(8,128)S(1)} %collective-permute-done.20.keep_rest_ref, f32[192,128]{1,0:T(8,128)S(1)} %collective-permute-done.21.other_rest_ref, ...), custom_call_target="tpu_custom_call" | custom-call | bytes 1048576 | tf_op jit(solution)/shard_map/pallas_call | solution.py:43
  (37 shorter events, 0.3 us)
Async XLA Ops:
  1.9 26.2 %collective-permute-start.3 = (bf16[1024,256]{1,0:T(8,128)(2,1)S(1)}, bf16[1024,256]{1,0:T(8,128)(2,1)S(1)}, u32[]{:S(2)}, u32[]{:S(2)}) collective-permute-start(bf16[1024,256]{1,0:T(8,128)(2,1)S(1)} %convert_element_type.3.rounded_ref), channel_id=1, source_target_pairs={{0,14},{1,15},{2,0},{3,1},{4,2},{5,3},{6,4},{7,5},{8,6},{9,7},{10,... | collective-permute-start | bytes 1572872 | tf_op jit(solution)/shard_map/ppermute | solution.py:20
  8.0 20.3 %collective-permute-start.1 = (bf16[1024,256]{1,0:T(8,128)(2,1)S(1)}, bf16[1024,256]{1,0:T(8,128)(2,1)S(1)}, u32[]{:S(2)}, u32[]{:S(2)}) collective-permute-start(bf16[1024,256]{1,0:T(8,128)(2,1)S(1)} %convert_element_type.3.rounded_ref), channel_id=1, source_target_pairs={{0,2},{1,3},{2,4},{3,5},{4,6},{5,7},{6,8},{7,9},{8,10},{9,11},{10,... | collective-permute-start | bytes 1572872 | tf_op jit(solution)/shard_map/ppermute | solution.py:20
  8.0 22.5 %collective-permute-start.5 = (bf16[1024,256]{1,0:T(8,128)(2,1)S(1)}, bf16[1024,256]{1,0:T(8,128)(2,1)S(1)}, u32[]{:S(2)}, u32[]{:S(2)}) collective-permute-start(bf16[1024,256]{1,0:T(8,128)(2,1)S(1)} %convert_element_type.3.rounded_ref), channel_id=1, source_target_pairs={{0,13},{1,4},{2,15},{3,6},{4,1},{5,8},{6,3},{7,10},{8,5},{9,12},{1... | collective-permute-start | bytes 1572872 | tf_op jit(solution)/shard_map/ppermute | solution.py:20
  8.0 0.7 copy-start.1
  8.7 4.0 %copy-start = (bf16[8,40,128,128]{3,2,1,0:T(8,128)(2,1)S(1)}, bf16[8,40,128,128]{3,2,1,0:T(8,128)(2,1)}, u32[]{:S(2)}) copy-start(bf16[8,40,128,128]{3,2,1,0:T(8,128)(2,1)} %tiles_ref.1) | copy-start | bytes 31457284
  13.6 16.9 %collective-permute-start = (bf16[1024,256]{1,0:T(8,128)(2,1)S(1)}, bf16[1024,256]{1,0:T(8,128)(2,1)S(1)}, u32[]{:S(2)}, u32[]{:S(2)}) collective-permute-start(bf16[1024,256]{1,0:T(8,128)(2,1)S(1)} %convert_element_type.3.rounded_ref), channel_id=1, source_target_pairs={{0,1},{1,0},{2,3},{3,2},{4,5},{5,4},{6,7},{7,6},{8,9},{9,8},{10,11... | collective-permute-start | bytes 1572872 | tf_op jit(solution)/shard_map/ppermute | solution.py:20
  28.2 2.2 %collective-permute-start.2 = (bf16[1024,256]{1,0:T(8,128)(2,1)S(1)}, bf16[1024,256]{1,0:T(8,128)(2,1)S(1)}, u32[]{:S(2)}, u32[]{:S(2)}) collective-permute-start(bf16[1024,256]{1,0:T(8,128)(2,1)S(1)} %collective-permute-done.1), channel_id=1, source_target_pairs={{0,1},{1,0},{2,3},{3,2},{4,5},{5,4},{6,7},{7,6},{8,9},{9,8},{10,11... | collective-permute-start | bytes 1572872 | tf_op jit(solution)/shard_map/ppermute | solution.py:20
  28.3 2.6 %collective-permute-start.4 = (bf16[1024,256]{1,0:T(8,128)(2,1)S(1)}, bf16[1024,256]{1,0:T(8,128)(2,1)S(1)}, u32[]{:S(2)}, u32[]{:S(2)}) collective-permute-start(bf16[1024,256]{1,0:T(8,128)(2,1)S(1)} %collective-permute-done.3), channel_id=1, source_target_pairs={{0,1},{1,0},{2,3},{3,2},{4,5},{5,4},{6,7},{7,6},{8,9},{9,8},{10,11... | collective-permute-start | bytes 1572872 | tf_op jit(solution)/shard_map/ppermute | solution.py:20
  35.2 28.3 %collective-permute-start.11 = (bf16[1024,256]{1,0:T(8,128)(2,1)S(1)}, bf16[1024,256]{1,0:T(8,128)(2,1)S(1)}, u32[]{:S(2)}, u32[]{:S(2)}) collective-permute-start(bf16[1024,256]{1,0:T(8,128)(2,1)S(1)} %get-tuple-element.45.sent_ref), channel_id=1, source_target_pairs={{0,14},{1,15},{2,0},{3,1},{4,2},{5,3},{6,4},{7,5},{8,6},{9,7},{10,... | collective-permute-start | bytes 1572872 | tf_op jit(solution)/shard_map/ppermute | solution.py:20
  40.1 23.5 %collective-permute-start.8 = (bf16[1024,256]{1,0:T(8,128)(2,1)S(1)}, bf16[1024,256]{1,0:T(8,128)(2,1)S(1)}, u32[]{:S(2)}, u32[]{:S(2)}) collective-permute-start(bf16[1024,256]{1,0:T(8,128)(2,1)S(1)} %get-tuple-element.45.sent_ref), channel_id=1, source_target_pairs={{0,2},{1,3},{2,4},{3,5},{4,6},{5,7},{6,8},{7,9},{8,10},{9,11},{10,... | collective-permute-start | bytes 1572872 | tf_op jit(solution)/shard_map/ppermute | solution.py:20
  41.5 1.5 %collective-permute-start.6 = (f32[384,128]{1,0:T(8,128)S(1)}, f32[384,128]{1,0:T(8,128)S(1)}, u32[]{:S(2)}, u32[]{:S(2)}) collective-permute-start(f32[384,128]{1,0:T(8,128)S(1)} %get-tuple-element.42), channel_id=1, source_target_pairs={{0,1},{1,0},{2,3},{3,2},{4,5},{5,4},{6,7},{7,6},{8,9},{9,8},{10,11... | collective-permute-start | bytes 589832 | tf_op jit(solution)/shard_map/ppermute | solution.py:20
  43.1 20.4 %collective-permute-start.9 = (f32[192,128]{1,0:T(8,128)S(1)}, f32[192,128]{1,0:T(8,128)S(1)}, u32[]{:S(2)}, u32[]{:S(2)}) collective-permute-start(f32[192,128]{1,0:T(8,128)S(1)} %get-tuple-element.44), channel_id=1, source_target_pairs={{0,2},{1,3},{2,0},{3,1},{4,6},{5,7},{6,4},{7,5},{8,10},{9,11},{10,... | collective-permute-start | bytes 294920 | tf_op jit(solution)/shard_map/ppermute | solution.py:20
  44.8 20.4 %collective-permute-start.13 = (bf16[1024,256]{1,0:T(8,128)(2,1)S(1)}, bf16[1024,256]{1,0:T(8,128)(2,1)S(1)}, u32[]{:S(2)}, u32[]{:S(2)}) collective-permute-start(bf16[1024,256]{1,0:T(8,128)(2,1)S(1)} %get-tuple-element.45.sent_ref), channel_id=1, source_target_pairs={{0,13},{1,4},{2,15},{3,6},{4,1},{5,8},{6,3},{7,10},{8,5},{9,12},{1... | collective-permute-start | bytes 1572872 | tf_op jit(solution)/shard_map/ppermute | solution.py:20
  47.9 17.3 %collective-permute-start.7 = (bf16[1024,256]{1,0:T(8,128)(2,1)S(1)}, bf16[1024,256]{1,0:T(8,128)(2,1)S(1)}, u32[]{:S(2)}, u32[]{:S(2)}) collective-permute-start(bf16[1024,256]{1,0:T(8,128)(2,1)S(1)} %get-tuple-element.45.sent_ref), channel_id=1, source_target_pairs={{0,1},{1,0},{2,3},{3,2},{4,5},{5,4},{6,7},{7,6},{8,9},{9,8},{10,11... | collective-permute-start | bytes 1572872 | tf_op jit(solution)/shard_map/ppermute | solution.py:20
  63.4 2.0 %collective-permute-start.12 = (bf16[1024,256]{1,0:T(8,128)(2,1)S(1)}, bf16[1024,256]{1,0:T(8,128)(2,1)S(1)}, u32[]{:S(2)}, u32[]{:S(2)}) collective-permute-start(bf16[1024,256]{1,0:T(8,128)(2,1)S(1)} %collective-permute-done.11), channel_id=1, source_target_pairs={{0,1},{1,0},{2,3},{3,2},{4,5},{5,4},{6,7},{7,6},{8,9},{9,8},{10,11... | collective-permute-start | bytes 1572872 | tf_op jit(solution)/shard_map/ppermute | solution.py:20
  63.6 2.6 %collective-permute-start.10 = (bf16[1024,256]{1,0:T(8,128)(2,1)S(1)}, bf16[1024,256]{1,0:T(8,128)(2,1)S(1)}, u32[]{:S(2)}, u32[]{:S(2)}) collective-permute-start(bf16[1024,256]{1,0:T(8,128)(2,1)S(1)} %collective-permute-done.8), channel_id=1, source_target_pairs={{0,1},{1,0},{2,3},{3,2},{4,5},{5,4},{6,7},{7,6},{8,9},{9,8},{10,11... | collective-permute-start | bytes 1572872 | tf_op jit(solution)/shard_map/ppermute | solution.py:20
  64.0 6.5 %collective-permute-start.14 = (f32[192,128]{1,0:T(8,128)S(1)}, f32[192,128]{1,0:T(8,128)S(1)}, u32[]{:S(2)}, u32[]{:S(2)}) collective-permute-start(f32[192,128]{1,0:T(8,128)S(1)} %shard_map.55.a_ref), channel_id=1, source_target_pairs={{0,4},{1,5},{2,6},{3,7},{4,0},{5,1},{6,2},{7,3},{8,12},{9,13},{10,... | collective-permute-start | bytes 294920 | tf_op jit(solution)/shard_map/ppermute | solution.py:20
  71.4 1.4 %collective-permute-start.15 = (f32[192,128]{1,0:T(8,128)S(1)}, f32[192,128]{1,0:T(8,128)S(1)}, u32[]{:S(2)}, u32[]{:S(2)}) collective-permute-start(f32[192,128]{1,0:T(8,128)S(1)} %get-tuple-element.50), channel_id=1, source_target_pairs={{0,1},{1,0},{2,3},{3,2},{4,5},{5,4},{6,7},{7,6},{8,9},{9,8},{10,11... | collective-permute-start | bytes 294920 | tf_op jit(solution)/shard_map/ppermute | solution.py:20
  72.8 5.7 %collective-permute-start.17 = (f32[192,128]{1,0:T(8,128)S(1)}, f32[192,128]{1,0:T(8,128)S(1)}, u32[]{:S(2)}, u32[]{:S(2)}) collective-permute-start(f32[192,128]{1,0:T(8,128)S(1)} %shard_map.58.a_ref), channel_id=1, source_target_pairs={{0,2},{1,3},{2,0},{3,1},{4,6},{5,7},{6,4},{7,5},{8,10},{9,11},{10,... | collective-permute-start | bytes 294920 | tf_op jit(solution)/shard_map/ppermute | solution.py:20
  75.3 10.1 %collective-permute-start.16 = (f32[192,128]{1,0:T(8,128)S(1)}, f32[192,128]{1,0:T(8,128)S(1)}, u32[]{:S(2)}, u32[]{:S(2)}) collective-permute-start(f32[192,128]{1,0:T(8,128)S(1)} %get-tuple-element.52.a_ref), channel_id=1, source_target_pairs={{0,8},{1,9},{2,10},{3,11},{4,12},{5,13},{6,14},{7,15},{8,0},{9,1},... | collective-permute-start | bytes 294920 | tf_op jit(solution)/shard_map/ppermute | solution.py:20
  78.5 6.3 %collective-permute-start.18 = (f32[192,128]{1,0:T(8,128)S(1)}, f32[192,128]{1,0:T(8,128)S(1)}, u32[]{:S(2)}, u32[]{:S(2)}) collective-permute-start(f32[192,128]{1,0:T(8,128)S(1)} %shard_map.59.a_ref), channel_id=1, source_target_pairs={{0,4},{1,5},{2,6},{3,7},{4,0},{5,1},{6,2},{7,3},{8,12},{9,13},{10,... | collective-permute-start | bytes 294920 | tf_op jit(solution)/shard_map/ppermute | solution.py:20
  80.5 6.7 %collective-permute-start.24 = (f32[192,128]{1,0:T(8,128)S(1)}, f32[192,128]{1,0:T(8,128)S(1)}, u32[]{:S(2)}, u32[]{:S(2)}) collective-permute-start(f32[192,128]{1,0:T(8,128)S(1)} %get-tuple-element.60), channel_id=1, source_target_pairs={{0,1},{1,0},{2,3},{3,2},{4,5},{5,4},{6,7},{7,6},{8,9},{9,8},{10,11... | collective-permute-start | bytes 294920 | tf_op jit(solution)/shard_map/ppermute | solution.py:20
  84.8 7.1 %collective-permute-start.22 = (f32[192,128]{1,0:T(8,128)S(1)}, f32[192,128]{1,0:T(8,128)S(1)}, u32[]{:S(2)}, u32[]{:S(2)}) collective-permute-start(f32[192,128]{1,0:T(8,128)S(1)} %shard_map.60.a_ref), channel_id=1, source_target_pairs={{0,8},{1,9},{2,10},{3,11},{4,12},{5,13},{6,14},{7,15},{8,0},{9,1},... | collective-permute-start | bytes 294920 | tf_op jit(solution)/shard_map/ppermute | solution.py:20
  85.4 6.5 %collective-permute-start.19 = (f32[192,128]{1,0:T(8,128)S(1)}, f32[192,128]{1,0:T(8,128)S(1)}, u32[]{:S(2)}, u32[]{:S(2)}) collective-permute-start(f32[192,128]{1,0:T(8,128)S(1)} %shard_map.61.keep_ref), channel_id=1, source_target_pairs={{0,2},{1,3},{2,0},{3,1},{4,6},{5,7},{6,4},{7,5},{8,10},{9,11},{10,... | collective-permute-start | bytes 294920 | tf_op jit(solution)/shard_map/ppermute | solution.py:20
  87.2 5.2 %collective-permute-start.25 = (f32[192,128]{1,0:T(8,128)S(1)}, f32[192,128]{1,0:T(8,128)S(1)}, u32[]{:S(2)}, u32[]{:S(2)}) collective-permute-start(f32[192,128]{1,0:T(8,128)S(1)} %shard_map.67.a_ref), channel_id=1, source_target_pairs={{0,2},{1,3},{2,0},{3,1},{4,6},{5,7},{6,4},{7,5},{8,10},{9,11},{10,... | collective-permute-start | bytes 294920 | tf_op jit(solution)/shard_map/ppermute | solution.py:20
  87.6 6.4 %collective-permute-start.20 = (f32[192,128]{1,0:T(8,128)S(1)}, f32[192,128]{1,0:T(8,128)S(1)}, u32[]{:S(2)}, u32[]{:S(2)}) collective-permute-start(f32[192,128]{1,0:T(8,128)S(1)} %shard_map.61.keep_ref), channel_id=1, source_target_pairs={{0,1},{1,0},{2,3},{3,2},{4,5},{5,4},{6,7},{7,6},{8,9},{9,8},{10,11... | collective-permute-start | bytes 294920 | tf_op jit(solution)/shard_map/ppermute | solution.py:20
  91.8 2.2 %collective-permute-start.23 = (f32[192,128]{1,0:T(8,128)S(1)}, f32[192,128]{1,0:T(8,128)S(1)}, u32[]{:S(2)}, u32[]{:S(2)}) collective-permute-start(f32[192,128]{1,0:T(8,128)S(1)} %shard_map.62.raw_ref), channel_id=1, source_target_pairs={{0,1},{1,0},{2,3},{3,2},{4,5},{5,4},{6,7},{7,6},{8,9},{9,8},{10,11... | collective-permute-start | bytes 294920 | tf_op jit(solution)/shard_map/ppermute | solution.py:20
  91.9 2.1 %collective-permute-start.21 = (f32[192,128]{1,0:T(8,128)S(1)}, f32[192,128]{1,0:T(8,128)S(1)}, u32[]{:S(2)}, u32[]{:S(2)}) collective-permute-start(f32[192,128]{1,0:T(8,128)S(1)} %collective-permute-done.19.other_ref), channel_id=1, source_target_pairs={{0,1},{1,0},{2,3},{3,2},{4,5},{5,4},{6,7},{7,6},{8,9},{9,8},{10,11... | collective-permute-start | bytes 294920 | tf_op jit(solution)/shard_map/ppermute | solution.py:20
  92.4 4.9 %collective-permute-start.26 = (f32[192,128]{1,0:T(8,128)S(1)}, f32[192,128]{1,0:T(8,128)S(1)}, u32[]{:S(2)}, u32[]{:S(2)}) collective-permute-start(f32[192,128]{1,0:T(8,128)S(1)} %shard_map.68.a_ref), channel_id=1, source_target_pairs={{0,4},{1,5},{2,6},{3,7},{4,0},{5,1},{6,2},{7,3},{8,12},{9,13},{10,... | collective-permute-start | bytes 294920 | tf_op jit(solution)/shard_map/ppermute | solution.py:20
  97.3 8.3 %collective-permute-start.27 = (f32[192,128]{1,0:T(8,128)S(1)}, f32[192,128]{1,0:T(8,128)S(1)}, u32[]{:S(2)}, u32[]{:S(2)}) collective-permute-start(f32[192,128]{1,0:T(8,128)S(1)} %shard_map.69.a_ref), channel_id=1, source_target_pairs={{0,8},{1,9},{2,10},{3,11},{4,12},{5,13},{6,14},{7,15},{8,0},{9,1},... | collective-permute-start | bytes 294920 | tf_op jit(solution)/shard_map/ppermute | solution.py:20
  105.7 1.7 %collective-permute-start.28 = (f32[192,128]{1,0:T(8,128)S(1)}, f32[192,128]{1,0:T(8,128)S(1)}, u32[]{:S(2)}, u32[]{:S(2)}) collective-permute-start(f32[192,128]{1,0:T(8,128)S(1)} %shard_map.70.proj_ref), channel_id=1, source_target_pairs={{0,1},{1,0},{2,3},{3,2},{4,5},{5,4},{6,7},{7,6},{8,9},{9,8},{10,11... | collective-permute-start | bytes 294920 | tf_op jit(solution)/shard_map/ppermute | solution.py:20

commit v5 on v4

--- a/solution.py
+++ b/solution.py
@@ -170,15 +170,40 @@
     mine_ref[n:, :], rest_ref[n:, :] = halves(rounded_ref[...].astype(jnp.float32), product)
 
 
+def shrunk(product_ref):
+    product = product_ref[...]
+    scale = 1.0 / jnp.max(jnp.abs(product))
+    return product * scale, scale
+
+
+def write_halves(pair, scale, mine_ref, rest_ref):
+    n = mine_ref.shape[0] - B
+    for ref, half in zip((mine_ref, rest_ref), pair):
+        ref[:n, :] = half
+        ref[n:, :] = jnp.full((B, ref.shape[1]), scale, jnp.float32)
+
+
 def gram_kernel(product_ref, a_ref, b_ref, mine_ref, rest_ref, added_ref):
-    product = product_ref[...]
-    mine_ref[...], rest_ref[...] = halves(product, product)
+    product, scale = shrunk(product_ref)
+    write_halves(halves(product, product), scale, mine_ref, rest_ref)
     added_ref[...] = a_ref[...] + b_ref[...]
 
 
 def proj_kernel(product_ref, sent_ref, turn_ref, mine_ref, rest_ref):
+    product, scale = shrunk(product_ref)
     rounded = jnp.dot(sent_ref[...], turn_ref[...], preferred_element_type=jnp.float32)
-    mine_ref[...], rest_ref[...] = halves(rounded, product_ref[...])
+    write_halves(halves(rounded, product), scale, mine_ref, rest_ref)
+
+
+def scaled_sum_kernel(a_ref, b_ref, out_ref, *, power):
+    n = out_ref.shape[0] - B
+    scale = jnp.minimum(a_ref[n:, :], b_ref[n:, :])
+    terms = []
+    for ref in (a_ref, b_ref):
+        ratio = (scale / ref[n:, :])[0:1, :]
+        terms.append(ref[:n, :] * (ratio * ratio if power == 2 else ratio))
+    out_ref[:n, :] = terms[0] + terms[1]
+    out_ref[n:, :] = scale
 
 
 def split_kernel(a_ref, b_ref, mine_ref, rest_ref):
@@ -197,12 +222,17 @@
     return kernel_call(added_kernel, jax.ShapeDtypeStruct(a.shape, a.dtype), a, b, limit=4)
 
 
-def summed(mine, rest, first=1, last=None):
+def summed(mine, rest, first=1, last=None, add=added):
     step = first
     while step < (last or lax.axis_size("rows")):
-        mine = added(mine, permuted(rest if step == 1 else mine, lambda i: i ^ step))
+        mine = add(mine, permuted(rest if step == 1 else mine, lambda i: i ^ step))
         step *= 2
     return mine
+
+
+def scaled_sum(power):
+    kernel = functools.partial(scaled_sum_kernel, power=power)
+    return lambda a, b: kernel_call(kernel, jax.ShapeDtypeStruct(a.shape, a.dtype), a, b, limit=4)
 
 
 def unpacked(mine, rest):
@@ -362,7 +392,7 @@
     mine = jnp.where(bit == 0, keep_ref[...], other_ref[...])
     rest = jnp.where(bit == 0, keep_rest_ref[...], other_rest_ref[...])
     one, scale_ref[0:1, :] = scaled(unpacked(mine, rest))
-    two, scale_ref[1:2, :] = scaled(unpacked(raw_ref[...], raw_rest_ref[...]))
+    two, scale_ref[1:2, :] = scaled(unpacked(raw_ref[:-B, :], raw_rest_ref[:-B, :]))
     done, rest = eliminated([one, two], 0, CHUNK)
     for m in range(2):
         done_ref[m] = done[m]
@@ -375,15 +405,16 @@
         ref[...] = inverse_factor(jnp.concatenate([done_ref[m], done[m]], axis=0), scale_ref[m : m + 1, :])
 
 
-def modes_kernel(product_ref, inverse_ref, modes_ref, held, sems, *, scale):
+def modes_kernel(product_ref, gram_ref, inverse_ref, modes_ref, held, sems, *, scale):
     inverse = two_parts(inverse_ref[...] * scale)
     h = inverse_ref.shape[0] // 2
     along = ((1,), (1,))
     step = product_ref.shape[0] // sems.shape[0]
+    shrink = gram_ref[-B:, :][0:1, 0:1]
     copies = []
     for i in range(sems.shape[0]):
         at = slice(i * step, (i + 1) * step)
-        product = two_parts(product_ref[at, :])
+        product = two_parts(product_ref[at, :] * shrink)
         held[at, :h] = near_dot([p[:, :h] for p in product], [w[:h, :h] for w in inverse], along)
         held[at, h:] = near_dot(product, [w[h:, :] for w in inverse], along)
         copies.append(pltpu.make_async_copy(held.at[at], modes_ref.at[at], sems.at[i]))
@@ -402,8 +433,8 @@
     held[0] = unpacked(mine, rest)
     copies[0].start()
     inverse = two_parts(inverse_ref[...])
-    proj = near_dot(inverse, two_parts(unpacked(proj_ref[...], proj_rest_ref[...])))
-    held[1] = near_dot(two_parts(proj), inverse, ((1,), (1,)))
+    proj = near_dot(inverse, two_parts(unpacked(proj_ref[:-B, :], proj_rest_ref[:-B, :])))
+    held[1] = near_dot(two_parts(proj), inverse, ((1,), (1,))) / proj_ref[-B:, :][0:1, 0:1]
     copies[1].start()
     for c in copies:
         c.wait()
@@ -440,17 +471,18 @@
     partner = permuted(first, lambda i: i ^ 4)
 
     (raw,) = product_of(place, kept, turn, pieces, jnp.float32)
-    gram, rest, first = kernel_call(gram_kernel, (half_sum,) * 3, raw, first, partner, flops=LONG)
-    gram = summed(gram, rest, 1, 2)
+    scaled_half = f32(3 * modes // 4 + B, modes // 2)
+    gram, rest, first = kernel_call(gram_kernel, (scaled_half,) * 2 + (half_sum,), raw, first, partner, flops=LONG)
+    gram = summed(gram, rest, 1, 2, scaled_sum(2))
     first = after(first, gram)
-    proj, rest = kernel_call(proj_kernel, (half_sum,) * 2, after(raw, gram), sent, turn, flops=LONG)
-    gram = summed(gram, None, 2, 8)
+    proj, rest = kernel_call(proj_kernel, (scaled_half,) * 2, after(raw, gram), sent, turn, flops=LONG)
+    gram = summed(gram, None, 2, 8, scaled_sum(2))
     partner = permuted(first, lambda i: i ^ 8)
     first = added(*after((first, partner), gram))
-    first, gram = summed(first, None, 16), summed(gram, None, 8)
+    first, gram = summed(first, None, 16), summed(gram, None, 8, add=scaled_sum(2))
     other = permuted(first, lambda i: i ^ 2)
     first = (first, other, swapped(first), swapped(other))
-    proj = summed(proj, rest, 1, peers // 4)
+    proj = summed(proj, rest, 1, peers // 4, scaled_sum(1))
     partner = permuted(proj, lambda i: i ^ (peers // 4))
     eliminating = kernel_call(
         upper_kernel,
@@ -458,12 +490,12 @@
         *first, gram, swapped(gram),
         flops=0,
     )
-    proj = added(*after((proj, partner), eliminating[0]))
+    proj = scaled_sum(1)(*after((proj, partner), eliminating[0]))
     partner = permuted(proj, lambda i: i ^ (peers // 2))
     inverse, both = kernel_call(lower_kernel, (f32(modes, modes),) * 2, *eliminating, flops=3 * LONG)
-    proj = added(*after((proj, partner), inverse))
+    proj = scaled_sum(1)(*after((proj, partner), inverse))
     modes_out = kernel_call(
-        functools.partial(modes_kernel, scale=math.sqrt(rows * peers)), f32(rows, modes), raw, both,
+        functools.partial(modes_kernel, scale=math.sqrt(rows * peers)), f32(rows, modes), raw, gram, both,
         flops=LONG,
         out_specs=pl.BlockSpec(memory_space=pltpu.HBM),
         scratch_shapes=[pltpu.VMEM((rows, modes), jnp.float32), pltpu.SemaphoreType.DMA((4,))],

time: 109 us -> 112 us (1.028)
  starting transfers between devices: 30.4 us -> 32 us
    ppermute x29, starting transfers between devices: 30.4 us -> 32 us  [permuted(): lax.ppermute(value, 'rows', [(i, target(i) % peers) for i in range(peers)])]
  transfers between devices with their start and end apart: 29 -> 29, of which waited for: 13 -> 14; matrix products, arithmetic and copies ran while one was open for 0% -> 0% of each run, Pallas kernels for 18% -> 17%
where the time goes in v5:
time: 112 us
  waiting for transfers between devices  46.9 us (42%)
  starting transfers between devices  32 us (29%)
  Pallas kernels  26.1 us (23%)
  local copies, waits for them, and re-layouts  4.66 us (4%)
  other arithmetic  1.28 us (1%)
    ppermute x29, waiting for transfers between devices, permuted(): lax.ppermute(value, 'rows', [(i, target(i) % peers) for i in range(peers)])  46.9 us
    ppermute x29, starting transfers between devices, permuted(): lax.ppermute(value, 'rows', [(i, target(i) % peers) for i in range(peers)])  32 us
    pallas_call x19, Pallas kernels, kernel_call(): pl.pallas_call(kernel, out_shape=out_shape, cost_estimate=pl.CostEstimate...  16.6 us
    pallas_call x2, Pallas kernels, product_of(): pl.pallas_call(functools.partial(product_kernel, pieces=n), in_specs=[pl....  8.63 us
    unnamed x4, local copies, waits for them, and re-layouts  4.66 us
  transfers between devices with their start and end apart: 29, of which 14 were waited for; matrix products, arithmetic and copies ran while one was open for 0% of the time, Pallas kernels for 17%

profile of v5, /device:TPU:0, one launch (start us, length us, event | category | flops | bytes accessed | tf_op | source)
XLA Modules:
  0.0 111.9 jit_solution(1031001558218963749)
XLA Ops:
  0.6 1.3 %convert_element_type.3.rounded_ref = bf16[1024,256]{1,0:T(8,128)(2,1)S(1)} convert(f32[1024,256]{1,0:T(8,128)} %param.5) | non-fusion elementwise | flops 262144 | bytes 1572864 | tf_op jit(solution)/shard_map/convert_element_type | solution.py:450
  1.9 6.1 %collective-permute-start.3 = (bf16[1024,256]{1,0:T(8,128)(2,1)S(1)}, bf16[1024,256]{1,0:T(8,128)(2,1)S(1)}, u32[]{:S(2)}, u32[]{:S(2)}) collective-permute-start(bf16[1024,256]{1,0:T(8,128)(2,1)S(1)} %convert_element_type.3.rounded_ref), channel_id=1, source_target_pairs={{0,14},{1,15},{2,0},{3,1},{4,2},{5,3},{6,4},{7,5},{8,6},{9,7},{10,... | collective-permute-start | bytes 1572872 | tf_op jit(solution)/shard_map/ppermute | solution.py:20
  8.0 0.7 copy-done.1
  8.7 4.0 %copy-done = bf16[8,40,128,128]{3,2,1,0:T(8,128)(2,1)S(1)} copy-done((bf16[8,40,128,128]{3,2,1,0:T(8,128)(2,1)S(1)}, bf16[8,40,128,128]{3,2,1,0:T(8,128)(2,1)}, u32[]{:S(2)}) %copy-start) | copy-done | bytes 10485784
  12.7 0.9 shard_map.51
  13.6 0.1 collective-permute-start
  13.6 14.4 %collective-permute-done.3 = bf16[1024,256]{1,0:T(8,128)(2,1)S(1)} collective-permute-done((bf16[1024,256]{1,0:T(8,128)(2,1)S(1)}, bf16[1024,256]{1,0:T(8,128)(2,1)S(1)}, u32[]{:S(2)}, u32[]{:S(2)}) %collective-permute-start.3) | collective-permute-done | bytes 524320 | tf_op jit(solution)/shard_map/ppermute | solution.py:20
  28.1 0.2 collective-permute-done.1
  28.3 0.5 collective-permute-start.4
  28.8 1.7 %collective-permute-done.5 = bf16[1024,256]{1,0:T(8,128)(2,1)S(1)} collective-permute-done((bf16[1024,256]{1,0:T(8,128)(2,1)S(1)}, bf16[1024,256]{1,0:T(8,128)(2,1)S(1)}, u32[]{:S(2)}, u32[]{:S(2)}) %collective-permute-start.5) | collective-permute-done | bytes 524320 | tf_op jit(solution)/shard_map/ppermute | solution.py:20
  30.4 0.5 collective-permute-done.4
  30.9 4.2 %shard_map.52 = (f32[1024,256]{1,0:T(8,128)S(1)}, bf16[1024,256]{1,0:T(8,128)(2,1)S(1)}) custom-call(s32[8,40]{1,0:T(8,128)S(1)} %shard_map.50.place_ref, bf16[8,40,128,128]{3,2,1,0:T(8,128)(2,1)S(1)} %get-tuple-element.34.tiles_ref, bf16[256,256]{1,0:T(8,128)(2,1)S(1)} %get-tuple-element.35.turn_ref, bf16[8,128,256]{2,1,0:T(8,128)(2,1)S(1)} %bitcast.14, ...), custom_call_target="tpu_custom_call" | custom-call | flops 8000000000 | bytes 10485760 | tf_op jit(solution)/shard_map/pallas_call | solution.py:126
  35.2 4.9 %collective-permute-start.11 = (bf16[1024,256]{1,0:T(8,128)(2,1)S(1)}, bf16[1024,256]{1,0:T(8,128)(2,1)S(1)}, u32[]{:S(2)}, u32[]{:S(2)}) collective-permute-start(bf16[1024,256]{1,0:T(8,128)(2,1)S(1)} %get-tuple-element.45.sent_ref), channel_id=1, source_target_pairs={{0,14},{1,15},{2,0},{3,1},{4,2},{5,3},{6,4},{7,5},{8,6},{9,7},{10,... | collective-permute-start | bytes 1572872 | tf_op jit(solution)/shard_map/ppermute | solution.py:20
  40.1 1.4 %shard_map.53 = (f32[384,128]{1,0:T(8,128)S(1)}, f32[384,128]{1,0:T(8,128)S(1)}) custom-call(f32[1024,256]{1,0:T(8,128)S(1)} %get-tuple-element.40.product_ref, bf16[1024,256]{1,0:T(8,128)(2,1)S(1)} %convert_element_type.3.rounded_ref), custom_call_target="tpu_custom_call" | custom-call | flops 8000000000 | bytes 1048576 | tf_op jit(solution)/shard_map/pallas_call | solution.py:43
  41.5 0.1 collective-permute-start.6
  41.6 1.4 %collective-permute-done.6.b_ref = f32[384,128]{1,0:T(8,128)S(1)} collective-permute-done((f32[384,128]{1,0:T(8,128)S(1)}, f32[384,128]{1,0:T(8,128)S(1)}, u32[]{:S(2)}, u32[]{:S(2)}) %collective-permute-start.6) | collective-permute-done | bytes 196640 | tf_op jit(solution)/shard_map/ppermute | solution.py:20
  43.1 1.7 %collective-permute-start.9 = (f32[192,128]{1,0:T(8,128)S(1)}, f32[192,128]{1,0:T(8,128)S(1)}, u32[]{:S(2)}, u32[]{:S(2)}) collective-permute-start(f32[192,128]{1,0:T(8,128)S(1)} %get-tuple-element.44), channel_id=1, source_target_pairs={{0,2},{1,3},{2,0},{3,1},{4,6},{5,7},{6,4},{7,5},{8,10},{9,11},{10,... | collective-permute-start | bytes 294920 | tf_op jit(solution)/shard_map/ppermute | solution.py:20
  44.8 3.1 %collective-permute-start.13 = (bf16[1024,256]{1,0:T(8,128)(2,1)S(1)}, bf16[1024,256]{1,0:T(8,128)(2,1)S(1)}, u32[]{:S(2)}, u32[]{:S(2)}) collective-permute-start(bf16[1024,256]{1,0:T(8,128)(2,1)S(1)} %get-tuple-element.45.sent_ref), channel_id=1, source_target_pairs={{0,13},{1,4},{2,15},{3,6},{4,1},{5,8},{6,3},{7,10},{8,5},{9,12},{1... | collective-permute-start | bytes 1572872 | tf_op jit(solution)/shard_map/ppermute | solution.py:20
  47.9 15.5 %collective-permute-done.9.b_ref = f32[192,128]{1,0:T(8,128)S(1)} collective-permute-done((f32[192,128]{1,0:T(8,128)S(1)}, f32[192,128]{1,0:T(8,128)S(1)}, u32[]{:S(2)}, u32[]{:S(2)}) %collective-permute-start.9) | collective-permute-done | bytes 98336 | tf_op jit(solution)/shard_map/ppermute | solution.py:20
  63.4 0.1 collective-permute-start.12
  63.6 0.5 collective-permute-start.10
  64.0 1.2 %collective-permute-start.14 = (f32[192,128]{1,0:T(8,128)S(1)}, f32[192,128]{1,0:T(8,128)S(1)}, u32[]{:S(2)}, u32[]{:S(2)}) collective-permute-start(f32[192,128]{1,0:T(8,128)S(1)} %shard_map.55.a_ref), channel_id=1, source_target_pairs={{0,4},{1,5},{2,6},{3,7},{4,0},{5,1},{6,2},{7,3},{8,12},{9,13},{10,... | collective-permute-start | bytes 294920 | tf_op jit(solution)/shard_map/ppermute | solution.py:20
  65.2 0.2 collective-permute-done.12
  65.4 0.7 collective-permute-done.10
  66.2 4.4 %shard_map.56.product_ref = f32[1024,256]{1,0:T(8,128)S(1)} custom-call(s32[8,40]{1,0:T(8,128)S(1)} %shard_map.50.place_ref, bf16[8,40,128,128]{3,2,1,0:T(8,128)(2,1)S(1)} %get-tuple-element.34.tiles_ref, bf16[256,256]{1,0:T(8,128)(2,1)S(1)} %get-tuple-element.35.turn_ref, bf16[8,128,256]{2,1,0:T(8,128)(2,1)S(1)} %bitcast.15, ...), custom_call_target="tpu_custom_call" | custom-call | flops 8000000000 | bytes 10485760 | tf_op jit(solution)/shard_map/pallas_call | solution.py:126
  70.6 1.1 shard_map.57
  71.7 0.2 collective-permute-start.15
  71.9 1.2 %collective-permute-done.15.b_ref = f32[200,128]{1,0:T(8,128)S(1)} collective-permute-done((f32[200,128]{1,0:T(8,128)S(1)}, f32[200,128]{1,0:T(8,128)S(1)}, u32[]{:S(2)}, u32[]{:S(2)}) %collective-permute-start.15) | collective-permute-done | bytes 102432 | tf_op jit(solution)/shard_map/ppermute | solution.py:20
  73.1 2.5 %collective-permute-start.16 = (f32[200,128]{1,0:T(8,128)S(1)}, f32[200,128]{1,0:T(8,128)S(1)}, u32[]{:S(2)}, u32[]{:S(2)}) collective-permute-start(f32[200,128]{1,0:T(8,128)S(1)} %shard_map.58.a_ref), channel_id=1, source_target_pairs={{0,2},{1,3},{2,0},{3,1},{4,6},{5,7},{6,4},{7,5},{8,10},{9,11},{10,... | collective-permute-start | bytes 307208 | tf_op jit(solution)/shard_map/ppermute | solution.py:20
  75.6 3.2 %collective-permute-done.16.b_ref = f32[200,128]{1,0:T(8,128)S(1)} collective-permute-done((f32[200,128]{1,0:T(8,128)S(1)}, f32[200,128]{1,0:T(8,128)S(1)}, u32[]{:S(2)}, u32[]{:S(2)}) %collective-permute-start.16) | collective-permute-done | bytes 102432 | tf_op jit(solution)/shard_map/ppermute | solution.py:20
  78.8 0.7 collective-permute-start.17
  79.6 1.3 %shard_map.66 = (f32[200,128]{1,0:T(8,128)S(1)}, f32[200,128]{1,0:T(8,128)S(1)}) custom-call(f32[1024,256]{1,0:T(8,128)S(1)} %shard_map.56.product_ref, bf16[1024,256]{1,0:T(8,128)(2,1)S(1)} %get-tuple-element.45.sent_ref, bf16[256,256]{1,0:T(8,128)(2,1)S(1)} %get-tuple-element.35.turn_ref), custom_call_target="tpu_custom_call" | custom-call | flops 8000000000 | bytes 1048576 | tf_op jit(solution)/shard_map/pallas_call | solution.py:43
  80.9 2.7 %collective-permute-start.19 = (f32[192,128]{1,0:T(8,128)S(1)}, f32[192,128]{1,0:T(8,128)S(1)}, u32[]{:S(2)}, u32[]{:S(2)}) collective-permute-start(f32[192,128]{1,0:T(8,128)S(1)} %get-tuple-element.52.a_ref), channel_id=1, source_target_pairs={{0,8},{1,9},{2,10},{3,11},{4,12},{5,13},{6,14},{7,15},{8,0},{9,1},... | collective-permute-start | bytes 294920 | tf_op jit(solution)/shard_map/ppermute | solution.py:20
  83.7 2.1 %collective-permute-start.18 = (f32[200,128]{1,0:T(8,128)S(1)}, f32[200,128]{1,0:T(8,128)S(1)}, u32[]{:S(2)}, u32[]{:S(2)}) collective-permute-start(f32[200,128]{1,0:T(8,128)S(1)} %shard_map.60.a_ref), channel_id=1, source_target_pairs={{0,8},{1,9},{2,10},{3,11},{4,12},{5,13},{6,14},{7,15},{8,0},{9,1},... | collective-permute-start | bytes 307208 | tf_op jit(solution)/shard_map/ppermute | solution.py:20
  85.8 1.8 %collective-permute-start.25 = (f32[200,128]{1,0:T(8,128)S(1)}, f32[200,128]{1,0:T(8,128)S(1)}, u32[]{:S(2)}, u32[]{:S(2)}) collective-permute-start(f32[200,128]{1,0:T(8,128)S(1)} %shard_map.67.a_ref), channel_id=1, source_target_pairs={{0,2},{1,3},{2,0},{3,1},{4,6},{5,7},{6,4},{7,5},{8,10},{9,11},{10,... | collective-permute-start | bytes 307208 | tf_op jit(solution)/shard_map/ppermute | solution.py:20
  87.6 4.2 %collective-permute-done.19.b_ref = f32[192,128]{1,0:T(8,128)S(1)} collective-permute-done((f32[192,128]{1,0:T(8,128)S(1)}, f32[192,128]{1,0:T(8,128)S(1)}, u32[]{:S(2)}, u32[]{:S(2)}) %collective-permute-start.19) | collective-permute-done | bytes 98336 | tf_op jit(solution)/shard_map/ppermute | solution.py:20
  91.8 1.8 %collective-permute-start.20 = (f32[192,128]{1,0:T(8,128)S(1)}, f32[192,128]{1,0:T(8,128)S(1)}, u32[]{:S(2)}, u32[]{:S(2)}) collective-permute-start(f32[192,128]{1,0:T(8,128)S(1)} %shard_map.62.keep_ref), channel_id=1, source_target_pairs={{0,2},{1,3},{2,0},{3,1},{4,6},{5,7},{6,4},{7,5},{8,10},{9,11},{10,... | collective-permute-start | bytes 294920 | tf_op jit(solution)/shard_map/ppermute | solution.py:20
  93.7 0.1 collective-permute-start.23
  93.8 0.2 collective-permute-start.26
  93.9 0.5 collective-permute-start.21
  94.4 2.1 %collective-permute-done.20.other_ref = f32[192,128]{1,0:T(8,128)S(1)} collective-permute-done((f32[192,128]{1,0:T(8,128)S(1)}, f32[192,128]{1,0:T(8,128)S(1)}, u32[]{:S(2)}, u32[]{:S(2)}) %collective-permute-start.20) | collective-permute-done | bytes 98336 | tf_op jit(solution)/shard_map/ppermute | solution.py:20
  96.5 1.3 %collective-permute-done.22.other_rest_ref = f32[192,128]{1,0:T(8,128)S(1)} collective-permute-done((f32[192,128]{1,0:T(8,128)S(1)}, f32[192,128]{1,0:T(8,128)S(1)}, u32[]{:S(2)}, u32[]{:S(2)}) %collective-permute-start.22) | collective-permute-done | bytes 98336 | tf_op jit(solution)/shard_map/ppermute | solution.py:20
  97.8 2.6 %shard_map.63 = (f32[2,64,256]{2,1,0:T(8,128)S(1)}, f32[2,192,256]{2,1,0:T(8,128)S(1)}, f32[2,256]{1,0:T(2,128)S(1)}) custom-call(f32[192,128]{1,0:T(8,128)S(1)} %shard_map.62.keep_ref, f32[192,128]{1,0:T(8,128)S(1)} %collective-permute-done.20.other_ref, f32[192,128]{1,0:T(8,128)S(1)} %collective-permute-done.21.keep_rest_ref, ...), custom_call_target="tpu_custom_call" | custom-call | bytes 1048576 | tf_op jit(solution)/shard_map/pallas_call | solution.py:43
  100.5 1.1 collective-permute-start.27
  101.6 6.8 %shard_map.64 = (f32[256,256]{1,0:T(8,128)S(1)}, f32[256,256]{1,0:T(8,128)S(1)}) custom-call(f32[2,64,256]{2,1,0:T(8,128)S(1)} %get-tuple-element.54.done_ref, f32[2,192,256]{2,1,0:T(8,128)S(1)} %get-tuple-element.55.rest_ref, f32[2,256]{1,0:T(2,128)S(1)} %get-tuple-element.56.scale_ref), custom_call_target="tpu_custom_call" | custom-call | flops 24000000000 | bytes 1048576 | tf_op jit(solution)/shard_map/pallas_call | solution.py:43
  108.4 0.2 collective-permute-done.27.b_ref
  108.7 1.6 %shard_map.65 = f32[1024,256]{1,0:T(8,128)} custom-call(f32[1024,256]{1,0:T(8,128)S(1)} %shard_map.56.product_ref, f32[200,128]{1,0:T(8,128)S(1)} %shard_map.61.raw_ref.gram_ref, f32[256,256]{1,0:T(8,128)S(1)} %get-tuple-element.57.inverse_ref), custom_call_target="tpu_custom_call" | custom-call | flops 8000000000 | bytes 1048576 | tf_op jit(solution)/shard_map/pallas_call | solution.py:43
  110.3 1.4 %shard_map.71 = f32[2,256,256]{2,1,0:T(8,128)} custom-call(f32[192,128]{1,0:T(8,128)S(1)} %shard_map.62.keep_ref, f32[192,128]{1,0:T(8,128)S(1)} %collective-permute-done.20.other_ref, f32[192,128]{1,0:T(8,128)S(1)} %collective-permute-done.21.keep_rest_ref, f32[192,128]{1,0:T(8,128)S(1)} %collective-permute-done.22.other_rest_ref, ...), custom_call_target="tpu_custom_call" | custom-call | bytes 1048576 | tf_op jit(solution)/shard_map/pallas_call | solution.py:43
  (37 shorter events, 0.5 us)
Async XLA Ops:
  1.9 26.2 %collective-permute-start.3 = (bf16[1024,256]{1,0:T(8,128)(2,1)S(1)}, bf16[1024,256]{1,0:T(8,128)(2,1)S(1)}, u32[]{:S(2)}, u32[]{:S(2)}) collective-permute-start(bf16[1024,256]{1,0:T(8,128)(2,1)S(1)} %convert_element_type.3.rounded_ref), channel_id=1, source_target_pairs={{0,14},{1,15},{2,0},{3,1},{4,2},{5,3},{6,4},{7,5},{8,6},{9,7},{10,... | collective-permute-start | bytes 1572872 | tf_op jit(solution)/shard_map/ppermute | solution.py:20
  8.0 20.3 %collective-permute-start.1 = (bf16[1024,256]{1,0:T(8,128)(2,1)S(1)}, bf16[1024,256]{1,0:T(8,128)(2,1)S(1)}, u32[]{:S(2)}, u32[]{:S(2)}) collective-permute-start(bf16[1024,256]{1,0:T(8,128)(2,1)S(1)} %convert_element_type.3.rounded_ref), channel_id=1, source_target_pairs={{0,2},{1,3},{2,4},{3,5},{4,6},{5,7},{6,8},{7,9},{8,10},{9,11},{10,... | collective-permute-start | bytes 1572872 | tf_op jit(solution)/shard_map/ppermute | solution.py:20
  8.0 22.5 %collective-permute-start.5 = (bf16[1024,256]{1,0:T(8,128)(2,1)S(1)}, bf16[1024,256]{1,0:T(8,128)(2,1)S(1)}, u32[]{:S(2)}, u32[]{:S(2)}) collective-permute-start(bf16[1024,256]{1,0:T(8,128)(2,1)S(1)} %convert_element_type.3.rounded_ref), channel_id=1, source_target_pairs={{0,13},{1,4},{2,15},{3,6},{4,1},{5,8},{6,3},{7,10},{8,5},{9,12},{1... | collective-permute-start | bytes 1572872 | tf_op jit(solution)/shard_map/ppermute | solution.py:20
  8.0 0.7 copy-start.1
  8.7 4.0 %copy-start = (bf16[8,40,128,128]{3,2,1,0:T(8,128)(2,1)S(1)}, bf16[8,40,128,128]{3,2,1,0:T(8,128)(2,1)}, u32[]{:S(2)}) copy-start(bf16[8,40,128,128]{3,2,1,0:T(8,128)(2,1)} %tiles_ref.1) | copy-start | bytes 31457284
  13.6 16.9 %collective-permute-start = (bf16[1024,256]{1,0:T(8,128)(2,1)S(1)}, bf16[1024,256]{1,0:T(8,128)(2,1)S(1)}, u32[]{:S(2)}, u32[]{:S(2)}) collective-permute-start(bf16[1024,256]{1,0:T(8,128)(2,1)S(1)} %convert_element_type.3.rounded_ref), channel_id=1, source_target_pairs={{0,1},{1,0},{2,3},{3,2},{4,5},{5,4},{6,7},{7,6},{8,9},{9,8},{10,11... | collective-permute-start | bytes 1572872 | tf_op jit(solution)/shard_map/ppermute | solution.py:20
  28.2 2.2 %collective-permute-start.2 = (bf16[1024,256]{1,0:T(8,128)(2,1)S(1)}, bf16[1024,256]{1,0:T(8,128)(2,1)S(1)}, u32[]{:S(2)}, u32[]{:S(2)}) collective-permute-start(bf16[1024,256]{1,0:T(8,128)(2,1)S(1)} %collective-permute-done.1), channel_id=1, source_target_pairs={{0,1},{1,0},{2,3},{3,2},{4,5},{5,4},{6,7},{7,6},{8,9},{9,8},{10,11... | collective-permute-start | bytes 1572872 | tf_op jit(solution)/shard_map/ppermute | solution.py:20
  28.3 2.6 %collective-permute-start.4 = (bf16[1024,256]{1,0:T(8,128)(2,1)S(1)}, bf16[1024,256]{1,0:T(8,128)(2,1)S(1)}, u32[]{:S(2)}, u32[]{:S(2)}) collective-permute-start(bf16[1024,256]{1,0:T(8,128)(2,1)S(1)} %collective-permute-done.3), channel_id=1, source_target_pairs={{0,1},{1,0},{2,3},{3,2},{4,5},{5,4},{6,7},{7,6},{8,9},{9,8},{10,11... | collective-permute-start | bytes 1572872 | tf_op jit(solution)/shard_map/ppermute | solution.py:20
  35.2 28.3 %collective-permute-start.11 = (bf16[1024,256]{1,0:T(8,128)(2,1)S(1)}, bf16[1024,256]{1,0:T(8,128)(2,1)S(1)}, u32[]{:S(2)}, u32[]{:S(2)}) collective-permute-start(bf16[1024,256]{1,0:T(8,128)(2,1)S(1)} %get-tuple-element.45.sent_ref), channel_id=1, source_target_pairs={{0,14},{1,15},{2,0},{3,1},{4,2},{5,3},{6,4},{7,5},{8,6},{9,7},{10,... | collective-permute-start | bytes 1572872 | tf_op jit(solution)/shard_map/ppermute | solution.py:20
  40.1 23.5 %collective-permute-start.8 = (bf16[1024,256]{1,0:T(8,128)(2,1)S(1)}, bf16[1024,256]{1,0:T(8,128)(2,1)S(1)}, u32[]{:S(2)}, u32[]{:S(2)}) collective-permute-start(bf16[1024,256]{1,0:T(8,128)(2,1)S(1)} %get-tuple-element.45.sent_ref), channel_id=1, source_target_pairs={{0,2},{1,3},{2,4},{3,5},{4,6},{5,7},{6,8},{7,9},{8,10},{9,11},{10,... | collective-permute-start | bytes 1572872 | tf_op jit(solution)/shard_map/ppermute | solution.py:20
  41.5 1.5 %collective-permute-start.6 = (f32[384,128]{1,0:T(8,128)S(1)}, f32[384,128]{1,0:T(8,128)S(1)}, u32[]{:S(2)}, u32[]{:S(2)}) collective-permute-start(f32[384,128]{1,0:T(8,128)S(1)} %get-tuple-element.42), channel_id=1, source_target_pairs={{0,1},{1,0},{2,3},{3,2},{4,5},{5,4},{6,7},{7,6},{8,9},{9,8},{10,11... | collective-permute-start | bytes 589832 | tf_op jit(solution)/shard_map/ppermute | solution.py:20
  43.1 20.4 %collective-permute-start.9 = (f32[192,128]{1,0:T(8,128)S(1)}, f32[192,128]{1,0:T(8,128)S(1)}, u32[]{:S(2)}, u32[]{:S(2)}) collective-permute-start(f32[192,128]{1,0:T(8,128)S(1)} %get-tuple-element.44), channel_id=1, source_target_pairs={{0,2},{1,3},{2,0},{3,1},{4,6},{5,7},{6,4},{7,5},{8,10},{9,11},{10,... | collective-permute-start | bytes 294920 | tf_op jit(solution)/shard_map/ppermute | solution.py:20
  44.8 20.4 %collective-permute-start.13 = (bf16[1024,256]{1,0:T(8,128)(2,1)S(1)}, bf16[1024,256]{1,0:T(8,128)(2,1)S(1)}, u32[]{:S(2)}, u32[]{:S(2)}) collective-permute-start(bf16[1024,256]{1,0:T(8,128)(2,1)S(1)} %get-tuple-element.45.sent_ref), channel_id=1, source_target_pairs={{0,13},{1,4},{2,15},{3,6},{4,1},{5,8},{6,3},{7,10},{8,5},{9,12},{1... | collective-permute-start | bytes 1572872 | tf_op jit(solution)/shard_map/ppermute | solution.py:20
  47.9 17.3 %collective-permute-start.7 = (bf16[1024,256]{1,0:T(8,128)(2,1)S(1)}, bf16[1024,256]{1,0:T(8,128)(2,1)S(1)}, u32[]{:S(2)}, u32[]{:S(2)}) collective-permute-start(bf16[1024,256]{1,0:T(8,128)(2,1)S(1)} %get-tuple-element.45.sent_ref), channel_id=1, source_target_pairs={{0,1},{1,0},{2,3},{3,2},{4,5},{5,4},{6,7},{7,6},{8,9},{9,8},{10,11... | collective-permute-start | bytes 1572872 | tf_op jit(solution)/shard_map/ppermute | solution.py:20
  63.4 2.0 %collective-permute-start.12 = (bf16[1024,256]{1,0:T(8,128)(2,1)S(1)}, bf16[1024,256]{1,0:T(8,128)(2,1)S(1)}, u32[]{:S(2)}, u32[]{:S(2)}) collective-permute-start(bf16[1024,256]{1,0:T(8,128)(2,1)S(1)} %collective-permute-done.11), channel_id=1, source_target_pairs={{0,1},{1,0},{2,3},{3,2},{4,5},{5,4},{6,7},{7,6},{8,9},{9,8},{10,11... | collective-permute-start | bytes 1572872 | tf_op jit(solution)/shard_map/ppermute | solution.py:20
  63.6 2.6 %collective-permute-start.10 = (bf16[1024,256]{1,0:T(8,128)(2,1)S(1)}, bf16[1024,256]{1,0:T(8,128)(2,1)S(1)}, u32[]{:S(2)}, u32[]{:S(2)}) collective-permute-start(bf16[1024,256]{1,0:T(8,128)(2,1)S(1)} %collective-permute-done.8), channel_id=1, source_target_pairs={{0,1},{1,0},{2,3},{3,2},{4,5},{5,4},{6,7},{7,6},{8,9},{9,8},{10,11... | collective-permute-start | bytes 1572872 | tf_op jit(solution)/shard_map/ppermute | solution.py:20
  64.0 6.5 %collective-permute-start.14 = (f32[192,128]{1,0:T(8,128)S(1)}, f32[192,128]{1,0:T(8,128)S(1)}, u32[]{:S(2)}, u32[]{:S(2)}) collective-permute-start(f32[192,128]{1,0:T(8,128)S(1)} %shard_map.55.a_ref), channel_id=1, source_target_pairs={{0,4},{1,5},{2,6},{3,7},{4,0},{5,1},{6,2},{7,3},{8,12},{9,13},{10,... | collective-permute-start | bytes 294920 | tf_op jit(solution)/shard_map/ppermute | solution.py:20
  71.7 1.4 %collective-permute-start.15 = (f32[200,128]{1,0:T(8,128)S(1)}, f32[200,128]{1,0:T(8,128)S(1)}, u32[]{:S(2)}, u32[]{:S(2)}) collective-permute-start(f32[200,128]{1,0:T(8,128)S(1)} %get-tuple-element.49), channel_id=1, source_target_pairs={{0,1},{1,0},{2,3},{3,2},{4,5},{5,4},{6,7},{7,6},{8,9},{9,8},{10,11... | collective-permute-start | bytes 307208 | tf_op jit(solution)/shard_map/ppermute | solution.py:20
  73.1 5.7 %collective-permute-start.16 = (f32[200,128]{1,0:T(8,128)S(1)}, f32[200,128]{1,0:T(8,128)S(1)}, u32[]{:S(2)}, u32[]{:S(2)}) collective-permute-start(f32[200,128]{1,0:T(8,128)S(1)} %shard_map.58.a_ref), channel_id=1, source_target_pairs={{0,2},{1,3},{2,0},{3,1},{4,6},{5,7},{6,4},{7,5},{8,10},{9,11},{10,... | collective-permute-start | bytes 307208 | tf_op jit(solution)/shard_map/ppermute | solution.py:20
  78.8 4.8 %collective-permute-start.17 = (f32[200,128]{1,0:T(8,128)S(1)}, f32[200,128]{1,0:T(8,128)S(1)}, u32[]{:S(2)}, u32[]{:S(2)}) collective-permute-start(f32[200,128]{1,0:T(8,128)S(1)} %shard_map.59.a_ref), channel_id=1, source_target_pairs={{0,4},{1,5},{2,6},{3,7},{4,0},{5,1},{6,2},{7,3},{8,12},{9,13},{10,... | collective-permute-start | bytes 307208 | tf_op jit(solution)/shard_map/ppermute | solution.py:20
  80.9 4.9 %collective-permute-start.24 = (f32[200,128]{1,0:T(8,128)S(1)}, f32[200,128]{1,0:T(8,128)S(1)}, u32[]{:S(2)}, u32[]{:S(2)}) collective-permute-start(f32[200,128]{1,0:T(8,128)S(1)} %get-tuple-element.60), channel_id=1, source_target_pairs={{0,1},{1,0},{2,3},{3,2},{4,5},{5,4},{6,7},{7,6},{8,9},{9,8},{10,11... | collective-permute-start | bytes 307208 | tf_op jit(solution)/shard_map/ppermute | solution.py:20
  80.9 10.9 %collective-permute-start.19 = (f32[192,128]{1,0:T(8,128)S(1)}, f32[192,128]{1,0:T(8,128)S(1)}, u32[]{:S(2)}, u32[]{:S(2)}) collective-permute-start(f32[192,128]{1,0:T(8,128)S(1)} %get-tuple-element.52.a_ref), channel_id=1, source_target_pairs={{0,8},{1,9},{2,10},{3,11},{4,12},{5,13},{6,14},{7,15},{8,0},{9,1},... | collective-permute-start | bytes 294920 | tf_op jit(solution)/shard_map/ppermute | solution.py:20
  83.7 9.9 %collective-permute-start.18 = (f32[200,128]{1,0:T(8,128)S(1)}, f32[200,128]{1,0:T(8,128)S(1)}, u32[]{:S(2)}, u32[]{:S(2)}) collective-permute-start(f32[200,128]{1,0:T(8,128)S(1)} %shard_map.60.a_ref), channel_id=1, source_target_pairs={{0,8},{1,9},{2,10},{3,11},{4,12},{5,13},{6,14},{7,15},{8,0},{9,1},... | collective-permute-start | bytes 307208 | tf_op jit(solution)/shard_map/ppermute | solution.py:20
  85.8 7.9 %collective-permute-start.25 = (f32[200,128]{1,0:T(8,128)S(1)}, f32[200,128]{1,0:T(8,128)S(1)}, u32[]{:S(2)}, u32[]{:S(2)}) collective-permute-start(f32[200,128]{1,0:T(8,128)S(1)} %shard_map.67.a_ref), channel_id=1, source_target_pairs={{0,2},{1,3},{2,0},{3,1},{4,6},{5,7},{6,4},{7,5},{8,10},{9,11},{10,... | collective-permute-start | bytes 307208 | tf_op jit(solution)/shard_map/ppermute | solution.py:20
  91.8 4.7 %collective-permute-start.20 = (f32[192,128]{1,0:T(8,128)S(1)}, f32[192,128]{1,0:T(8,128)S(1)}, u32[]{:S(2)}, u32[]{:S(2)}) collective-permute-start(f32[192,128]{1,0:T(8,128)S(1)} %shard_map.62.keep_ref), channel_id=1, source_target_pairs={{0,2},{1,3},{2,0},{3,1},{4,6},{5,7},{6,4},{7,5},{8,10},{9,11},{10,... | collective-permute-start | bytes 294920 | tf_op jit(solution)/shard_map/ppermute | solution.py:20
  93.7 4.1 %collective-permute-start.23 = (f32[200,128]{1,0:T(8,128)S(1)}, f32[200,128]{1,0:T(8,128)S(1)}, u32[]{:S(2)}, u32[]{:S(2)}) collective-permute-start(f32[200,128]{1,0:T(8,128)S(1)} %shard_map.61.raw_ref.gram_ref), channel_id=1, source_target_pairs={{0,1},{1,0},{2,3},{3,2},{4,5},{5,4},{6,7},{7,6},{8,9},{9,8},{10,11... | collective-permute-start | bytes 307208 | tf_op jit(solution)/shard_map/ppermute | solution.py:20
  93.8 6.7 %collective-permute-start.26 = (f32[200,128]{1,0:T(8,128)S(1)}, f32[200,128]{1,0:T(8,128)S(1)}, u32[]{:S(2)}, u32[]{:S(2)}) collective-permute-start(f32[200,128]{1,0:T(8,128)S(1)} %shard_map.68.a_ref), channel_id=1, source_target_pairs={{0,4},{1,5},{2,6},{3,7},{4,0},{5,1},{6,2},{7,3},{8,12},{9,13},{10,... | collective-permute-start | bytes 307208 | tf_op jit(solution)/shard_map/ppermute | solution.py:20
  93.9 2.6 %collective-permute-start.21 = (f32[192,128]{1,0:T(8,128)S(1)}, f32[192,128]{1,0:T(8,128)S(1)}, u32[]{:S(2)}, u32[]{:S(2)}) collective-permute-start(f32[192,128]{1,0:T(8,128)S(1)} %shard_map.62.keep_ref), channel_id=1, source_target_pairs={{0,1},{1,0},{2,3},{3,2},{4,5},{5,4},{6,7},{7,6},{8,9},{9,8},{10,11... | collective-permute-start | bytes 294920 | tf_op jit(solution)/shard_map/ppermute | solution.py:20
  96.5 1.3 %collective-permute-start.22 = (f32[192,128]{1,0:T(8,128)S(1)}, f32[192,128]{1,0:T(8,128)S(1)}, u32[]{:S(2)}, u32[]{:S(2)}) collective-permute-start(f32[192,128]{1,0:T(8,128)S(1)} %collective-permute-done.20.other_ref), channel_id=1, source_target_pairs={{0,1},{1,0},{2,3},{3,2},{4,5},{5,4},{6,7},{7,6},{8,9},{9,8},{10,11... | collective-permute-start | bytes 294920 | tf_op jit(solution)/shard_map/ppermute | solution.py:20
  100.5 8.1 %collective-permute-start.27 = (f32[200,128]{1,0:T(8,128)S(1)}, f32[200,128]{1,0:T(8,128)S(1)}, u32[]{:S(2)}, u32[]{:S(2)}) collective-permute-start(f32[200,128]{1,0:T(8,128)S(1)} %shard_map.69.a_ref), channel_id=1, source_target_pairs={{0,8},{1,9},{2,10},{3,11},{4,12},{5,13},{6,14},{7,15},{8,0},{9,1},... | collective-permute-start | bytes 307208 | tf_op jit(solution)/shard_map/ppermute | solution.py:20
  108.6 1.7 %collective-permute-start.28 = (f32[200,128]{1,0:T(8,128)S(1)}, f32[200,128]{1,0:T(8,128)S(1)}, u32[]{:S(2)}, u32[]{:S(2)}) collective-permute-start(f32[200,128]{1,0:T(8,128)S(1)} %shard_map.70.proj_ref), channel_id=1, source_target_pairs={{0,1},{1,0},{2,3},{3,2},{4,5},{5,4},{6,7},{7,6},{8,9},{9,8},{10,11... | collective-permute-start | bytes 307208 | tf_op jit(solution)/shard_map/ppermute | solution.py:20
